TPU v7x, 32 devices: a whole 2x2x4 slice. The times are simulated.
32 devices in a mesh: space: 8 (over z, y), pairs: 4 (over x, core).
Axes of the slice: x: 2, y: 2, z: 4, core: 2. Of those that a mesh axis runs over, the one named last changes fastest.
Arguments:
- positions: float32 [2048, 3, 512], P(('space', 'pairs')), may hold values from -3 to 25.2, as said below
- forces: float32 [2048, 3, 512], P(('space', 'pairs')), may hold values from -6 to 6
- pair_cells: int32 [2, 1536], P(None, ('space', 'pairs')), may hold values from 0 to 2047, as said below
- pair_count: int32 [32], P(('space', 'pairs')), may hold values from 6 to 48, as said below
Outputs:
- velocity: float32 [2048, 3, 512], P(('space', 'pairs'))
Inputs may be any that keep to these rules, and one draw needn't show every extreme that they name: `pair_cells`: device g holds cells [g * 64, (g + 1) * 64). Row 0 of its slot columns names one of its own cells. Row 1 names a cell other than row 0's; over the 48 slots of one device it names cells of each of the 12 devices of the device's region and of the two regions beside it exactly 4 times, the first and the last region counting as beside each other. Slots at or past a device's count hold pairs too but are not in its list. `pair_count`: in every region one device holds 48 live slots. `positions`: the cells of region r have their first coordinates within 1.2 of [3 r, 3 r + 3); the other two coordinates lie within -3 to 5.
All inputs are finite; a program needn't handle non-finite values.
Results may differ from a plain program's by a relative error of at most 0.0003.
Values sent between devices are 32-bit elements; how exact they have to be, the bound alone decides.
No kernel may reach another device: no remote copies, remote signals or barrier semaphores. Data moves between devices by JAX's collectives and lax.ppermute only.
A program may use at most 128 MiB of HBM per device.

v0:
```python
import functools
import math

import jax
import jax.numpy as jnp
from jax import lax
from jax.experimental import pallas as pl
from jax.experimental.pallas import tpu as pltpu
from jax.sharding import PartitionSpec as P

stokes_coef = 1.0 / (8.0 * math.pi)
eps_sq = 0.01
slab_width = 3.0
across_middle = 1.0
LANES = 128
FEATURES = 16

f32 = jnp.float32
bf16 = jnp.bfloat16


def split(value, terms):
    parts = []
    for _ in range(terms - 1):
        part = value.astype(bf16).astype(f32)
        parts.append(part)
        value = value - part
    parts.append(value)
    return parts


def features(x, f):
    norm = jnp.sum(x * x, axis=0, keepdims=True)
    along = jnp.sum(x * f, axis=0, keepdims=True)
    rows = [f] + [x[k : k + 1] * f for k in range(3)] + [norm * f + x * along]
    rows.append(jnp.zeros_like(norm))
    stacked = jnp.concatenate(rows, axis=0)
    return jnp.concatenate([part.astype(bf16) for part in split(stacked, 3)], axis=0)


def combine(sums, y):
    force = sums[0:3]
    moment = [sums[3 + 3 * k : 6 + 3 * k] for k in range(3)]
    second = sums[12:15]
    norm = jnp.sum(y * y, axis=0, keepdims=True)
    trace = moment[0][0:1] + moment[1][1:2] + moment[2][2:3]
    along = jnp.sum(y * force, axis=0, keepdims=True) - trace
    turned = jnp.concatenate(
        [jnp.sum(y * moment[k], axis=0, keepdims=True) for k in range(3)], axis=0
    )
    mixed = y[0:1] * moment[0] + y[1:2] * moment[1] + y[2:3] * moment[2]
    velocity = (norm + 2.0 * eps_sq) * force + second - 2.0 * mixed + y * along - turned
    return velocity * stokes_coef


def gram_factors(x, y):
    one = jnp.ones((1, x.shape[1]), f32)
    none = jnp.zeros((3, x.shape[1]), f32)
    norm_x = jnp.sum(x * x, axis=0, keepdims=True)
    norm_y = jnp.sum(y * y, axis=0, keepdims=True) + eps_sq
    left = split(jnp.concatenate([x, norm_x, one, none], axis=0), 3)
    right = split(jnp.concatenate([-2.0 * y, one, norm_y, none], axis=0), 3)
    order = ((0, 0), (0, 1), (1, 0), (0, 2), (1, 1), (2, 0))
    return (
        jnp.concatenate([left[p] for p, _ in order], axis=0).astype(bf16),
        jnp.concatenate([right[q] for _, q in order], axis=0).astype(bf16),
    )


def dot(left, right, left_dim, right_dim):
    return lax.dot_general(
        left, right, (((left_dim,), (right_dim,)), ((), ())), preferred_element_type=f32
    )


def fold(sums):
    return sums[0:FEATURES] + sums[FEATURES : 2 * FEATURES] + sums[2 * FEATURES :]


def weights(dist_sq):
    inverse = lax.rsqrt(dist_sq)
    cubed = inverse * inverse * inverse
    high = cubed.astype(bf16)
    low = (cubed - high.astype(f32)).astype(bf16)
    return high, low


def pair_velocities(cells):
    grams = [dot(*gram_factors(xa, xb), 0, 0) for xa, _, xb, _ in cells]
    feats = [(features(xa, fa), features(xb, fb)) for xa, fa, xb, fb in cells]
    results = []
    waiting = []

    def finish():
        sums_a, sums_b, xa, xb = waiting.pop(0)
        results.append((combine(fold(sums_a), xa), combine(fold(sums_b), xb)))

    for gram, (feat_a, feat_b), (xa, _, xb, _) in zip(grams, feats, cells):
        high, low = weights(gram)
        rows = jnp.concatenate([high, low], axis=0)
        columns = jnp.concatenate([high, low], axis=1)
        sums_b = dot(jnp.concatenate([feat_a, feat_a], axis=1), rows, 1, 0)
        sums_a = dot(jnp.concatenate([feat_b, feat_b], axis=1), columns, 1, 1)
        waiting.append((sums_a, sums_b, xa, xb))
        if len(waiting) > 1:
            finish()
    finish()
    return results


def row_base(cell, tiles):
    return cell // 8 * (8 * tiles) + lax.rem(cell, 8)


def away_of(kind, odd):
    return (0, 1 - 2 * odd, 2 * odd - 1)[kind]


def pack_kernel(sizes, cells, count, pos_hbm, frc_hbm, *refs):
    n_space, n_pairs, share, cell_dev, tiles = sizes
    outs, table = refs[:n_pairs], refs[n_pairs]
    slots, used, pos, frc, sems = refs[n_pairs + 1 :]
    fetches = [
        pltpu.make_async_copy(pos_hbm, pos, sems.at[0]),
        pltpu.make_async_copy(frc_hbm, frc, sems.at[1]),
    ]
    for fetch in fetches:
        fetch.start()
    n_slots = cells.shape[1]
    owner = cells[0, 0] // cell_dev
    here = owner // n_pairs
    here_turn = lax.rem(owner, n_pairs)
    for bucket in range(3 * n_pairs):
        used[bucket] = 0
    for s in range(n_slots):
        owner = cells[1, s] // cell_dev
        there = owner // n_pairs
        turn = lax.rem(owner, n_pairs) ^ here_turn
        kind = jnp.where(there == here, 0, jnp.where(there // 2 == here // 2, 1, 2))
        bucket = kind * n_pairs + turn
        rank = used[bucket]
        used[bucket] = rank + 1
        slots[bucket * share + rank] = s
    for fetch in fetches:
        fetch.wait()
    lane = lax.broadcasted_iota(jnp.int32, (1, LANES), 1)
    plane = cell_dev * tiles
    for m in range(3 * n_pairs):
        kind, turn = m // n_pairs, m % n_pairs
        out = outs[turn]
        label = jnp.full((1, LANES), -1.0, f32)
        for k in range(share):
            s = slots[m * share + k]
            a = lax.rem(cells[0, s], cell_dev)
            live = s < count[0]
            b = jnp.where(live, lax.rem(cells[1, s], cell_dev), -1)
            table[m * share + k] = jnp.where(live, a, -1)
            label = jnp.where(lane == k, b.astype(f32), label)
            base = row_base(a, tiles)
            for c in range(6):
                source = pos if c < 3 else frc
                row = (k * 6 + c) * tiles
                out[kind, row : row + tiles, :] = source[
                    pl.ds(base + c % 3 * plane, tiles, stride=8), :
                ]
        last = share * 6 * tiles
        out[kind, last : last + 1, :] = label


def pair_kernel(sizes, kinds, started, *refs):
    n_space, n_pairs, share, cell_dev, tiles = sizes
    n = len(kinds)
    messages, (pos, frc) = refs[:n], refs[n : n + 2]
    outs = refs[n + 2 + started :]
    (acc, reply), (inbox, todo, middles) = outs[:2], outs[-3:]
    rows_in = share * 6 * tiles
    plane = cell_dev * tiles
    if not started:
        acc[...] = jnp.zeros_like(acc)
        outs[2][...] = jnp.zeros_like(outs[2])
    here = lax.axis_index("space")
    number = jnp.int32(0)
    first = 0
    for kind, message in zip(kinds, messages):
        away = jnp.int32(away_of(kind, lax.rem(here, 2)))
        there = lax.rem(here + away + n_space, n_space)
        half = 0.5 * slab_width * away.astype(f32)
        middle_a = slab_width * (there.astype(f32) + 0.5) - half
        middle_b = slab_width * (here.astype(f32) + 0.5) + half
        for block in range(message.shape[0]):
            inbox[first * rows_in : (first + 1) * rows_in, :] = message[block, 0:rows_in, :]
            label = message[block, rows_in : rows_in + 1, :].astype(jnp.int32)
            for k in range(share):
                b = label[0, k]
                todo[0, number] = first * share + k
                todo[1, number] = b
                middles[0, number] = middle_a
                middles[1, number] = middle_b
                number = number + jnp.where(b >= 0, 1, 0)
            first += 1

    axis = lax.broadcasted_iota(jnp.int32, (3, 1), 0)

    def load(i):
        base = todo[0, i] * (6 * tiles)
        data = jnp.concatenate(
            [inbox[pl.ds(base + t, 6, stride=tiles), :] for t in range(tiles)], axis=1
        )
        start = row_base(todo[1, i], tiles)
        xb, fb = (
            jnp.concatenate(
                [ref[pl.ds(start + 8 * t, 3, stride=plane), :] for t in range(tiles)], axis=1
            )
            for ref in (pos, frc)
        )
        xa = data[0:3] - jnp.where(axis == 0, middles[0, i], across_middle)
        xb = xb - jnp.where(axis == 0, middles[1, i], across_middle)
        return xa, data[3:6], xb, fb

    def store(i, vel_a, vel_b):
        base = todo[0, i] * (3 * tiles)
        start = row_base(todo[1, i], tiles)
        parts = [slice(t * LANES, (t + 1) * LANES) for t in range(tiles)]
        places = [pl.ds(start + 8 * t, 3, stride=plane) for t in range(tiles)]
        totals = [acc[place, :] + vel_b[:, part] for place, part in zip(places, parts)]
        for t in range(tiles):
            acc[places[t], :] = totals[t]
            reply[pl.ds(base + t, 3, stride=tiles), :] = vel_a[:, parts[t]]

    def several(numbers):
        results = pair_velocities([load(i) for i in numbers])
        for i, result in zip(numbers, results):
            store(i, *result)

    def four(i, _):
        several([4 * i + j for j in range(4)])
        return 0

    lax.fori_loop(0, number // 4, four, 0)
    left = lax.rem(number, 4)

    @pl.when(left >= 2)
    def _():
        several([number - left, number - left + 1])

    @pl.when(lax.rem(left, 2) == 1)
    def _():
        several([number - 1])


def add_kernel(sizes, table, acc, *refs):
    n_space, n_pairs, share, cell_dev, tiles = sizes
    replies, out = refs[:-1], refs[-1]
    plane = cell_dev * tiles
    out[...] = acc[...]
    for m in range(3 * n_pairs):
        kind, turn = m // n_pairs, m % n_pairs
        for k in range(share):
            a = table[m * share + k]
            live = a >= 0
            base = row_base(jnp.maximum(a, 0), tiles)
            places = [pl.ds(base + c * plane, tiles, stride=8) for c in range(3)]
            totals = []
            for c in range(3):
                row = (k * 3 + c) * tiles
                term = jnp.where(live, replies[turn][kind, row : row + tiles, :], 0.0)
                totals.append(out[places[c], :] + term)
            for c in range(3):
                out[places[c], :] = totals[c]


def flat_rows(cells):
    count, _, points = cells.shape
    value = jnp.transpose(cells, (1, 0, 2)).reshape(3, count // 8, 8, points // LANES, LANES)
    return jnp.transpose(value, (0, 1, 3, 2, 4)).reshape(-1, LANES)


def cell_rows(rows, count, points):
    value = rows.reshape(3, count // 8, points // LANES, 8, LANES)
    value = jnp.transpose(value, (0, 1, 3, 2, 4)).reshape(3, count, points)
    return jnp.transpose(value, (1, 0, 2))


def body(positions, forces, pair_cells, pair_count):
    n_space = lax.axis_size("space")
    n_pairs = lax.axis_size("pairs")
    cell_dev, _, points = positions.shape
    n_slots = pair_cells.shape[1]
    share = n_slots // (3 * n_pairs)
    tiles = points // LANES
    sizes = (n_space, n_pairs, share, cell_dev, tiles)
    rows_in = share * 6 * tiles
    rows_out = share * 3 * tiles
    pos = flat_rows(positions)
    frc = flat_rows(forces)
    vmem = pl.BlockSpec(memory_space=pltpu.VMEM)
    smem = pl.BlockSpec(memory_space=pltpu.SMEM)
    hbm = pl.BlockSpec(memory_space=pltpu.HBM)
    message = jax.ShapeDtypeStruct((3, rows_in + 8, LANES), f32)
    total = jax.ShapeDtypeStruct((3 * cell_dev * tiles, LANES), f32)

    def across(value, turn):
        return lax.ppermute(value, "pairs", [(j, j ^ turn) for j in range(n_pairs)])

    def beyond(value, kind):
        moves = [(i, (i + away_of(kind, i % 2)) % n_space) for i in range(n_space)]
        return lax.ppermute(value, "space", moves)

    packed = pl.pallas_call(
        functools.partial(pack_kernel, sizes),
        out_shape=[message] * n_pairs + [jax.ShapeDtypeStruct((n_slots,), jnp.int32)],
        in_specs=[smem, smem, hbm, hbm],
        out_specs=[vmem] * n_pairs + [smem],
        scratch_shapes=[
            pltpu.SMEM((n_slots,), jnp.int32),
            pltpu.SMEM((3 * n_pairs,), jnp.int32),
            pltpu.VMEM(total.shape, f32),
            pltpu.VMEM(total.shape, f32),
            pltpu.SemaphoreType.DMA((2,)),
        ],
        compiler_params=pltpu.CompilerParams(vmem_limit_bytes=60 * 1024 * 1024),
        name="pack",
    )(pair_cells, pair_count, pos, frc)
    sent, table = packed[:n_pairs], packed[n_pairs]
    got = [sent[0]] + [across(sent[turn], turn) for turn in range(1, n_pairs)]

    def pairs(arrived, before):
        kinds = [kind for kind, _ in arrived]
        values = [value for _, value in arrived]
        n = len(values)
        blocks = sum(value.shape[0] for value in values)
        return pl.pallas_call(
            functools.partial(pair_kernel, sizes, kinds, len(before)),
            out_shape=[total, jax.ShapeDtypeStruct((blocks * rows_out, LANES), f32)]
            + [jax.ShapeDtypeStruct((1, LANES), f32)] * (not before),
            in_specs=[vmem] * (n + 2 + len(before)),
            out_specs=[vmem] * (2 + (not before)),
            scratch_shapes=[
                pltpu.VMEM((blocks * rows_in, LANES), f32),
                pltpu.SMEM((2, blocks * share + 1), jnp.int32),
                pltpu.SMEM((2, blocks * share + 1), f32),
            ],
            input_output_aliases={n + 2: 0} if before else {},
            compiler_params=pltpu.CompilerParams(vmem_limit_bytes=48 * 1024 * 1024),
            cost_estimate=pl.CostEstimate(
                flops=blocks * 1_000_000_000, bytes_accessed=2_000_000, transcendentals=2_000_000
            ),
            name="pairs",
        )(*values, pos, frc, *before)

    near, far = range(2), range(2, n_pairs)
    own = [sent[0][kind : kind + 1] for kind in range(3)]
    core = [got[1][kind : kind + 1] for kind in range(3)]
    out_1n = beyond(jnp.concatenate([own[1], core[1]]), 1)
    acc, reply_0n, nothing = pairs([(0, own[0]), (0, core[0])], [])
    rest = [got[turn] + nothing[None] for turn in far]
    out_1f = beyond(jnp.stack([value[1] for value in rest]), 1)
    out_2 = beyond(jnp.concatenate([own[2], core[2]] + [value[2:] for value in rest]), 2)
    acc, reply_m = pairs([(1, out_1n)] + [(0, got[turn][0:1]) for turn in far], [acc])
    acc, reply_f = pairs([(1, out_1f), (2, out_2)], [acc])
    reply_0n, reply_m, reply_f = (
        value.reshape(-1, rows_out, LANES) for value in (reply_0n, reply_m, reply_f)
    )
    cut = n_pairs - 2
    back_0 = jnp.concatenate([reply_0n, reply_m[2:]])
    back_1 = beyond(jnp.concatenate([reply_m[:2], reply_f[:cut]]), 1)
    back_2 = beyond(reply_f[cut:], 2)
    back = []
    for turn in range(n_pairs):
        value = jnp.stack([back_0[turn], back_1[turn], back_2[turn]])
        back.append(across(value, turn) if turn else value)
    velocity = pl.pallas_call(
        functools.partial(add_kernel, sizes),
        out_shape=total,
        in_specs=[smem] + [vmem] * (1 + n_pairs),
        out_specs=vmem,
        compiler_params=pltpu.CompilerParams(vmem_limit_bytes=48 * 1024 * 1024),
        name="add",
    )(table, acc, *back)
    return cell_rows(velocity, cell_dev, points)


def solution(mesh):
    placed = (
        P(("space", "pairs"), None, None),
        P(("space", "pairs"), None, None),
        P(None, ("space", "pairs")),
        P(("space", "pairs")),
    )
    return jax.shard_map(
        body,
        mesh=mesh,
        in_specs=placed,
        out_specs=P(("space", "pairs"), None, None),
        check_vma=False,
    )
```

profile of v0, /device:TPU:0, one launch (start us, length us, event | category | flops | bytes accessed | tf_op | source)
XLA Modules:
  0.0 52.8 jit_solution(14769156863519667346)
XLA Ops:
  0.7 3.2 %pack.1 = (f32[3,104,128]{2,1,0:T(8,128)}, f32[3,104,128]{2,1,0:T(8,128)}, f32[3,104,128]{2,1,0:T(8,128)}, f32[3,104,128]{2,1,0:T(8,128)}, s32[48]{0:T(128)}) custom-call(s32[2,48]{1,0:T(2,128)} %cells.1, s32[1]{0:T(128)S(6)} %copy.9.count, f32[768,128]{1,0:T(8,128)} %bitcast.33, f32[768,128]{1,0:T(8,128)} %bitcast.37), custom_call_target="tpu_custom_call" | custom-call | tf_op jit(solution)/shard_map/pack/pallas_call | solution.py:309
  3.9 3.0 %collective-permute-start = (f32[3,104,128]{2,1,0:T(8,128)}, f32[3,104,128]{2,1,0:T(8,128)S(1)}, u32[]{:S(2)}, u32[]{:S(2)}) collective-permute-start(f32[3,104,128]{2,1,0:T(8,128)} %get-tuple-element.18), channel_id=1, source_target_pairs={{0,2},{1,3},{2,0},{3,1},{4,6},{5,7},{6,4},{7,5},{8,10},{9,11},{10,... | collective-permute-start | bytes 479240 | tf_op jit(solution)/shard_map/ppermute | solution.py:303
  6.9 0.0 collective-permute-start.1
  6.9 0.2 collective-permute-start.2
  7.1 0.0 copy-start
  7.1 0.9 %fusion = (f32[1,104,128]{2,1,0:T(8,128)S(1)}, f32[1,104,128]{2,1,0:T(8,128)S(1)}, f32[1,104,128]{2,1,0:T(8,128)S(1)}) fusion(f32[3,104,128]{2,1,0:T(8,128)} %get-tuple-element.19), kind=kLoop, calls=%fused_computation.14 | loop fusion | bytes 319488 | tf_op jit(solution)/shard_map/slice | solution.py:352
  8.0 0.4 collective-permute-done.1
  8.5 1.6 %collective-permute-start.5 = (f32[2,104,128]{2,1,0:T(8,128)S(1)}, f32[2,104,128]{2,1,0:T(8,128)S(1)}, u32[]{:S(2)}, u32[]{:S(2)}) collective-permute-start(f32[2,104,128]{2,1,0:T(8,128)S(1)} %pad_maximum_fusion.2), channel_id=1, source_target_pairs={{0,4},{4,0},{8,12},{12,8},{16,20},{20,16},{24,28},{28,24},{1,5},{5... | collective-permute-start | bytes 319496 | tf_op jit(solution)/shard_map/ppermute | solution.py:307
  10.1 0.0 copy-done
  10.1 0.0 copy-done.1
  10.1 3.8 %pairs.3 = (f32[768,128]{1,0:T(8,128)S(1)}, f32[96,128]{1,0:T(8,128)S(1)}, f32[1,128]{1,0:T(1,128)S(1)}) custom-call(f32[1,104,128]{2,1,0:T(8,128)S(1)} %get-tuple-element.31.refs_0_, f32[1,104,128]{2,1,0:T(8,128)S(1)} %get-tuple-element.34.refs_1_, f32[768,128]{1,0:T(8,128)S(1)} %bitcast.34, f32[768,128]{1,0:T(8,128)S(1)} %bitcast.38), custom_call_target="tpu_custom_call" | custom-call | flops 2000000000 | bytes 2000000 | tf_op jit(solution)/shard_map/pairs/pallas_call | solution.py:332
  14.0 0.0 collective-permute-done
  14.0 0.0 collective-permute-done.2
  14.1 1.6 %collective-permute-start.3 = (f32[2,104,128]{2,1,0:T(8,128)S(1)}, f32[2,104,128]{2,1,0:T(8,128)S(1)}, u32[]{:S(2)}, u32[]{:S(2)}) collective-permute-start(f32[2,104,128]{2,1,0:T(8,128)S(1)} %pad_maximum_fusion.1), channel_id=1, source_target_pairs={{0,4},{4,0},{8,12},{12,8},{16,20},{20,16},{24,28},{28,24},{1,5},{5... | collective-permute-start | bytes 319496 | tf_op jit(solution)/shard_map/ppermute | solution.py:307
  15.7 3.6 %collective-permute-start.4 = (f32[4,104,128]{2,1,0:T(8,128)S(1)}, f32[4,104,128]{2,1,0:T(8,128)S(1)}, u32[]{:S(2)}, u32[]{:S(2)}) collective-permute-start(f32[4,104,128]{2,1,0:T(8,128)S(1)} %pad_maximum_fusion), channel_id=1, source_target_pairs={{0,28},{4,8},{8,4},{12,16},{16,12},{20,24},{24,20},{28,0},{1,29},{... | collective-permute-start | bytes 638984 | tf_op jit(solution)/shard_map/ppermute | solution.py:307
  19.3 0.0 collective-permute-done.5.refs_0_
  19.3 4.4 %pairs.4 = (f32[768,128]{1,0:T(8,128)S(1)}, f32[192,128]{1,0:T(8,128)S(1)}) custom-call(f32[2,104,128]{2,1,0:T(8,128)S(1)} %collective-permute-done.5.refs_0_, f32[1,104,128]{2,1,0:T(8,128)S(1)} %slice.147.refs_1_, f32[1,104,128]{2,1,0:T(8,128)S(1)} %slice.148.refs_2_, f32[768,128]{1,0:T(8,128)S(1)} %bitcast.35, ...), custom_call_target="tpu_custom_call", output_to_operand_aliasing={{0}: (5, {})} | custom-call | flops 4000000000 | bytes 2000000 | tf_op jit(solution)/shard_map/pairs/pallas_call | solution.py:332
  23.7 0.0 collective-permute-done.3.refs_0_
  23.8 2.3 %collective-permute-done.4.refs_1_ = f32[4,104,128]{2,1,0:T(8,128)S(1)} collective-permute-done((f32[4,104,128]{2,1,0:T(8,128)S(1)}, f32[4,104,128]{2,1,0:T(8,128)S(1)}, u32[]{:S(2)}, u32[]{:S(2)}) %collective-permute-start.4) | collective-permute-done | bytes 213024 | tf_op jit(solution)/shard_map/ppermute | solution.py:307
  26.0 11.1 %pairs.5 = (f32[768,128]{1,0:T(8,128)S(1)}, f32[288,128]{1,0:T(8,128)S(1)}) custom-call(f32[2,104,128]{2,1,0:T(8,128)S(1)} %collective-permute-done.3.refs_0_, f32[4,104,128]{2,1,0:T(8,128)S(1)} %collective-permute-done.4.refs_1_, f32[768,128]{1,0:T(8,128)S(1)} %bitcast.36, f32[768,128]{1,0:T(8,128)S(1)} %bitcast.40, ...), custom_call_target="tpu_custom_call", output_to_operand_aliasing={{0}: (4, {})} | custom-call | flops 6000000000 | bytes 2000000 | tf_op jit(solution)/shard_map/pairs/pallas_call | solution.py:332
  37.2 0.1 collective-permute-start.6
  37.3 0.6 %collective-permute-start.7 = (f32[4,48,128]{2,1,0:T(8,128)S(1)}, f32[4,48,128]{2,1,0:T(8,128)S(1)}, u32[]{:S(2)}, u32[]{:S(2)}) collective-permute-start(f32[4,48,128]{2,1,0:T(8,128)S(1)} %bitcast.44), channel_id=1, source_target_pairs={{0,28},{4,8},{8,4},{12,16},{16,12},{20,24},{24,20},{28,0},{1,29},{... | collective-permute-start | bytes 294920 | tf_op jit(solution)/shard_map/ppermute | solution.py:307
  37.9 5.0 %collective-permute-done.6 = f32[4,48,128]{2,1,0:T(8,128)S(1)} collective-permute-done((f32[4,48,128]{2,1,0:T(8,128)S(1)}, f32[4,48,128]{2,1,0:T(8,128)S(1)}, u32[]{:S(2)}, u32[]{:S(2)}) %collective-permute-start.6) | collective-permute-done | bytes 98336 | tf_op jit(solution)/shard_map/ppermute | solution.py:307
  42.9 1.7 %collective-permute-done.7 = f32[4,48,128]{2,1,0:T(8,128)S(1)} collective-permute-done((f32[4,48,128]{2,1,0:T(8,128)S(1)}, f32[4,48,128]{2,1,0:T(8,128)S(1)}, u32[]{:S(2)}, u32[]{:S(2)}) %collective-permute-start.7) | collective-permute-done | bytes 98336 | tf_op jit(solution)/shard_map/ppermute | solution.py:307
  44.7 0.1 collective-permute-start.8
  44.8 1.3 %collective-permute-start.9 = (f32[3,48,128]{2,1,0:T(8,128)S(1)}, f32[3,48,128]{2,1,0:T(8,128)S(1)}, u32[]{:S(2)}, u32[]{:S(2)}) collective-permute-start(f32[3,48,128]{2,1,0:T(8,128)S(1)} %pad_maximum_fusion.6), channel_id=1, source_target_pairs={{0,2},{1,3},{2,0},{3,1},{4,6},{5,7},{6,4},{7,5},{8,10},{9,11},{10,... | collective-permute-start | bytes 221192 | tf_op jit(solution)/shard_map/ppermute | solution.py:303
  46.1 0.6 %collective-permute-start.10 = (f32[3,48,128]{2,1,0:T(8,128)S(1)}, f32[3,48,128]{2,1,0:T(8,128)S(1)}, u32[]{:S(2)}, u32[]{:S(2)}) collective-permute-start(f32[3,48,128]{2,1,0:T(8,128)S(1)} %pad_maximum_fusion.7), channel_id=1, source_target_pairs={{0,3},{1,2},{2,1},{3,0},{4,7},{5,6},{6,5},{7,4},{8,11},{9,10},{10,... | collective-permute-start | bytes 221192 | tf_op jit(solution)/shard_map/ppermute | solution.py:303
  46.7 0.0 collective-permute-done.8.refs_1_
  46.7 3.2 %collective-permute-done.9.refs_2_ = f32[3,48,128]{2,1,0:T(8,128)S(1)} collective-permute-done((f32[3,48,128]{2,1,0:T(8,128)S(1)}, f32[3,48,128]{2,1,0:T(8,128)S(1)}, u32[]{:S(2)}, u32[]{:S(2)}) %collective-permute-start.9) | collective-permute-done | bytes 73760 | tf_op jit(solution)/shard_map/ppermute | solution.py:303
  49.9 0.7 %collective-permute-done.10.refs_3_ = f32[3,48,128]{2,1,0:T(8,128)S(1)} collective-permute-done((f32[3,48,128]{2,1,0:T(8,128)S(1)}, f32[3,48,128]{2,1,0:T(8,128)S(1)}, u32[]{:S(2)}, u32[]{:S(2)}) %collective-permute-start.10) | collective-permute-done | bytes 73760 | tf_op jit(solution)/shard_map/ppermute | solution.py:303
  50.6 0.6 %copy-done.2 = s32[48]{0:T(128)S(1)} copy-done((s32[48]{0:T(128)S(1)}, s32[48]{0:T(128)}, u32[]{:S(2)}) %copy-start.2) | copy-done | bytes 216
  51.2 1.6 %add.25 = f32[768,128]{1,0:T(8,128)} custom-call(s32[48]{0:T(128)S(1)} %copy-done.2, f32[768,128]{1,0:T(8,128)S(1)} %get-tuple-element.25.acc, f32[3,48,128]{2,1,0:T(8,128)S(1)} %pad_maximum_fusion.4.refs_0_, f32[3,48,128]{2,1,0:T(8,128)S(1)} %collective-permute-done.8.refs_1_, f32[3,48,128]{2,1,0:T(8,128)S(1)} %collective-permute-done.9.refs_2_, ...), custom_call_target="tpu_custom_call" | custom-call | tf_op jit(solution)/shard_map/add/pallas_call | solution.py:372
  (22 shorter events, 0.2 us)
Async XLA Ops:
  3.9 10.1 %collective-permute-start = (f32[3,104,128]{2,1,0:T(8,128)}, f32[3,104,128]{2,1,0:T(8,128)S(1)}, u32[]{:S(2)}, u32[]{:S(2)}) collective-permute-start(f32[3,104,128]{2,1,0:T(8,128)} %get-tuple-element.18), channel_id=1, source_target_pairs={{0,2},{1,3},{2,0},{3,1},{4,6},{5,7},{6,4},{7,5},{8,10},{9,11},{10,... | collective-permute-start | bytes 479240 | tf_op jit(solution)/shard_map/ppermute | solution.py:303
  6.9 1.6 %collective-permute-start.1 = (f32[3,104,128]{2,1,0:T(8,128)}, f32[3,104,128]{2,1,0:T(8,128)S(1)}, u32[]{:S(2)}, u32[]{:S(2)}) collective-permute-start(f32[3,104,128]{2,1,0:T(8,128)} %get-tuple-element.20), channel_id=1, source_target_pairs={{0,1},{1,0},{2,3},{3,2},{4,5},{5,4},{6,7},{7,6},{8,9},{9,8},{10,11... | collective-permute-start | bytes 479240 | tf_op jit(solution)/shard_map/ppermute | solution.py:303
  6.9 7.1 %collective-permute-start.2 = (f32[3,104,128]{2,1,0:T(8,128)}, f32[3,104,128]{2,1,0:T(8,128)S(1)}, u32[]{:S(2)}, u32[]{:S(2)}) collective-permute-start(f32[3,104,128]{2,1,0:T(8,128)} %get-tuple-element.22), channel_id=1, source_target_pairs={{0,3},{1,2},{2,1},{3,0},{4,7},{5,6},{6,5},{7,4},{8,11},{9,10},{10,... | collective-permute-start | bytes 479240 | tf_op jit(solution)/shard_map/ppermute | solution.py:303
  7.1 3.0 %copy-start = (f32[64,3,512]{2,0,1:T(8,128)S(1)}, f32[64,3,512]{2,0,1:T(8,128)}, u32[]{:S(2)}) copy-start(f32[64,3,512]{2,0,1:T(8,128)} %param.4) | copy-start | bytes 1179652
  7.1 3.0 %copy-start.1 = (f32[64,3,512]{2,0,1:T(8,128)S(1)}, f32[64,3,512]{2,0,1:T(8,128)}, u32[]{:S(2)}) copy-start(f32[64,3,512]{2,0,1:T(8,128)} %param.5) | copy-start | bytes 1179652
  8.5 10.8 %collective-permute-start.5 = (f32[2,104,128]{2,1,0:T(8,128)S(1)}, f32[2,104,128]{2,1,0:T(8,128)S(1)}, u32[]{:S(2)}, u32[]{:S(2)}) collective-permute-start(f32[2,104,128]{2,1,0:T(8,128)S(1)} %pad_maximum_fusion.2), channel_id=1, source_target_pairs={{0,4},{4,0},{8,12},{12,8},{16,20},{20,16},{24,28},{28,24},{1,5},{5... | collective-permute-start | bytes 319496 | tf_op jit(solution)/shard_map/ppermute | solution.py:307
  14.1 9.7 %collective-permute-start.3 = (f32[2,104,128]{2,1,0:T(8,128)S(1)}, f32[2,104,128]{2,1,0:T(8,128)S(1)}, u32[]{:S(2)}, u32[]{:S(2)}) collective-permute-start(f32[2,104,128]{2,1,0:T(8,128)S(1)} %pad_maximum_fusion.1), channel_id=1, source_target_pairs={{0,4},{4,0},{8,12},{12,8},{16,20},{20,16},{24,28},{28,24},{1,5},{5... | collective-permute-start | bytes 319496 | tf_op jit(solution)/shard_map/ppermute | solution.py:307
  15.7 10.4 %collective-permute-start.4 = (f32[4,104,128]{2,1,0:T(8,128)S(1)}, f32[4,104,128]{2,1,0:T(8,128)S(1)}, u32[]{:S(2)}, u32[]{:S(2)}) collective-permute-start(f32[4,104,128]{2,1,0:T(8,128)S(1)} %pad_maximum_fusion), channel_id=1, source_target_pairs={{0,28},{4,8},{8,4},{12,16},{16,12},{20,24},{24,20},{28,0},{1,29},{... | collective-permute-start | bytes 638984 | tf_op jit(solution)/shard_map/ppermute | solution.py:307
  37.2 5.7 %collective-permute-start.6 = (f32[4,48,128]{2,1,0:T(8,128)S(1)}, f32[4,48,128]{2,1,0:T(8,128)S(1)}, u32[]{:S(2)}, u32[]{:S(2)}) collective-permute-start(f32[4,48,128]{2,1,0:T(8,128)S(1)} %pad_maximum_fusion.3), channel_id=1, source_target_pairs={{0,4},{4,0},{8,12},{12,8},{16,20},{20,16},{24,28},{28,24},{1,5},{5... | collective-permute-start | bytes 294920 | tf_op jit(solution)/shard_map/ppermute | solution.py:307
  37.3 7.4 %collective-permute-start.7 = (f32[4,48,128]{2,1,0:T(8,128)S(1)}, f32[4,48,128]{2,1,0:T(8,128)S(1)}, u32[]{:S(2)}, u32[]{:S(2)}) collective-permute-start(f32[4,48,128]{2,1,0:T(8,128)S(1)} %bitcast.44), channel_id=1, source_target_pairs={{0,28},{4,8},{8,4},{12,16},{16,12},{20,24},{24,20},{28,0},{1,29},{... | collective-permute-start | bytes 294920 | tf_op jit(solution)/shard_map/ppermute | solution.py:307
  44.7 2.0 %collective-permute-start.8 = (f32[3,48,128]{2,1,0:T(8,128)S(1)}, f32[3,48,128]{2,1,0:T(8,128)S(1)}, u32[]{:S(2)}, u32[]{:S(2)}) collective-permute-start(f32[3,48,128]{2,1,0:T(8,128)S(1)} %pad_maximum_fusion.5), channel_id=1, source_target_pairs={{0,1},{1,0},{2,3},{3,2},{4,5},{5,4},{6,7},{7,6},{8,9},{9,8},{10,11... | collective-permute-start | bytes 221192 | tf_op jit(solution)/shard_map/ppermute | solution.py:303
  44.8 5.1 %collective-permute-start.9 = (f32[3,48,128]{2,1,0:T(8,128)S(1)}, f32[3,48,128]{2,1,0:T(8,128)S(1)}, u32[]{:S(2)}, u32[]{:S(2)}) collective-permute-start(f32[3,48,128]{2,1,0:T(8,128)S(1)} %pad_maximum_fusion.6), channel_id=1, source_target_pairs={{0,2},{1,3},{2,0},{3,1},{4,6},{5,7},{6,4},{7,5},{8,10},{9,11},{10,... | collective-permute-start | bytes 221192 | tf_op jit(solution)/shard_map/ppermute | solution.py:303
  46.1 4.5 %collective-permute-start.10 = (f32[3,48,128]{2,1,0:T(8,128)S(1)}, f32[3,48,128]{2,1,0:T(8,128)S(1)}, u32[]{:S(2)}, u32[]{:S(2)}) collective-permute-start(f32[3,48,128]{2,1,0:T(8,128)S(1)} %pad_maximum_fusion.7), channel_id=1, source_target_pairs={{0,3},{1,2},{2,1},{3,0},{4,7},{5,6},{6,5},{7,4},{8,11},{9,10},{10,... | collective-permute-start | bytes 221192 | tf_op jit(solution)/shard_map/ppermute | solution.py:303
  50.6 0.6 %copy-start.2 = (s32[48]{0:T(128)S(1)}, s32[48]{0:T(128)}, u32[]{:S(2)}) copy-start(s32[48]{0:T(128)} %get-tuple-element.17.table) | copy-start | bytes 580
where the time goes:
time: 53.1 us; the launch traced here: 52.8 us
  Pallas kernels  24.2 us (46%)
  waiting for transfers between devices  13.4 us (25%)
  starting transfers between devices  12.6 us (24%)
  local copies, waits for them, and re-layouts  1.67 us (3%)
  between operations  0.83 us (2%)
    pallas_call x3, Pallas kernels, pairs(): pl.pallas_call(functools.partial(pair_kernel, sizes, kinds, len(before)),...  19.4 us
    ppermute x5, waiting for transfers between devices, beyond(): return lax.ppermute(value, 'space', moves)  9.03 us
    ppermute x5, starting transfers between devices, beyond(): return lax.ppermute(value, 'space', moves)  7.47 us
    ppermute x6, starting transfers between devices, across(): return lax.ppermute(value, 'pairs', [(j, j ^ turn) for j in range(n_pairs)])  5.13 us
    ppermute x6, waiting for transfers between devices, across(): return lax.ppermute(value, 'pairs', [(j, j ^ turn) for j in range(n_pairs)])  4.4 us
    pallas_call x1, Pallas kernels, body(): pl.pallas_call(functools.partial(pack_kernel, sizes), out_shape=[message]...  3.22 us
    pallas_call x1, Pallas kernels, body(): pl.pallas_call(functools.partial(add_kernel, sizes), out_shape=total, in_...  1.59 us
  transfers between devices with their start and end apart: 11, of which 6 were waited for; matrix products, arithmetic and copies ran while one was open for 2% of the time, Pallas kernels for 16%

commit v1 on v0

--- a/solution.py
+++ b/solution.py
@@ -118,8 +118,8 @@
 
 def pack_kernel(sizes, cells, count, pos_hbm, frc_hbm, *refs):
     n_space, n_pairs, share, cell_dev, tiles = sizes
-    outs, table = refs[:n_pairs], refs[n_pairs]
-    slots, used, pos, frc, sems = refs[n_pairs + 1 :]
+    targets, table = refs[:n_pairs], refs[n_pairs]
+    slots, used, pos, frc, built, sems, out_sems = refs[n_pairs + 1 :]
     fetches = [
         pltpu.make_async_copy(pos_hbm, pos, sems.at[0]),
         pltpu.make_async_copy(frc_hbm, frc, sems.at[1]),
@@ -145,9 +145,10 @@
         fetch.wait()
     lane = lax.broadcasted_iota(jnp.int32, (1, LANES), 1)
     plane = cell_dev * tiles
-    for m in range(3 * n_pairs):
-        kind, turn = m // n_pairs, m % n_pairs
-        out = outs[turn]
+    sends = []
+    for turn, kind in [(turn, kind) for turn in reversed(range(n_pairs)) for kind in range(3)]:
+        m = kind * n_pairs + turn
+        out = built.at[turn]
         label = jnp.full((1, LANES), -1.0, f32)
         for k in range(share):
             s = slots[m * share + k]
@@ -165,11 +166,18 @@
                 ]
         last = share * 6 * tiles
         out[kind, last : last + 1, :] = label
-
-
-def pair_kernel(sizes, kinds, started, *refs):
+        if kind == 2:
+            send = pltpu.make_async_copy(out, targets[turn], out_sems.at[turn])
+            send.start()
+            sends.append(send)
+    for send in sends:
+        send.wait()
+
+
+def pair_kernel(sizes, kinds, started, extra, *refs):
     n_space, n_pairs, share, cell_dev, tiles = sizes
     n = len(kinds)
+    refs = refs[extra:]
     messages, (pos, frc) = refs[:n], refs[n : n + 2]
     outs = refs[n + 2 + started :]
     (acc, reply), (inbox, todo, middles) = outs[:2], outs[-3:]
@@ -250,23 +258,27 @@
 
 def add_kernel(sizes, table, acc, *refs):
     n_space, n_pairs, share, cell_dev, tiles = sizes
-    replies, out = refs[:-1], refs[-1]
+    replies, (out, *others) = refs[:n_pairs], refs[n_pairs:]
     plane = cell_dev * tiles
     out[...] = acc[...]
-    for m in range(3 * n_pairs):
-        kind, turn = m // n_pairs, m % n_pairs
+    for other in others:
+        other[...] = jnp.zeros_like(other)
+    chains = [out, *others]
+    for turn in range(n_pairs):
         for k in range(share):
-            a = table[m * share + k]
-            live = a >= 0
-            base = row_base(jnp.maximum(a, 0), tiles)
-            places = [pl.ds(base + c * plane, tiles, stride=8) for c in range(3)]
-            totals = []
-            for c in range(3):
-                row = (k * 3 + c) * tiles
-                term = jnp.where(live, replies[turn][kind, row : row + tiles, :], 0.0)
-                totals.append(out[places[c], :] + term)
-            for c in range(3):
-                out[places[c], :] = totals[c]
+            steps = []
+            for kind, chain in enumerate(chains):
+                a = table[(kind * n_pairs + turn) * share + k]
+                live = a >= 0
+                base = row_base(jnp.maximum(a, 0), tiles)
+                for c in range(3):
+                    place = pl.ds(base + c * plane, tiles, stride=8)
+                    row = (k * 3 + c) * tiles
+                    term = jnp.where(live, replies[turn][kind, row : row + tiles, :], 0.0)
+                    steps.append((chain, place, chain[place, :] + term))
+            for chain, place, value in steps:
+                chain[place, :] = value
+    out[...] += others[0][...] + others[1][...]
 
 
 def flat_rows(cells):
@@ -310,13 +322,15 @@
         functools.partial(pack_kernel, sizes),
         out_shape=[message] * n_pairs + [jax.ShapeDtypeStruct((n_slots,), jnp.int32)],
         in_specs=[smem, smem, hbm, hbm],
-        out_specs=[vmem] * n_pairs + [smem],
+        out_specs=[hbm] * n_pairs + [smem],
         scratch_shapes=[
             pltpu.SMEM((n_slots,), jnp.int32),
             pltpu.SMEM((3 * n_pairs,), jnp.int32),
             pltpu.VMEM(total.shape, f32),
             pltpu.VMEM(total.shape, f32),
+            pltpu.VMEM((n_pairs,) + message.shape, f32),
             pltpu.SemaphoreType.DMA((2,)),
+            pltpu.SemaphoreType.DMA((n_pairs,)),
         ],
         compiler_params=pltpu.CompilerParams(vmem_limit_bytes=60 * 1024 * 1024),
         name="pack",
@@ -324,29 +338,29 @@
     sent, table = packed[:n_pairs], packed[n_pairs]
     got = [sent[0]] + [across(sent[turn], turn) for turn in range(1, n_pairs)]
 
-    def pairs(arrived, before):
+    def pairs(arrived, before, extra=()):
         kinds = [kind for kind, _ in arrived]
         values = [value for _, value in arrived]
         n = len(values)
         blocks = sum(value.shape[0] for value in values)
         return pl.pallas_call(
-            functools.partial(pair_kernel, sizes, kinds, len(before)),
+            functools.partial(pair_kernel, sizes, kinds, len(before), len(extra)),
             out_shape=[total, jax.ShapeDtypeStruct((blocks * rows_out, LANES), f32)]
             + [jax.ShapeDtypeStruct((1, LANES), f32)] * (not before),
-            in_specs=[vmem] * (n + 2 + len(before)),
+            in_specs=[spec for spec, _ in extra] + [vmem] * (n + 2 + len(before)),
             out_specs=[vmem] * (2 + (not before)),
             scratch_shapes=[
                 pltpu.VMEM((blocks * rows_in, LANES), f32),
                 pltpu.SMEM((2, blocks * share + 1), jnp.int32),
                 pltpu.SMEM((2, blocks * share + 1), f32),
             ],
-            input_output_aliases={n + 2: 0} if before else {},
+            input_output_aliases={len(extra) + n + 2: 0} if before else {},
             compiler_params=pltpu.CompilerParams(vmem_limit_bytes=48 * 1024 * 1024),
             cost_estimate=pl.CostEstimate(
                 flops=blocks * 1_000_000_000, bytes_accessed=2_000_000, transcendentals=2_000_000
             ),
             name="pairs",
-        )(*values, pos, frc, *before)
+        )(*[value for _, value in extra], *values, pos, frc, *before)
 
     near, far = range(2), range(2, n_pairs)
     own = [sent[0][kind : kind + 1] for kind in range(3)]
@@ -354,17 +368,27 @@
     out_1n = beyond(jnp.concatenate([own[1], core[1]]), 1)
     acc, reply_0n, nothing = pairs([(0, own[0]), (0, core[0])], [])
     rest = [got[turn] + nothing[None] for turn in far]
+    out_2 = beyond(jnp.concatenate([own[2], core[2]] + [value[2:] for value in rest]), 2)
     out_1f = beyond(jnp.stack([value[1] for value in rest]), 1)
-    out_2 = beyond(jnp.concatenate([own[2], core[2]] + [value[2:] for value in rest]), 2)
-    acc, reply_m = pairs([(1, out_1n)] + [(0, got[turn][0:1]) for turn in far], [acc])
-    acc, reply_f = pairs([(1, out_1f), (2, out_2)], [acc])
-    reply_0n, reply_m, reply_f = (
-        value.reshape(-1, rows_out, LANES) for value in (reply_0n, reply_m, reply_f)
-    )
-    cut = n_pairs - 2
-    back_0 = jnp.concatenate([reply_0n, reply_m[2:]])
-    back_1 = beyond(jnp.concatenate([reply_m[:2], reply_f[:cut]]), 1)
-    back_2 = beyond(reply_f[cut:], 2)
+    half = (n_pairs - 2) // 2
+    early, late = far[:half], far[half:]
+    acc, reply_m = pairs(
+        [(1, out_1n)] + [(0, got[turn][0:1]) for turn in early], [acc], [(smem, table)]
+    )
+    acc, reply_2 = pairs([(2, out_2)], [acc])
+    back_2 = beyond(reply_2, 2)
+    acc, reply_l = pairs(
+        [(0, got[turn][0:1]) for turn in late] + [(1, out_1f[:half])], [acc]
+    )
+    acc, reply_f = pairs([(1, out_1f[half:])], [acc], [(hbm, back_2)])
+    reply_0n, reply_m, reply_l, reply_f, back_2 = (
+        value.reshape(-1, rows_out, LANES)
+        for value in (reply_0n, reply_m, reply_l, reply_f, back_2)
+    )
+    back_0 = jnp.concatenate([reply_0n, reply_m[2:], reply_l[:half]])
+    back_1n = beyond(reply_m[:2], 1)
+    back_1f = beyond(jnp.concatenate([reply_l[half:], reply_f]), 1)
+    back_1 = jnp.concatenate([back_1n, back_1f])
     back = []
     for turn in range(n_pairs):
         value = jnp.stack([back_0[turn], back_1[turn], back_2[turn]])
@@ -374,6 +398,7 @@
         out_shape=total,
         in_specs=[smem] + [vmem] * (1 + n_pairs),
         out_specs=vmem,
+        scratch_shapes=[pltpu.VMEM(total.shape, f32)] * 2,
         compiler_params=pltpu.CompilerParams(vmem_limit_bytes=48 * 1024 * 1024),
         name="add",
     )(table, acc, *back)

time: 53.1 us -> 56.1 us (1.056); the launches traced: 52.8 us -> 56.8 us
  waiting for transfers between devices: 13.4 us -> 20.6 us
  starting transfers between devices: 12.6 us -> 10.7 us
  Pallas kernels: 24.2 us -> 22.9 us
    ppermute x6, waiting for transfers between devices: 4.4 us -> 9.53 us  [across(): return lax.ppermute(value, 'pairs', [(j, j ^ turn) for j in range(n_pairs)])]
    ppermute x5 -> x6, waiting for transfers between devices: 9.03 us -> 11 us  [beyond(): return lax.ppermute(value, 'space', moves)]
    ppermute x6, starting transfers between devices: 5.13 us -> 3.36 us  [across(): return lax.ppermute(value, 'pairs', [(j, j ^ turn) for j in range(n_pairs)])]
    pallas_call x3 -> x5, Pallas kernels: 19.4 us -> 17.7 us  [pairs(): pl.pallas_call(functools.partial(pair_kernel, sizes, kinds, len(before),...]
    ppermute x5 -> x6, starting transfers between devices: 7.47 us -> 7.33 us  [beyond(): return lax.ppermute(value, 'space', moves)]
  transfers between devices with their start and end apart: 11 -> 12, of which waited for: 6 -> 6; matrix products, arithmetic and copies ran while one was open for 2% -> 2% of each run, Pallas kernels for 16% -> 16%
where the time goes in v1:
time: 56.1 us; the launch traced here: 56.8 us
  Pallas kernels  22.9 us (41%)
  waiting for transfers between devices  20.6 us (37%)
  starting transfers between devices  10.7 us (19%)
  local copies, waits for them, and re-layouts  1.61 us (3%)
  between operations  0.89 us (2%)
    pallas_call x5, Pallas kernels, pairs(): pl.pallas_call(functools.partial(pair_kernel, sizes, kinds, len(before),...  17.7 us
    ppermute x6, waiting for transfers between devices, beyond(): return lax.ppermute(value, 'space', moves)  11 us
    ppermute x6, waiting for transfers between devices, across(): return lax.ppermute(value, 'pairs', [(j, j ^ turn) for j in range(n_pairs)])  9.53 us
    ppermute x6, starting transfers between devices, beyond(): return lax.ppermute(value, 'space', moves)  7.33 us
    pallas_call x1, Pallas kernels, body(): pl.pallas_call(functools.partial(pack_kernel, sizes), out_shape=[message]...  3.62 us
    ppermute x6, starting transfers between devices, across(): return lax.ppermute(value, 'pairs', [(j, j ^ turn) for j in range(n_pairs)])  3.36 us
    pallas_call x1, Pallas kernels, body(): pl.pallas_call(functools.partial(add_kernel, sizes), out_shape=total, in_...  1.64 us
  transfers between devices with their start and end apart: 12, of which 6 were waited for; matrix products, arithmetic and copies ran while one was open for 2% of the time, Pallas kernels for 16%

profile of v1, /device:TPU:0, one launch (start us, length us, event | category | flops | bytes accessed | tf_op | source)
XLA Modules:
  0.0 56.8 jit_solution(7316261150497711750)
XLA Ops:
  0.7 3.6 %pack.1 = (f32[3,104,128]{2,1,0:T(8,128)}, f32[3,104,128]{2,1,0:T(8,128)}, f32[3,104,128]{2,1,0:T(8,128)}, f32[3,104,128]{2,1,0:T(8,128)}, s32[48]{0:T(128)}) custom-call(s32[2,48]{1,0:T(2,128)} %cells.1, s32[1]{0:T(128)S(6)} %copy.13.count, f32[768,128]{1,0:T(8,128)} %bitcast.42, f32[768,128]{1,0:T(8,128)} %bitcast.48), custom_call_target="tpu_custom_call" | custom-call | tf_op jit(solution)/shard_map/pack/pallas_call | solution.py:321
  4.3 0.5 collective-permute-start
  4.8 2.6 %collective-permute-start.1 = (f32[3,104,128]{2,1,0:T(8,128)}, f32[3,104,128]{2,1,0:T(8,128)S(1)}, u32[]{:S(2)}, u32[]{:S(2)}) collective-permute-start(f32[3,104,128]{2,1,0:T(8,128)} %get-tuple-element.24), channel_id=1, source_target_pairs={{0,2},{1,3},{2,0},{3,1},{4,6},{5,7},{6,4},{7,5},{8,10},{9,11},{10,... | collective-permute-start | bytes 479240 | tf_op jit(solution)/shard_map/ppermute | solution.py:315
  7.4 0.1 collective-permute-start.2
  7.4 0.9 %fusion.2 = (f32[1,104,128]{2,1,0:T(8,128)S(1)}, f32[1,104,128]{2,1,0:T(8,128)S(1)}, f32[1,104,128]{2,1,0:T(8,128)S(1)}) fusion(f32[3,104,128]{2,1,0:T(8,128)} %get-tuple-element.22), kind=kLoop, calls=%fused_computation.21 | loop fusion | bytes 319488 | tf_op jit(solution)/shard_map/slice | solution.py:366
  8.4 0.0 collective-permute-done
  8.4 1.8 %collective-permute-start.4 = (f32[2,104,128]{2,1,0:T(8,128)S(1)}, f32[2,104,128]{2,1,0:T(8,128)S(1)}, u32[]{:S(2)}, u32[]{:S(2)}) collective-permute-start(f32[2,104,128]{2,1,0:T(8,128)S(1)} %pad_maximum_fusion.1), channel_id=1, source_target_pairs={{0,4},{4,0},{8,12},{12,8},{16,20},{20,16},{24,28},{28,24},{1,5},{5... | collective-permute-start | bytes 319496 | tf_op jit(solution)/shard_map/ppermute | solution.py:319
  10.3 0.2 pairs.5
  10.4 2.1 %collective-permute-done.1 = f32[3,104,128]{2,1,0:T(8,128)S(1)} collective-permute-done((f32[3,104,128]{2,1,0:T(8,128)}, f32[3,104,128]{2,1,0:T(8,128)S(1)}, u32[]{:S(2)}, u32[]{:S(2)}) %collective-permute-start.1) | collective-permute-done | bytes 159776 | tf_op jit(solution)/shard_map/ppermute | solution.py:315
  12.5 2.9 %collective-permute-done.2 = f32[3,104,128]{2,1,0:T(8,128)S(1)} collective-permute-done((f32[3,104,128]{2,1,0:T(8,128)}, f32[3,104,128]{2,1,0:T(8,128)S(1)}, u32[]{:S(2)}, u32[]{:S(2)}) %collective-permute-start.2) | collective-permute-done | bytes 159776 | tf_op jit(solution)/shard_map/ppermute | solution.py:315
  15.5 1.7 %collective-permute-start.6 = (f32[2,104,128]{2,1,0:T(8,128)S(1)}, f32[2,104,128]{2,1,0:T(8,128)S(1)}, u32[]{:S(2)}, u32[]{:S(2)}) collective-permute-start(f32[2,104,128]{2,1,0:T(8,128)S(1)} %pad_maximum_fusion.2), channel_id=1, source_target_pairs={{0,4},{4,0},{8,12},{12,8},{16,20},{20,16},{24,28},{28,24},{1,5},{5... | collective-permute-start | bytes 319496 | tf_op jit(solution)/shard_map/ppermute | solution.py:319
  17.2 3.6 %collective-permute-start.3 = (f32[4,104,128]{2,1,0:T(8,128)S(1)}, f32[4,104,128]{2,1,0:T(8,128)S(1)}, u32[]{:S(2)}, u32[]{:S(2)}) collective-permute-start(f32[4,104,128]{2,1,0:T(8,128)S(1)} %pad_maximum_fusion), channel_id=1, source_target_pairs={{0,28},{4,8},{8,4},{12,16},{16,12},{20,24},{24,20},{28,0},{1,29},{... | collective-permute-start | bytes 638984 | tf_op jit(solution)/shard_map/ppermute | solution.py:319
  20.8 0.0 collective-permute-done.4.refs_1_
  20.8 0.6 copy-done.2
  21.4 4.4 %pairs.6 = (f32[768,128]{1,0:T(8,128)S(1)}, f32[144,128]{1,0:T(8,128)S(1)}) custom-call(s32[48]{0:T(128)S(1)} %copy-done.2, f32[2,104,128]{2,1,0:T(8,128)S(1)} %collective-permute-done.4.refs_1_, f32[1,104,128]{2,1,0:T(8,128)S(1)} %slice.157.refs_2_, f32[768,128]{1,0:T(8,128)S(1)} %bitcast.44, ...), custom_call_target="tpu_custom_call", output_to_operand_aliasing={{0}: (5, {})} | custom-call | flops 3000000000 | bytes 2000000 | tf_op jit(solution)/shard_map/pairs/pallas_call | solution.py:346
  25.8 0.1 collective-permute-start.7
  25.9 0.0 collective-permute-done.6
  25.9 4.0 %collective-permute-done.7 = f32[2,48,128]{2,1,0:T(8,128)S(1)} collective-permute-done((f32[2,48,128]{2,1,0:T(8,128)S(1)}, f32[2,48,128]{2,1,0:T(8,128)S(1)}, u32[]{:S(2)}, u32[]{:S(2)}) %collective-permute-start.7) | collective-permute-done | bytes 49184 | tf_op jit(solution)/shard_map/ppermute | solution.py:319
  30.0 0.0 collective-permute-done.3.refs_0_
  30.0 5.9 %pairs.7 = (f32[768,128]{1,0:T(8,128)S(1)}, f32[192,128]{1,0:T(8,128)S(1)}) custom-call(f32[4,104,128]{2,1,0:T(8,128)S(1)} %collective-permute-done.3.refs_0_, f32[768,128]{1,0:T(8,128)S(1)} %bitcast.45, f32[768,128]{1,0:T(8,128)S(1)} %bitcast.51, f32[768,128]{1,0:T(8,128)S(1)} %get-tuple-element.28.refs_3_), custom_call_target="tpu_custom_call", output_to_operand_aliasing={{0}: (3, {})} | custom-call | flops 4000000000 | bytes 2000000 | tf_op jit(solution)/shard_map/pairs/pallas_call | solution.py:346
  35.9 0.1 collective-permute-start.5
  36.0 4.4 %pairs.8 = (f32[768,128]{1,0:T(8,128)S(1)}, f32[96,128]{1,0:T(8,128)S(1)}) custom-call(f32[1,104,128]{2,1,0:T(8,128)S(1)} %slice.161.refs_0_, f32[1,104,128]{2,1,0:T(8,128)S(1)} %get-tuple-element.47.refs_1_, f32[768,128]{1,0:T(8,128)S(1)} %bitcast.46, f32[768,128]{1,0:T(8,128)S(1)} %bitcast.52, ...), custom_call_target="tpu_custom_call", output_to_operand_aliasing={{0}: (4, {})} | custom-call | flops 2000000000 | bytes 2000000 | tf_op jit(solution)/shard_map/pairs/pallas_call | solution.py:346
  40.3 3.0 %collective-permute-done.5.refs_0_ = f32[192,128]{1,0:T(8,128)S(1)} collective-permute-done((f32[192,128]{1,0:T(8,128)S(1)}, f32[192,128]{1,0:T(8,128)S(1)}, u32[]{:S(2)}, u32[]{:S(2)}) %collective-permute-start.5) | collective-permute-done | bytes 98336 | tf_op jit(solution)/shard_map/ppermute | solution.py:319
  43.4 2.9 %pairs.9 = (f32[768,128]{1,0:T(8,128)S(1)}, f32[48,128]{1,0:T(8,128)S(1)}) custom-call(f32[192,128]{1,0:T(8,128)S(1)} %collective-permute-done.5.refs_0_, f32[1,104,128]{2,1,0:T(8,128)S(1)} %get-tuple-element.48.refs_1_, f32[768,128]{1,0:T(8,128)S(1)} %bitcast.47, f32[768,128]{1,0:T(8,128)S(1)} %bitcast.53, ...), custom_call_target="tpu_custom_call", output_to_operand_aliasing={{0}: (4, {})} | custom-call | flops 1000000000 | bytes 2000000 | tf_op jit(solution)/shard_map/pairs/pallas_call | solution.py:346
  46.3 0.1 collective-permute-start.9
  46.4 0.1 collective-permute-start.8
  46.5 4.0 %collective-permute-done.9 = f32[2,48,128]{2,1,0:T(8,128)S(1)} collective-permute-done((f32[2,48,128]{2,1,0:T(8,128)S(1)}, f32[2,48,128]{2,1,0:T(8,128)S(1)}, u32[]{:S(2)}, u32[]{:S(2)}) %collective-permute-start.9) | collective-permute-done | bytes 49184 | tf_op jit(solution)/shard_map/ppermute | solution.py:319
  50.4 0.1 collective-permute-start.10
  50.5 0.1 collective-permute-start.11
  50.6 0.0 collective-permute-done.8.refs_1_
  50.6 4.5 %collective-permute-done.10.refs_2_ = f32[3,48,128]{2,1,0:T(8,128)S(1)} collective-permute-done((f32[3,48,128]{2,1,0:T(8,128)S(1)}, f32[3,48,128]{2,1,0:T(8,128)S(1)}, u32[]{:S(2)}, u32[]{:S(2)}) %collective-permute-start.10) | collective-permute-done | bytes 73760 | tf_op jit(solution)/shard_map/ppermute | solution.py:315
  55.2 1.6 %add.25 = f32[768,128]{1,0:T(8,128)} custom-call(s32[48]{0:T(128)S(1)} %copy-done.2, f32[768,128]{1,0:T(8,128)S(1)} %get-tuple-element.32.acc, f32[3,48,128]{2,1,0:T(8,128)S(1)} %pad_maximum_fusion.3.refs_0_, f32[3,48,128]{2,1,0:T(8,128)S(1)} %collective-permute-done.8.refs_1_, f32[3,48,128]{2,1,0:T(8,128)S(1)} %collective-permute-done.10.refs_2_, ...), custom_call_target="tpu_custom_call" | custom-call | tf_op jit(solution)/shard_map/add/pallas_call | solution.py:396
  (27 shorter events, 0.2 us)
Async XLA Ops:
  4.3 4.1 %collective-permute-start = (f32[3,104,128]{2,1,0:T(8,128)}, f32[3,104,128]{2,1,0:T(8,128)S(1)}, u32[]{:S(2)}, u32[]{:S(2)}) collective-permute-start(f32[3,104,128]{2,1,0:T(8,128)} %get-tuple-element.23), channel_id=1, source_target_pairs={{0,1},{1,0},{2,3},{3,2},{4,5},{5,4},{6,7},{7,6},{8,9},{9,8},{10,11... | collective-permute-start | bytes 479240 | tf_op jit(solution)/shard_map/ppermute | solution.py:315
  4.8 7.7 %collective-permute-start.1 = (f32[3,104,128]{2,1,0:T(8,128)}, f32[3,104,128]{2,1,0:T(8,128)S(1)}, u32[]{:S(2)}, u32[]{:S(2)}) collective-permute-start(f32[3,104,128]{2,1,0:T(8,128)} %get-tuple-element.24), channel_id=1, source_target_pairs={{0,2},{1,3},{2,0},{3,1},{4,6},{5,7},{6,4},{7,5},{8,10},{9,11},{10,... | collective-permute-start | bytes 479240 | tf_op jit(solution)/shard_map/ppermute | solution.py:315
  7.4 8.1 %collective-permute-start.2 = (f32[3,104,128]{2,1,0:T(8,128)}, f32[3,104,128]{2,1,0:T(8,128)S(1)}, u32[]{:S(2)}, u32[]{:S(2)}) collective-permute-start(f32[3,104,128]{2,1,0:T(8,128)} %get-tuple-element.26), channel_id=1, source_target_pairs={{0,3},{1,2},{2,1},{3,0},{4,7},{5,6},{6,5},{7,4},{8,11},{9,10},{10,... | collective-permute-start | bytes 479240 | tf_op jit(solution)/shard_map/ppermute | solution.py:315
  7.4 2.8 %copy-start = (f32[64,3,512]{2,0,1:T(8,128)S(1)}, f32[64,3,512]{2,0,1:T(8,128)}, u32[]{:S(2)}) copy-start(f32[64,3,512]{2,0,1:T(8,128)} %param.4) | copy-start | bytes 1179652
  7.4 2.8 %copy-start.1 = (f32[64,3,512]{2,0,1:T(8,128)S(1)}, f32[64,3,512]{2,0,1:T(8,128)}, u32[]{:S(2)}) copy-start(f32[64,3,512]{2,0,1:T(8,128)} %param.5) | copy-start | bytes 1179652
  8.4 12.4 %collective-permute-start.4 = (f32[2,104,128]{2,1,0:T(8,128)S(1)}, f32[2,104,128]{2,1,0:T(8,128)S(1)}, u32[]{:S(2)}, u32[]{:S(2)}) collective-permute-start(f32[2,104,128]{2,1,0:T(8,128)S(1)} %pad_maximum_fusion.1), channel_id=1, source_target_pairs={{0,4},{4,0},{8,12},{12,8},{16,20},{20,16},{24,28},{28,24},{1,5},{5... | collective-permute-start | bytes 319496 | tf_op jit(solution)/shard_map/ppermute | solution.py:319
  15.5 10.4 %collective-permute-start.6 = (f32[2,104,128]{2,1,0:T(8,128)S(1)}, f32[2,104,128]{2,1,0:T(8,128)S(1)}, u32[]{:S(2)}, u32[]{:S(2)}) collective-permute-start(f32[2,104,128]{2,1,0:T(8,128)S(1)} %pad_maximum_fusion.2), channel_id=1, source_target_pairs={{0,4},{4,0},{8,12},{12,8},{16,20},{20,16},{24,28},{28,24},{1,5},{5... | collective-permute-start | bytes 319496 | tf_op jit(solution)/shard_map/ppermute | solution.py:319
  17.2 12.8 %collective-permute-start.3 = (f32[4,104,128]{2,1,0:T(8,128)S(1)}, f32[4,104,128]{2,1,0:T(8,128)S(1)}, u32[]{:S(2)}, u32[]{:S(2)}) collective-permute-start(f32[4,104,128]{2,1,0:T(8,128)S(1)} %pad_maximum_fusion), channel_id=1, source_target_pairs={{0,28},{4,8},{8,4},{12,16},{16,12},{20,24},{24,20},{28,0},{1,29},{... | collective-permute-start | bytes 638984 | tf_op jit(solution)/shard_map/ppermute | solution.py:319
  20.8 0.6 %copy-start.2 = (s32[48]{0:T(128)S(1)}, s32[48]{0:T(128)}, u32[]{:S(2)}) copy-start(s32[48]{0:T(128)} %get-tuple-element.21.refs_0_.table) | copy-start | bytes 580
  25.8 4.2 %collective-permute-start.7 = (f32[2,48,128]{2,1,0:T(8,128)S(1)}, f32[2,48,128]{2,1,0:T(8,128)S(1)}, u32[]{:S(2)}, u32[]{:S(2)}) collective-permute-start(f32[2,48,128]{2,1,0:T(8,128)S(1)} %bitcast.56), channel_id=1, source_target_pairs={{0,4},{4,0},{8,12},{12,8},{16,20},{20,16},{24,28},{28,24},{1,5},{5... | collective-permute-start | bytes 147464 | tf_op jit(solution)/shard_map/ppermute | solution.py:319
  35.9 7.5 %collective-permute-start.5 = (f32[192,128]{1,0:T(8,128)S(1)}, f32[192,128]{1,0:T(8,128)S(1)}, u32[]{:S(2)}, u32[]{:S(2)}) collective-permute-start(f32[192,128]{1,0:T(8,128)S(1)} %get-tuple-element.29), channel_id=1, source_target_pairs={{0,28},{4,8},{8,4},{12,16},{16,12},{20,24},{24,20},{28,0},{1,29},{... | collective-permute-start | bytes 294920 | tf_op jit(solution)/shard_map/ppermute | solution.py:319
  46.3 4.2 %collective-permute-start.9 = (f32[2,48,128]{2,1,0:T(8,128)S(1)}, f32[2,48,128]{2,1,0:T(8,128)S(1)}, u32[]{:S(2)}, u32[]{:S(2)}) collective-permute-start(f32[2,48,128]{2,1,0:T(8,128)S(1)} %pad_maximum_fusion.7), channel_id=1, source_target_pairs={{0,4},{4,0},{8,12},{12,8},{16,20},{20,16},{24,28},{28,24},{1,5},{5... | collective-permute-start | bytes 147464 | tf_op jit(solution)/shard_map/ppermute | solution.py:319
  46.4 4.2 %collective-permute-start.8 = (f32[3,48,128]{2,1,0:T(8,128)S(1)}, f32[3,48,128]{2,1,0:T(8,128)S(1)}, u32[]{:S(2)}, u32[]{:S(2)}) collective-permute-start(f32[3,48,128]{2,1,0:T(8,128)S(1)} %pad_maximum_fusion.4), channel_id=1, source_target_pairs={{0,1},{1,0},{2,3},{3,2},{4,5},{5,4},{6,7},{7,6},{8,9},{9,8},{10,11... | collective-permute-start | bytes 221192 | tf_op jit(solution)/shard_map/ppermute | solution.py:315
  50.4 4.7 %collective-permute-start.10 = (f32[3,48,128]{2,1,0:T(8,128)S(1)}, f32[3,48,128]{2,1,0:T(8,128)S(1)}, u32[]{:S(2)}, u32[]{:S(2)}) collective-permute-start(f32[3,48,128]{2,1,0:T(8,128)S(1)} %pad_maximum_fusion.5), channel_id=1, source_target_pairs={{0,2},{1,3},{2,0},{3,1},{4,6},{5,7},{6,4},{7,5},{8,10},{9,11},{10,... | collective-permute-start | bytes 221192 | tf_op jit(solution)/shard_map/ppermute | solution.py:315
  50.5 4.6 %collective-permute-start.11 = (f32[3,48,128]{2,1,0:T(8,128)S(1)}, f32[3,48,128]{2,1,0:T(8,128)S(1)}, u32[]{:S(2)}, u32[]{:S(2)}) collective-permute-start(f32[3,48,128]{2,1,0:T(8,128)S(1)} %pad_maximum_fusion.6), channel_id=1, source_target_pairs={{0,3},{1,2},{2,1},{3,0},{4,7},{5,6},{6,5},{7,4},{8,11},{9,10},{10,... | collective-permute-start | bytes 221192 | tf_op jit(solution)/shard_map/ppermute | solution.py:315

commit v2 on v0

--- a/solution.py
+++ b/solution.py
@@ -118,8 +118,8 @@
 
 def pack_kernel(sizes, cells, count, pos_hbm, frc_hbm, *refs):
     n_space, n_pairs, share, cell_dev, tiles = sizes
-    outs, table = refs[:n_pairs], refs[n_pairs]
-    slots, used, pos, frc, sems = refs[n_pairs + 1 :]
+    outs, (first, second, table) = refs[:n_pairs], refs[n_pairs : n_pairs + 3]
+    slots, used, pos, frc, sems = refs[n_pairs + 3 :]
     fetches = [
         pltpu.make_async_copy(pos_hbm, pos, sems.at[0]),
         pltpu.make_async_copy(frc_hbm, frc, sems.at[1]),
@@ -147,7 +147,7 @@
     plane = cell_dev * tiles
     for m in range(3 * n_pairs):
         kind, turn = m // n_pairs, m % n_pairs
-        out = outs[turn]
+        out = (outs[turn].at[0], first.at[turn], second.at[turn])[kind]
         label = jnp.full((1, LANES), -1.0, f32)
         for k in range(share):
             s = slots[m * share + k]
@@ -160,16 +160,17 @@
             for c in range(6):
                 source = pos if c < 3 else frc
                 row = (k * 6 + c) * tiles
-                out[kind, row : row + tiles, :] = source[
+                out[row : row + tiles, :] = source[
                     pl.ds(base + c % 3 * plane, tiles, stride=8), :
                 ]
         last = share * 6 * tiles
-        out[kind, last : last + 1, :] = label
-
-
-def pair_kernel(sizes, kinds, started, *refs):
+        out[last : last + 1, :] = label
+
+
+def pair_kernel(sizes, kinds, started, extra, *refs):
     n_space, n_pairs, share, cell_dev, tiles = sizes
     n = len(kinds)
+    refs = refs[extra:]
     messages, (pos, frc) = refs[:n], refs[n : n + 2]
     outs = refs[n + 2 + started :]
     (acc, reply), (inbox, todo, middles) = outs[:2], outs[-3:]
@@ -177,17 +178,17 @@
     plane = cell_dev * tiles
     if not started:
         acc[...] = jnp.zeros_like(acc)
-        outs[2][...] = jnp.zeros_like(outs[2])
+    outs[2][...] = jnp.zeros_like(outs[2])
     here = lax.axis_index("space")
     number = jnp.int32(0)
     first = 0
-    for kind, message in zip(kinds, messages):
-        away = jnp.int32(away_of(kind, lax.rem(here, 2)))
-        there = lax.rem(here + away + n_space, n_space)
-        half = 0.5 * slab_width * away.astype(f32)
-        middle_a = slab_width * (there.astype(f32) + 0.5) - half
-        middle_b = slab_width * (here.astype(f32) + 0.5) + half
-        for block in range(message.shape[0]):
+    for several_kinds, message in zip(kinds, messages):
+        for block, kind in enumerate(several_kinds):
+            away = jnp.int32(away_of(kind, lax.rem(here, 2)))
+            there = lax.rem(here + away + n_space, n_space)
+            half = 0.5 * slab_width * away.astype(f32)
+            middle_a = slab_width * (there.astype(f32) + 0.5) - half
+            middle_b = slab_width * (here.astype(f32) + 0.5) + half
             inbox[first * rows_in : (first + 1) * rows_in, :] = message[block, 0:rows_in, :]
             label = message[block, rows_in : rows_in + 1, :].astype(jnp.int32)
             for k in range(share):
@@ -296,7 +297,8 @@
     vmem = pl.BlockSpec(memory_space=pltpu.VMEM)
     smem = pl.BlockSpec(memory_space=pltpu.SMEM)
     hbm = pl.BlockSpec(memory_space=pltpu.HBM)
-    message = jax.ShapeDtypeStruct((3, rows_in + 8, LANES), f32)
+    message = jax.ShapeDtypeStruct((1, rows_in + 8, LANES), f32)
+    messages = jax.ShapeDtypeStruct((n_pairs, rows_in + 8, LANES), f32)
     total = jax.ShapeDtypeStruct((3 * cell_dev * tiles, LANES), f32)
 
     def across(value, turn):
@@ -308,9 +310,11 @@
 
     packed = pl.pallas_call(
         functools.partial(pack_kernel, sizes),
-        out_shape=[message] * n_pairs + [jax.ShapeDtypeStruct((n_slots,), jnp.int32)],
+        out_shape=[message] * n_pairs
+        + [messages] * 2
+        + [jax.ShapeDtypeStruct((n_slots,), jnp.int32)],
         in_specs=[smem, smem, hbm, hbm],
-        out_specs=[vmem] * n_pairs + [smem],
+        out_specs=[vmem] * (n_pairs + 2) + [smem],
         scratch_shapes=[
             pltpu.SMEM((n_slots,), jnp.int32),
             pltpu.SMEM((3 * n_pairs,), jnp.int32),
@@ -321,50 +325,49 @@
         compiler_params=pltpu.CompilerParams(vmem_limit_bytes=60 * 1024 * 1024),
         name="pack",
     )(pair_cells, pair_count, pos, frc)
-    sent, table = packed[:n_pairs], packed[n_pairs]
-    got = [sent[0]] + [across(sent[turn], turn) for turn in range(1, n_pairs)]
-
-    def pairs(arrived, before):
-        kinds = [kind for kind, _ in arrived]
+    sent, (first, second, table) = packed[:n_pairs], packed[n_pairs:]
+    first, second = beyond(first, 1), beyond(second, 2)
+    own = [sent[0]] + [across(sent[turn], turn) for turn in range(1, n_pairs)]
+
+    def pairs(arrived, before, extra=()):
+        kinds = [kinds for kinds, _ in arrived]
         values = [value for _, value in arrived]
         n = len(values)
         blocks = sum(value.shape[0] for value in values)
         return pl.pallas_call(
-            functools.partial(pair_kernel, sizes, kinds, len(before)),
+            functools.partial(pair_kernel, sizes, kinds, len(before), len(extra)),
             out_shape=[total, jax.ShapeDtypeStruct((blocks * rows_out, LANES), f32)]
-            + [jax.ShapeDtypeStruct((1, LANES), f32)] * (not before),
-            in_specs=[vmem] * (n + 2 + len(before)),
-            out_specs=[vmem] * (2 + (not before)),
+            + [jax.ShapeDtypeStruct((1, LANES), f32)],
+            in_specs=[smem] * len(extra) + [vmem] * (n + 2 + len(before)),
+            out_specs=[vmem] * 3,
             scratch_shapes=[
                 pltpu.VMEM((blocks * rows_in, LANES), f32),
                 pltpu.SMEM((2, blocks * share + 1), jnp.int32),
                 pltpu.SMEM((2, blocks * share + 1), f32),
             ],
-            input_output_aliases={n + 2: 0} if before else {},
+            input_output_aliases={len(extra) + n + 2: 0} if before else {},
             compiler_params=pltpu.CompilerParams(vmem_limit_bytes=48 * 1024 * 1024),
             cost_estimate=pl.CostEstimate(
                 flops=blocks * 1_000_000_000, bytes_accessed=2_000_000, transcendentals=2_000_000
             ),
             name="pairs",
-        )(*values, pos, frc, *before)
+        )(*extra, *values, pos, frc, *before)
 
     near, far = range(2), range(2, n_pairs)
-    own = [sent[0][kind : kind + 1] for kind in range(3)]
-    core = [got[1][kind : kind + 1] for kind in range(3)]
-    out_1n = beyond(jnp.concatenate([own[1], core[1]]), 1)
-    acc, reply_0n, nothing = pairs([(0, own[0]), (0, core[0])], [])
-    rest = [got[turn] + nothing[None] for turn in far]
-    out_1f = beyond(jnp.stack([value[1] for value in rest]), 1)
-    out_2 = beyond(jnp.concatenate([own[2], core[2]] + [value[2:] for value in rest]), 2)
-    acc, reply_m = pairs([(1, out_1n)] + [(0, got[turn][0:1]) for turn in far], [acc])
-    acc, reply_f = pairs([(1, out_1f), (2, out_2)], [acc])
-    reply_0n, reply_m, reply_f = (
-        value.reshape(-1, rows_out, LANES) for value in (reply_0n, reply_m, reply_f)
-    )
-    cut = n_pairs - 2
-    back_0 = jnp.concatenate([reply_0n, reply_m[2:]])
-    back_1 = beyond(jnp.concatenate([reply_m[:2], reply_f[:cut]]), 1)
-    back_2 = beyond(reply_f[cut:], 2)
+    acc, reply_0n, nothing = pairs([((0,), own[turn]) for turn in near], [])
+    acc, reply_0f, nothing = pairs([((0,), own[turn]) for turn in far], [acc], [table])
+    first, second = first + nothing[None], second + nothing[None]
+    got = [
+        across(jnp.stack([first[turn], second[turn]]), turn) for turn in range(1, n_pairs)
+    ]
+    acc, reply_n, _ = pairs([((1,), first[:1]), ((2,), second[:1])], [acc])
+    acc, reply_f, _ = pairs([((1, 2), value) for value in got], [acc])
+    reply_0n, reply_0f, reply_n, reply_f = (
+        value.reshape(-1, rows_out, LANES) for value in (reply_0n, reply_0f, reply_n, reply_f)
+    )
+    back_0 = jnp.concatenate([reply_0n, reply_0f])
+    back_1 = beyond(jnp.concatenate([reply_n[0:1], reply_f[0::2]]), 1)
+    back_2 = beyond(jnp.concatenate([reply_n[1:2], reply_f[1::2]]), 2)
     back = []
     for turn in range(n_pairs):
         value = jnp.stack([back_0[turn], back_1[turn], back_2[turn]])

time: 53.1 us -> 55.3 us (1.041)
  starting transfers between devices: 12.6 us -> 15.1 us
  waiting for transfers between devices: 13.4 us -> 12.1 us
  Pallas kernels: 24.2 us -> 25.3 us
    ppermute x5 -> x4, waiting for transfers between devices: 9.03 us -> 5.8 us  [beyond(): return lax.ppermute(value, 'space', moves)]
    ppermute x6 -> x9, starting transfers between devices: 5.13 us -> 7.12 us  [across(): return lax.ppermute(value, 'pairs', [(j, j ^ turn) for j in range(n_pairs)])]
    ppermute x6 -> x9, waiting for transfers between devices: 4.4 us -> 6.26 us  [across(): return lax.ppermute(value, 'pairs', [(j, j ^ turn) for j in range(n_pairs)])]
    pallas_call x3 -> x4, Pallas kernels: 19.4 us -> 20.4 us  [pairs(): pl.pallas_call(functools.partial(pair_kernel, sizes, kinds, len(before),...]
    slice x8 -> x3, local copies, waits for them, and re-layouts: 1.01 us -> 0.05 us  [the longest x1 0.03 us: body(): acc, reply_n, _ = pairs([((1,), first[:1]), ((2,), second[:1])], [acc])]
    unnamed x6 -> x8, local copies, waits for them, and re-layouts: 0.64 us -> 1.44 us
    ppermute x5 -> x4, starting transfers between devices: 7.47 us -> 7.96 us  [beyond(): return lax.ppermute(value, 'space', moves)]
  transfers between devices with their start and end apart: 11 -> 13, of which waited for: 6 -> 6; matrix products, arithmetic and copies ran while one was open for 2% -> 0% of each run, Pallas kernels for 16% -> 19%
where the time goes in v2:
time: 55.3 us; the launch traced here: 54.9 us
  Pallas kernels  25.3 us (46%)
  starting transfers between devices  15.1 us (27%)
  waiting for transfers between devices  12.1 us (22%)
  local copies, waits for them, and re-layouts  1.51 us (3%)
  between operations  0.84 us (2%)
    pallas_call x4, Pallas kernels, pairs(): pl.pallas_call(functools.partial(pair_kernel, sizes, kinds, len(before),...  20.4 us
    ppermute x4, starting transfers between devices, beyond(): return lax.ppermute(value, 'space', moves)  7.96 us
    ppermute x9, starting transfers between devices, across(): return lax.ppermute(value, 'pairs', [(j, j ^ turn) for j in range(n_pairs)])  7.12 us
    ppermute x9, waiting for transfers between devices, across(): return lax.ppermute(value, 'pairs', [(j, j ^ turn) for j in range(n_pairs)])  6.26 us
    ppermute x4, waiting for transfers between devices, beyond(): return lax.ppermute(value, 'space', moves)  5.8 us
    pallas_call x1, Pallas kernels, body(): pl.pallas_call(functools.partial(pack_kernel, sizes), out_shape=[message]...  3.38 us
    pallas_call x1, Pallas kernels, body(): pl.pallas_call(functools.partial(add_kernel, sizes), out_shape=total, in_...  1.59 us
    unnamed x8, local copies, waits for them, and re-layouts  1.44 us
  transfers between devices with their start and end apart: 13, of which 6 were waited for; matrix products, arithmetic and copies ran while one was open for 0% of the time, Pallas kernels for 19%

profile of v2, /device:TPU:0, one launch (start us, length us, event | category | flops | bytes accessed | tf_op | source)
XLA Modules:
  0.0 54.9 jit_solution(2456584685685873016)
XLA Ops:
  0.7 3.4 %pack.1 = (f32[1,104,128]{2,1,0:T(8,128)}, f32[1,104,128]{2,1,0:T(8,128)}, f32[1,104,128]{2,1,0:T(8,128)}, f32[1,104,128]{2,1,0:T(8,128)}, f32[4,104,128]{2,1,0:...) custom-call(s32[2,48]{1,0:T(2,128)} %cells.1, s32[1]{0:T(128)S(6)} %copy.11.count, f32[768,128]{1,0:T(8,128)} %bitcast.35, ...), custom_call_target="tpu_custom_call" | custom-call | tf_op jit(solution)/shard_map/pack/pallas_call | solution.py:311
  4.1 0.5 collective-permute-start.3
  4.6 2.6 %collective-permute-start.1 = (f32[1,104,128]{2,1,0:T(8,128)}, f32[1,104,128]{2,1,0:T(8,128)S(1)}, u32[]{:S(2)}, u32[]{:S(2)}) collective-permute-start(f32[1,104,128]{2,1,0:T(8,128)} %get-tuple-element.23), channel_id=1, source_target_pairs={{0,2},{1,3},{2,0},{3,1},{4,6},{5,7},{6,4},{7,5},{8,10},{9,11},{10,... | collective-permute-start | bytes 159752 | tf_op jit(solution)/shard_map/ppermute | solution.py:305
  7.1 0.1 collective-permute-start.2
  7.2 1.8 %collective-permute-start = (f32[4,104,128]{2,1,0:T(8,128)}, f32[4,104,128]{2,1,0:T(8,128)S(1)}, u32[]{:S(2)}, u32[]{:S(2)}) collective-permute-start(f32[4,104,128]{2,1,0:T(8,128)} %get-tuple-element.22), channel_id=1, source_target_pairs={{0,4},{4,0},{8,12},{12,8},{16,20},{20,16},{24,28},{28,24},{1,5},{5... | collective-permute-start | bytes 638984 | tf_op jit(solution)/shard_map/ppermute | solution.py:309
  9.0 3.5 %collective-permute-start.4 = (f32[4,104,128]{2,1,0:T(8,128)}, f32[4,104,128]{2,1,0:T(8,128)S(1)}, u32[]{:S(2)}, u32[]{:S(2)}) collective-permute-start(f32[4,104,128]{2,1,0:T(8,128)} %get-tuple-element.29), channel_id=1, source_target_pairs={{0,28},{4,8},{8,4},{12,16},{16,12},{20,24},{24,20},{28,0},{1,29},{... | collective-permute-start | bytes 638984 | tf_op jit(solution)/shard_map/ppermute | solution.py:309
  12.5 0.0 collective-permute-done.3.refs_1_
  12.5 0.8 %copy-done.3 = f32[1,104,128]{2,1,0:T(8,128)S(1)} copy-done((f32[1,104,128]{2,1,0:T(8,128)S(1)}, f32[1,104,128]{2,1,0:T(8,128)}, u32[]{:S(2)}) %copy-start.3) | copy-done | bytes 53272
  13.3 5.0 %pairs.4 = (f32[768,128]{1,0:T(8,128)S(1)}, f32[96,128]{1,0:T(8,128)S(1)}, f32[1,128]{1,0:T(1,128)}) custom-call(f32[1,104,128]{2,1,0:T(8,128)S(1)} %copy-done.3, f32[1,104,128]{2,1,0:T(8,128)S(1)} %collective-permute-done.3.refs_1_, f32[768,128]{1,0:T(8,128)S(1)} %bitcast.36, f32[768,128]{1,0:T(8,128)S(1)} %bitcast.41), custom_call_target="tpu_custom_call" | custom-call | flops 2000000000 | bytes 2000000 | tf_op jit(solution)/shard_map/pairs/pallas_call | solution.py:337
  18.3 0.0 collective-permute-done.1.refs_1_
  18.3 0.0 collective-permute-done.2.refs_2_
  18.3 0.6 %copy-done.2 = s32[48]{0:T(128)S(1)} copy-done((s32[48]{0:T(128)S(1)}, s32[48]{0:T(128)}, u32[]{:S(2)}) %copy-start.2) | copy-done | bytes 216
  18.9 2.2 %pairs.5 = (f32[768,128]{1,0:T(8,128)S(1)}, f32[96,128]{1,0:T(8,128)S(1)}, f32[1,128]{1,0:T(1,128)S(1)}) custom-call(s32[48]{0:T(128)S(1)} %copy-done.2, f32[1,104,128]{2,1,0:T(8,128)S(1)} %collective-permute-done.1.refs_1_, f32[1,104,128]{2,1,0:T(8,128)S(1)} %collective-permute-done.2.refs_2_, ...), custom_call_target="tpu_custom_call", output_to_operand_aliasing={{0}: (5, {})} | custom-call | flops 2000000000 | bytes 2000000 | tf_op jit(solution)/shard_map/pairs/pallas_call | solution.py:337
  21.1 0.0 collective-permute-done
  21.2 0.1 collective-permute-start.5
  21.3 1.5 %collective-permute-start.6 = (f32[2,104,128]{2,1,0:T(8,128)S(1)}, f32[2,104,128]{2,1,0:T(8,128)S(1)}, u32[]{:S(2)}, u32[]{:S(2)}) collective-permute-start(f32[2,104,128]{2,1,0:T(8,128)S(1)} %pad_maximum_fusion.1), channel_id=1, source_target_pairs={{0,2},{1,3},{2,0},{3,1},{4,6},{5,7},{6,4},{7,5},{8,10},{9,11},{10,... | collective-permute-start | bytes 319496 | tf_op jit(solution)/shard_map/ppermute | solution.py:305
  22.9 0.4 collective-permute-start.7
  23.3 3.3 %pairs.6 = (f32[768,128]{1,0:T(8,128)S(1)}, f32[96,128]{1,0:T(8,128)S(1)}, f32[1,128]{1,0:T(1,128)}) custom-call(f32[1,104,128]{2,1,0:T(8,128)S(1)} %get-tuple-element.66.refs_0_, f32[1,104,128]{2,1,0:T(8,128)S(1)} %get-tuple-element.37.refs_1_, f32[768,128]{1,0:T(8,128)S(1)} %bitcast.38, f32[768,128]{1,0:T(8,128)S(1)} %bitcast.43, ...), custom_call_target="tpu_custom_call", output_to_operand_aliasing={{0}: (4, {})} | custom-call | flops 2000000000 | bytes 2000000 | tf_op jit(solution)/shard_map/pairs/pallas_call | solution.py:337
  26.6 0.0 collective-permute-done.5.refs_0_
  26.6 0.6 %collective-permute-done.6.refs_1_ = f32[2,104,128]{2,1,0:T(8,128)S(1)} collective-permute-done((f32[2,104,128]{2,1,0:T(8,128)S(1)}, f32[2,104,128]{2,1,0:T(8,128)S(1)}, u32[]{:S(2)}, u32[]{:S(2)}) %collective-permute-start.6) | collective-permute-done | bytes 106528 | tf_op jit(solution)/shard_map/ppermute | solution.py:305
  27.2 1.5 %collective-permute-done.7.refs_2_ = f32[2,104,128]{2,1,0:T(8,128)S(1)} collective-permute-done((f32[2,104,128]{2,1,0:T(8,128)S(1)}, f32[2,104,128]{2,1,0:T(8,128)S(1)}, u32[]{:S(2)}, u32[]{:S(2)}) %collective-permute-start.7) | collective-permute-done | bytes 106528 | tf_op jit(solution)/shard_map/ppermute | solution.py:305
  28.6 10.0 %pairs.7 = (f32[768,128]{1,0:T(8,128)S(1)}, f32[288,128]{1,0:T(8,128)S(1)}, f32[1,128]{1,0:T(1,128)}) custom-call(f32[2,104,128]{2,1,0:T(8,128)S(1)} %collective-permute-done.5.refs_0_, f32[2,104,128]{2,1,0:T(8,128)S(1)} %collective-permute-done.6.refs_1_, f32[2,104,128]{2,1,0:T(8,128)S(1)} %collective-permute-done.7.refs_2_, ...), custom_call_target="tpu_custom_call", output_to_operand_aliasing={{0}: (5, {})} | custom-call | flops 6000000000 | bytes 2000000 | tf_op jit(solution)/shard_map/pairs/pallas_call | solution.py:337
  38.7 2.6 %collective-permute-start.9 = (f32[4,48,128]{2,1,0:T(8,128)S(1)}, f32[4,48,128]{2,1,0:T(8,128)S(1)}, u32[]{:S(2)}, u32[]{:S(2)}) collective-permute-start(f32[4,48,128]{2,1,0:T(8,128)S(1)} %pad_maximum_fusion.4), channel_id=1, source_target_pairs={{0,28},{4,8},{8,4},{12,16},{16,12},{20,24},{24,20},{28,0},{1,29},{... | collective-permute-start | bytes 294920 | tf_op jit(solution)/shard_map/ppermute | solution.py:309
  41.3 0.1 collective-permute-start.8
  41.3 4.8 %collective-permute-done.9 = f32[4,48,128]{2,1,0:T(8,128)S(1)} collective-permute-done((f32[4,48,128]{2,1,0:T(8,128)S(1)}, f32[4,48,128]{2,1,0:T(8,128)S(1)}, u32[]{:S(2)}, u32[]{:S(2)}) %collective-permute-start.9) | collective-permute-done | bytes 98336 | tf_op jit(solution)/shard_map/ppermute | solution.py:309
  46.2 1.0 %collective-permute-done.8 = f32[4,48,128]{2,1,0:T(8,128)S(1)} collective-permute-done((f32[4,48,128]{2,1,0:T(8,128)S(1)}, f32[4,48,128]{2,1,0:T(8,128)S(1)}, u32[]{:S(2)}, u32[]{:S(2)}) %collective-permute-start.8) | collective-permute-done | bytes 98336 | tf_op jit(solution)/shard_map/ppermute | solution.py:309
  47.2 0.1 collective-permute-start.10
  47.3 1.5 %collective-permute-start.11 = (f32[3,48,128]{2,1,0:T(8,128)S(1)}, f32[3,48,128]{2,1,0:T(8,128)S(1)}, u32[]{:S(2)}, u32[]{:S(2)}) collective-permute-start(f32[3,48,128]{2,1,0:T(8,128)S(1)} %pad_maximum_fusion.7), channel_id=1, source_target_pairs={{0,2},{1,3},{2,0},{3,1},{4,6},{5,7},{6,4},{7,5},{8,10},{9,11},{10,... | collective-permute-start | bytes 221192 | tf_op jit(solution)/shard_map/ppermute | solution.py:305
  48.8 0.3 collective-permute-start.12
  49.1 3.0 %collective-permute-done.11.refs_2_ = f32[3,48,128]{2,1,0:T(8,128)S(1)} collective-permute-done((f32[3,48,128]{2,1,0:T(8,128)S(1)}, f32[3,48,128]{2,1,0:T(8,128)S(1)}, u32[]{:S(2)}, u32[]{:S(2)}) %collective-permute-start.11) | collective-permute-done | bytes 73760 | tf_op jit(solution)/shard_map/ppermute | solution.py:305
  52.1 1.2 %collective-permute-done.12.refs_3_ = f32[3,48,128]{2,1,0:T(8,128)S(1)} collective-permute-done((f32[3,48,128]{2,1,0:T(8,128)S(1)}, f32[3,48,128]{2,1,0:T(8,128)S(1)}, u32[]{:S(2)}, u32[]{:S(2)}) %collective-permute-start.12) | collective-permute-done | bytes 73760 | tf_op jit(solution)/shard_map/ppermute | solution.py:305
  53.3 1.6 %add.25 = f32[768,128]{1,0:T(8,128)} custom-call(s32[48]{0:T(128)S(1)} %copy-done.2, f32[768,128]{1,0:T(8,128)S(1)} %get-tuple-element.32.acc, f32[3,48,128]{2,1,0:T(8,128)S(1)} %pad_maximum_fusion.5.refs_0_, f32[3,48,128]{2,1,0:T(8,128)S(1)} %collective-permute-done.10.refs_1_, f32[3,48,128]{2,1,0:T(8,128)S(1)} %collective-permute-done.11.refs_2_, ...), custom_call_target="tpu_custom_call" | custom-call | tf_op jit(solution)/shard_map/add/pallas_call | solution.py:375
  (25 shorter events, 0.2 us)
Async XLA Ops:
  0.7 11.9 %copy-start = (f32[64,3,512]{2,0,1:T(8,128)S(1)}, f32[64,3,512]{2,0,1:T(8,128)}, u32[]{:S(2)}) copy-start(f32[64,3,512]{2,0,1:T(8,128)} %param.4) | copy-start | bytes 1179652
  0.7 11.9 %copy-start.1 = (f32[64,3,512]{2,0,1:T(8,128)S(1)}, f32[64,3,512]{2,0,1:T(8,128)}, u32[]{:S(2)}) copy-start(f32[64,3,512]{2,0,1:T(8,128)} %param.5) | copy-start | bytes 1179652
  4.1 8.5 %collective-permute-start.3 = (f32[1,104,128]{2,1,0:T(8,128)}, f32[1,104,128]{2,1,0:T(8,128)S(1)}, u32[]{:S(2)}, u32[]{:S(2)}) collective-permute-start(f32[1,104,128]{2,1,0:T(8,128)} %get-tuple-element.26), channel_id=1, source_target_pairs={{0,1},{1,0},{2,3},{3,2},{4,5},{5,4},{6,7},{7,6},{8,9},{9,8},{10,11... | collective-permute-start | bytes 159752 | tf_op jit(solution)/shard_map/ppermute | solution.py:305
  4.6 13.7 %collective-permute-start.1 = (f32[1,104,128]{2,1,0:T(8,128)}, f32[1,104,128]{2,1,0:T(8,128)S(1)}, u32[]{:S(2)}, u32[]{:S(2)}) collective-permute-start(f32[1,104,128]{2,1,0:T(8,128)} %get-tuple-element.23), channel_id=1, source_target_pairs={{0,2},{1,3},{2,0},{3,1},{4,6},{5,7},{6,4},{7,5},{8,10},{9,11},{10,... | collective-permute-start | bytes 159752 | tf_op jit(solution)/shard_map/ppermute | solution.py:305
  7.1 11.2 %collective-permute-start.2 = (f32[1,104,128]{2,1,0:T(8,128)}, f32[1,104,128]{2,1,0:T(8,128)S(1)}, u32[]{:S(2)}, u32[]{:S(2)}) collective-permute-start(f32[1,104,128]{2,1,0:T(8,128)} %get-tuple-element.24), channel_id=1, source_target_pairs={{0,3},{1,2},{2,1},{3,0},{4,7},{5,6},{6,5},{7,4},{8,11},{9,10},{10,... | collective-permute-start | bytes 159752 | tf_op jit(solution)/shard_map/ppermute | solution.py:305
  7.2 13.9 %collective-permute-start = (f32[4,104,128]{2,1,0:T(8,128)}, f32[4,104,128]{2,1,0:T(8,128)S(1)}, u32[]{:S(2)}, u32[]{:S(2)}) collective-permute-start(f32[4,104,128]{2,1,0:T(8,128)} %get-tuple-element.22), channel_id=1, source_target_pairs={{0,4},{4,0},{8,12},{12,8},{16,20},{20,16},{24,28},{28,24},{1,5},{5... | collective-permute-start | bytes 638984 | tf_op jit(solution)/shard_map/ppermute | solution.py:309
  9.0 12.2 %collective-permute-start.4 = (f32[4,104,128]{2,1,0:T(8,128)}, f32[4,104,128]{2,1,0:T(8,128)S(1)}, u32[]{:S(2)}, u32[]{:S(2)}) collective-permute-start(f32[4,104,128]{2,1,0:T(8,128)} %get-tuple-element.29), channel_id=1, source_target_pairs={{0,28},{4,8},{8,4},{12,16},{16,12},{20,24},{24,20},{28,0},{1,29},{... | collective-permute-start | bytes 638984 | tf_op jit(solution)/shard_map/ppermute | solution.py:309
  12.5 0.8 %copy-start.3 = (f32[1,104,128]{2,1,0:T(8,128)S(1)}, f32[1,104,128]{2,1,0:T(8,128)}, u32[]{:S(2)}) copy-start(f32[1,104,128]{2,1,0:T(8,128)} %get-tuple-element.25.refs_0_) | copy-start | bytes 159748
  18.3 0.6 %copy-start.2 = (s32[48]{0:T(128)S(1)}, s32[48]{0:T(128)}, u32[]{:S(2)}) copy-start(s32[48]{0:T(128)} %get-tuple-element.21.refs_0_.table) | copy-start | bytes 580
  21.2 5.3 %collective-permute-start.5 = (f32[2,104,128]{2,1,0:T(8,128)S(1)}, f32[2,104,128]{2,1,0:T(8,128)S(1)}, u32[]{:S(2)}, u32[]{:S(2)}) collective-permute-start(f32[2,104,128]{2,1,0:T(8,128)S(1)} %pad_maximum_fusion), channel_id=1, source_target_pairs={{0,1},{1,0},{2,3},{3,2},{4,5},{5,4},{6,7},{7,6},{8,9},{9,8},{10,11... | collective-permute-start | bytes 319496 | tf_op jit(solution)/shard_map/ppermute | solution.py:305
  21.3 5.8 %collective-permute-start.6 = (f32[2,104,128]{2,1,0:T(8,128)S(1)}, f32[2,104,128]{2,1,0:T(8,128)S(1)}, u32[]{:S(2)}, u32[]{:S(2)}) collective-permute-start(f32[2,104,128]{2,1,0:T(8,128)S(1)} %pad_maximum_fusion.1), channel_id=1, source_target_pairs={{0,2},{1,3},{2,0},{3,1},{4,6},{5,7},{6,4},{7,5},{8,10},{9,11},{10,... | collective-permute-start | bytes 319496 | tf_op jit(solution)/shard_map/ppermute | solution.py:305
  22.9 5.7 %collective-permute-start.7 = (f32[2,104,128]{2,1,0:T(8,128)S(1)}, f32[2,104,128]{2,1,0:T(8,128)S(1)}, u32[]{:S(2)}, u32[]{:S(2)}) collective-permute-start(f32[2,104,128]{2,1,0:T(8,128)S(1)} %pad_maximum_fusion.2), channel_id=1, source_target_pairs={{0,3},{1,2},{2,1},{3,0},{4,7},{5,6},{6,5},{7,4},{8,11},{9,10},{10,... | collective-permute-start | bytes 319496 | tf_op jit(solution)/shard_map/ppermute | solution.py:305
  38.7 7.5 %collective-permute-start.9 = (f32[4,48,128]{2,1,0:T(8,128)S(1)}, f32[4,48,128]{2,1,0:T(8,128)S(1)}, u32[]{:S(2)}, u32[]{:S(2)}) collective-permute-start(f32[4,48,128]{2,1,0:T(8,128)S(1)} %pad_maximum_fusion.4), channel_id=1, source_target_pairs={{0,28},{4,8},{8,4},{12,16},{16,12},{20,24},{24,20},{28,0},{1,29},{... | collective-permute-start | bytes 294920 | tf_op jit(solution)/shard_map/ppermute | solution.py:309
  41.3 5.9 %collective-permute-start.8 = (f32[4,48,128]{2,1,0:T(8,128)S(1)}, f32[4,48,128]{2,1,0:T(8,128)S(1)}, u32[]{:S(2)}, u32[]{:S(2)}) collective-permute-start(f32[4,48,128]{2,1,0:T(8,128)S(1)} %pad_maximum_fusion.3), channel_id=1, source_target_pairs={{0,4},{4,0},{8,12},{12,8},{16,20},{20,16},{24,28},{28,24},{1,5},{5... | collective-permute-start | bytes 294920 | tf_op jit(solution)/shard_map/ppermute | solution.py:309
  47.2 2.0 %collective-permute-start.10 = (f32[3,48,128]{2,1,0:T(8,128)S(1)}, f32[3,48,128]{2,1,0:T(8,128)S(1)}, u32[]{:S(2)}, u32[]{:S(2)}) collective-permute-start(f32[3,48,128]{2,1,0:T(8,128)S(1)} %pad_maximum_fusion.6), channel_id=1, source_target_pairs={{0,1},{1,0},{2,3},{3,2},{4,5},{5,4},{6,7},{7,6},{8,9},{9,8},{10,11... | collective-permute-start | bytes 221192 | tf_op jit(solution)/shard_map/ppermute | solution.py:305
  47.3 4.9 %collective-permute-start.11 = (f32[3,48,128]{2,1,0:T(8,128)S(1)}, f32[3,48,128]{2,1,0:T(8,128)S(1)}, u32[]{:S(2)}, u32[]{:S(2)}) collective-permute-start(f32[3,48,128]{2,1,0:T(8,128)S(1)} %pad_maximum_fusion.7), channel_id=1, source_target_pairs={{0,2},{1,3},{2,0},{3,1},{4,6},{5,7},{6,4},{7,5},{8,10},{9,11},{10,... | collective-permute-start | bytes 221192 | tf_op jit(solution)/shard_map/ppermute | solution.py:305
  48.8 4.5 %collective-permute-start.12 = (f32[3,48,128]{2,1,0:T(8,128)S(1)}, f32[3,48,128]{2,1,0:T(8,128)S(1)}, u32[]{:S(2)}, u32[]{:S(2)}) collective-permute-start(f32[3,48,128]{2,1,0:T(8,128)S(1)} %pad_maximum_fusion.8), channel_id=1, source_target_pairs={{0,3},{1,2},{2,1},{3,0},{4,7},{5,6},{6,5},{7,4},{8,11},{9,10},{10,... | collective-permute-start | bytes 221192 | tf_op jit(solution)/shard_map/ppermute | solution.py:305

commit v3 on v0

--- a/solution.py
+++ b/solution.py
@@ -14,6 +14,7 @@
 across_middle = 1.0
 LANES = 128
 FEATURES = 16
+ROWS = 32
 
 f32 = jnp.float32
 bf16 = jnp.bfloat16
@@ -77,15 +78,17 @@
     return sums[0:FEATURES] + sums[FEATURES : 2 * FEATURES] + sums[2 * FEATURES :]
 
 
-def weights(dist_sq):
-    inverse = lax.rsqrt(dist_sq)
-    cubed = inverse * inverse * inverse
-    high = cubed.astype(bf16)
-    low = (cubed - high.astype(f32)).astype(bf16)
-    return high, low
-
-
-def pair_velocities(cells):
+def weights(dist_sq, out):
+    for start in range(0, dist_sq.shape[0], ROWS):
+        rows = slice(start, start + ROWS)
+        inverse = lax.rsqrt(dist_sq[rows])
+        cubed = inverse * inverse * inverse
+        high = cubed.astype(bf16)
+        out[0, rows, :] = high
+        out[1, rows, :] = (cubed - high.astype(f32)).astype(bf16)
+
+
+def pair_velocities(cells, kept):
     grams = [dot(*gram_factors(xa, xb), 0, 0) for xa, _, xb, _ in cells]
     feats = [(features(xa, fa), features(xb, fb)) for xa, fa, xb, fb in cells]
     results = []
@@ -95,10 +98,10 @@
         sums_a, sums_b, xa, xb = waiting.pop(0)
         results.append((combine(fold(sums_a), xa), combine(fold(sums_b), xb)))
 
-    for gram, (feat_a, feat_b), (xa, _, xb, _) in zip(grams, feats, cells):
-        high, low = weights(gram)
-        rows = jnp.concatenate([high, low], axis=0)
-        columns = jnp.concatenate([high, low], axis=1)
+    for i, (gram, (feat_a, feat_b), (xa, _, xb, _)) in enumerate(zip(grams, feats, cells)):
+        weights(gram, kept.at[i])
+        rows = jnp.concatenate([kept[i, 0], kept[i, 1]], axis=0)
+        columns = jnp.concatenate([kept[i, 0], kept[i, 1]], axis=1)
         sums_b = dot(jnp.concatenate([feat_a, feat_a], axis=1), rows, 1, 0)
         sums_a = dot(jnp.concatenate([feat_b, feat_b], axis=1), columns, 1, 1)
         waiting.append((sums_a, sums_b, xa, xb))
@@ -167,12 +170,13 @@
         out[kind, last : last + 1, :] = label
 
 
-def pair_kernel(sizes, kinds, started, *refs):
+def pair_kernel(sizes, kinds, started, extra, *refs):
     n_space, n_pairs, share, cell_dev, tiles = sizes
     n = len(kinds)
+    refs = refs[extra:]
     messages, (pos, frc) = refs[:n], refs[n : n + 2]
     outs = refs[n + 2 + started :]
-    (acc, reply), (inbox, todo, middles) = outs[:2], outs[-3:]
+    (acc, reply), (inbox, kept, todo, middles) = outs[:2], outs[-4:]
     rows_in = share * 6 * tiles
     plane = cell_dev * tiles
     if not started:
@@ -228,7 +232,7 @@
             reply[pl.ds(base + t, 3, stride=tiles), :] = vel_a[:, parts[t]]
 
     def several(numbers):
-        results = pair_velocities([load(i) for i in numbers])
+        results = pair_velocities([load(i) for i in numbers], kept)
         for i, result in zip(numbers, results):
             store(i, *result)
 
@@ -324,29 +328,30 @@
     sent, table = packed[:n_pairs], packed[n_pairs]
     got = [sent[0]] + [across(sent[turn], turn) for turn in range(1, n_pairs)]
 
-    def pairs(arrived, before):
+    def pairs(arrived, before, extra=()):
         kinds = [kind for kind, _ in arrived]
         values = [value for _, value in arrived]
         n = len(values)
         blocks = sum(value.shape[0] for value in values)
         return pl.pallas_call(
-            functools.partial(pair_kernel, sizes, kinds, len(before)),
+            functools.partial(pair_kernel, sizes, kinds, len(before), len(extra)),
             out_shape=[total, jax.ShapeDtypeStruct((blocks * rows_out, LANES), f32)]
             + [jax.ShapeDtypeStruct((1, LANES), f32)] * (not before),
-            in_specs=[vmem] * (n + 2 + len(before)),
+            in_specs=[smem] * len(extra) + [vmem] * (n + 2 + len(before)),
             out_specs=[vmem] * (2 + (not before)),
             scratch_shapes=[
                 pltpu.VMEM((blocks * rows_in, LANES), f32),
+                pltpu.VMEM((4, 2, points, points), bf16),
                 pltpu.SMEM((2, blocks * share + 1), jnp.int32),
                 pltpu.SMEM((2, blocks * share + 1), f32),
             ],
-            input_output_aliases={n + 2: 0} if before else {},
+            input_output_aliases={len(extra) + n + 2: 0} if before else {},
             compiler_params=pltpu.CompilerParams(vmem_limit_bytes=48 * 1024 * 1024),
             cost_estimate=pl.CostEstimate(
                 flops=blocks * 1_000_000_000, bytes_accessed=2_000_000, transcendentals=2_000_000
             ),
             name="pairs",
-        )(*values, pos, frc, *before)
+        )(*extra, *values, pos, frc, *before)
 
     near, far = range(2), range(2, n_pairs)
     own = [sent[0][kind : kind + 1] for kind in range(3)]
@@ -356,7 +361,9 @@
     rest = [got[turn] + nothing[None] for turn in far]
     out_1f = beyond(jnp.stack([value[1] for value in rest]), 1)
     out_2 = beyond(jnp.concatenate([own[2], core[2]] + [value[2:] for value in rest]), 2)
-    acc, reply_m = pairs([(1, out_1n)] + [(0, got[turn][0:1]) for turn in far], [acc])
+    acc, reply_m = pairs(
+        [(1, out_1n)] + [(0, got[turn][0:1]) for turn in far], [acc], [table]
+    )
     acc, reply_f = pairs([(1, out_1f), (2, out_2)], [acc])
     reply_0n, reply_m, reply_f = (
         value.reshape(-1, rows_out, LANES) for value in (reply_0n, reply_m, reply_f)

time: 53.1 us -> 54.1 us (1.019)
  Pallas kernels: 24.2 us -> 27.4 us
  starting transfers between devices: 12.6 us -> 10 us
  waiting for transfers between devices: 13.4 us -> 14.3 us
    pallas_call x3, Pallas kernels: 19.4 us -> 22.6 us  [pairs(): pl.pallas_call(functools.partial(pair_kernel, sizes, kinds, len(before),...]
    ppermute x5, starting transfers between devices: 7.47 us -> 4.88 us  [beyond(): return lax.ppermute(value, 'space', moves)]
    ppermute x5, waiting for transfers between devices: 9.03 us -> 9.9 us  [beyond(): return lax.ppermute(value, 'space', moves)]
  transfers between devices with their start and end apart: 11 -> 11, of which waited for: 6 -> 6; matrix products, arithmetic and copies ran while one was open for 2% -> 2% of each run, Pallas kernels for 16% -> 18%
where the time goes in v3:
time: 54.1 us; the launch traced here: 54.3 us
  Pallas kernels  27.4 us (51%)
  waiting for transfers between devices  14.3 us (26%)
  starting transfers between devices  10 us (18%)
  local copies, waits for them, and re-layouts  1.66 us (3%)
  between operations  0.86 us (2%)
    pallas_call x3, Pallas kernels, pairs(): pl.pallas_call(functools.partial(pair_kernel, sizes, kinds, len(before),...  22.6 us
    ppermute x5, waiting for transfers between devices, beyond(): return lax.ppermute(value, 'space', moves)  9.9 us
    ppermute x6, starting transfers between devices, across(): return lax.ppermute(value, 'pairs', [(j, j ^ turn) for j in range(n_pairs)])  5.13 us
    ppermute x5, starting transfers between devices, beyond(): return lax.ppermute(value, 'space', moves)  4.88 us
    ppermute x6, waiting for transfers between devices, across(): return lax.ppermute(value, 'pairs', [(j, j ^ turn) for j in range(n_pairs)])  4.36 us
    pallas_call x1, Pallas kernels, body(): pl.pallas_call(functools.partial(pack_kernel, sizes), out_shape=[message]...  3.22 us
    pallas_call x1, Pallas kernels, body(): pl.pallas_call(functools.partial(add_kernel, sizes), out_shape=total, in_...  1.59 us
  transfers between devices with their start and end apart: 11, of which 6 were waited for; matrix products, arithmetic and copies ran while one was open for 2% of the time, Pallas kernels for 18%

profile of v3, /device:TPU:0, one launch (start us, length us, event | category | flops | bytes accessed | tf_op | source)
XLA Modules:
  0.0 54.3 jit_solution(4546961072687267773)
XLA Ops:
  0.7 3.2 %pack.1 = (f32[3,104,128]{2,1,0:T(8,128)}, f32[3,104,128]{2,1,0:T(8,128)}, f32[3,104,128]{2,1,0:T(8,128)}, f32[3,104,128]{2,1,0:T(8,128)}, s32[48]{0:T(128)}) custom-call(s32[2,48]{1,0:T(2,128)} %cells.1, s32[1]{0:T(128)S(6)} %copy.9.count, f32[768,128]{1,0:T(8,128)} %bitcast.33, f32[768,128]{1,0:T(8,128)} %bitcast.37), custom_call_target="tpu_custom_call" | custom-call | tf_op jit(solution)/shard_map/pack/pallas_call | solution.py:313
  3.9 3.0 %collective-permute-start = (f32[3,104,128]{2,1,0:T(8,128)}, f32[3,104,128]{2,1,0:T(8,128)S(1)}, u32[]{:S(2)}, u32[]{:S(2)}) collective-permute-start(f32[3,104,128]{2,1,0:T(8,128)} %get-tuple-element.18), channel_id=1, source_target_pairs={{0,2},{1,3},{2,0},{3,1},{4,6},{5,7},{6,4},{7,5},{8,10},{9,11},{10,... | collective-permute-start | bytes 479240 | tf_op jit(solution)/shard_map/ppermute | solution.py:307
  6.9 0.0 collective-permute-start.1
  6.9 0.2 collective-permute-start.2
  7.1 0.9 %fusion = (f32[1,104,128]{2,1,0:T(8,128)S(1)}, f32[1,104,128]{2,1,0:T(8,128)S(1)}, f32[1,104,128]{2,1,0:T(8,128)S(1)}) fusion(f32[3,104,128]{2,1,0:T(8,128)} %get-tuple-element.19), kind=kLoop, calls=%fused_computation.14 | loop fusion | bytes 319488 | tf_op jit(solution)/shard_map/slice | solution.py:357
  8.0 0.4 collective-permute-done.1
  8.5 1.6 %collective-permute-start.5 = (f32[2,104,128]{2,1,0:T(8,128)S(1)}, f32[2,104,128]{2,1,0:T(8,128)S(1)}, u32[]{:S(2)}, u32[]{:S(2)}) collective-permute-start(f32[2,104,128]{2,1,0:T(8,128)S(1)} %pad_maximum_fusion.2), channel_id=1, source_target_pairs={{0,4},{4,0},{8,12},{12,8},{16,20},{20,16},{24,28},{28,24},{1,5},{5... | collective-permute-start | bytes 319496 | tf_op jit(solution)/shard_map/ppermute | solution.py:311
  10.1 0.0 copy-done
  10.1 0.0 copy-done.1
  10.1 6.4 %pairs.3 = (f32[768,128]{1,0:T(8,128)S(1)}, f32[96,128]{1,0:T(8,128)S(1)}, f32[1,128]{1,0:T(1,128)S(1)}) custom-call(f32[1,104,128]{2,1,0:T(8,128)S(1)} %get-tuple-element.31.refs_0_, f32[1,104,128]{2,1,0:T(8,128)S(1)} %get-tuple-element.34.refs_1_, f32[768,128]{1,0:T(8,128)S(1)} %bitcast.34, f32[768,128]{1,0:T(8,128)S(1)} %bitcast.38), custom_call_target="tpu_custom_call" | custom-call | flops 2000000000 | bytes 2000000 | tf_op jit(solution)/shard_map/pairs/pallas_call | solution.py:336
  16.5 0.0 collective-permute-done
  16.5 0.0 collective-permute-done.2
  16.6 0.1 collective-permute-start.3
  16.7 3.1 %collective-permute-start.4 = (f32[4,104,128]{2,1,0:T(8,128)S(1)}, f32[4,104,128]{2,1,0:T(8,128)S(1)}, u32[]{:S(2)}, u32[]{:S(2)}) collective-permute-start(f32[4,104,128]{2,1,0:T(8,128)S(1)} %pad_maximum_fusion), channel_id=1, source_target_pairs={{0,28},{4,8},{8,4},{12,16},{16,12},{20,24},{24,20},{28,0},{1,29},{... | collective-permute-start | bytes 638984 | tf_op jit(solution)/shard_map/ppermute | solution.py:311
  19.8 0.0 collective-permute-done.5.refs_1_
  19.8 0.0 copy-start.2
  19.8 0.6 %copy-done.2 = s32[48]{0:T(128)S(1)} copy-done((s32[48]{0:T(128)S(1)}, s32[48]{0:T(128)}, u32[]{:S(2)}) %copy-start.2) | copy-done | bytes 216
  20.4 3.4 %pairs.4 = (f32[768,128]{1,0:T(8,128)S(1)}, f32[192,128]{1,0:T(8,128)S(1)}) custom-call(s32[48]{0:T(128)S(1)} %copy-done.2, f32[2,104,128]{2,1,0:T(8,128)S(1)} %collective-permute-done.5.refs_1_, f32[1,104,128]{2,1,0:T(8,128)S(1)} %slice.147.refs_2_, f32[1,104,128]{2,1,0:T(8,128)S(1)} %slice.148.refs_3_, ...), custom_call_target="tpu_custom_call", output_to_operand_aliasing={{0}: (6, {})} | custom-call | flops 4000000000 | bytes 2000000 | tf_op jit(solution)/shard_map/pairs/pallas_call | solution.py:336
  23.9 0.0 collective-permute-done.3.refs_0_
  23.9 2.1 %collective-permute-done.4.refs_1_ = f32[4,104,128]{2,1,0:T(8,128)S(1)} collective-permute-done((f32[4,104,128]{2,1,0:T(8,128)S(1)}, f32[4,104,128]{2,1,0:T(8,128)S(1)}, u32[]{:S(2)}, u32[]{:S(2)}) %collective-permute-start.4) | collective-permute-done | bytes 213024 | tf_op jit(solution)/shard_map/ppermute | solution.py:311
  26.0 12.8 %pairs.5 = (f32[768,128]{1,0:T(8,128)S(1)}, f32[288,128]{1,0:T(8,128)S(1)}) custom-call(f32[2,104,128]{2,1,0:T(8,128)S(1)} %collective-permute-done.3.refs_0_, f32[4,104,128]{2,1,0:T(8,128)S(1)} %collective-permute-done.4.refs_1_, f32[768,128]{1,0:T(8,128)S(1)} %bitcast.36, f32[768,128]{1,0:T(8,128)S(1)} %bitcast.40, ...), custom_call_target="tpu_custom_call", output_to_operand_aliasing={{0}: (4, {})} | custom-call | flops 6000000000 | bytes 2000000 | tf_op jit(solution)/shard_map/pairs/pallas_call | solution.py:336
  38.9 0.1 collective-permute-start.6
  39.0 0.1 collective-permute-start.7
  39.1 4.5 %collective-permute-done.6 = f32[4,48,128]{2,1,0:T(8,128)S(1)} collective-permute-done((f32[4,48,128]{2,1,0:T(8,128)S(1)}, f32[4,48,128]{2,1,0:T(8,128)S(1)}, u32[]{:S(2)}, u32[]{:S(2)}) %collective-permute-start.6) | collective-permute-done | bytes 98336 | tf_op jit(solution)/shard_map/ppermute | solution.py:311
  43.6 3.3 %collective-permute-done.7 = f32[4,48,128]{2,1,0:T(8,128)S(1)} collective-permute-done((f32[4,48,128]{2,1,0:T(8,128)S(1)}, f32[4,48,128]{2,1,0:T(8,128)S(1)}, u32[]{:S(2)}, u32[]{:S(2)}) %collective-permute-start.7) | collective-permute-done | bytes 98336 | tf_op jit(solution)/shard_map/ppermute | solution.py:311
  46.9 0.1 collective-permute-start.8
  47.0 0.3 collective-permute-start.9
  47.2 1.6 %collective-permute-start.10 = (f32[3,48,128]{2,1,0:T(8,128)S(1)}, f32[3,48,128]{2,1,0:T(8,128)S(1)}, u32[]{:S(2)}, u32[]{:S(2)}) collective-permute-start(f32[3,48,128]{2,1,0:T(8,128)S(1)} %pad_maximum_fusion.7), channel_id=1, source_target_pairs={{0,3},{1,2},{2,1},{3,0},{4,7},{5,6},{6,5},{7,4},{8,11},{9,10},{10,... | collective-permute-start | bytes 221192 | tf_op jit(solution)/shard_map/ppermute | solution.py:307
  48.8 0.0 collective-permute-done.8.refs_1_
  48.8 3.3 %collective-permute-done.9.refs_2_ = f32[3,48,128]{2,1,0:T(8,128)S(1)} collective-permute-done((f32[3,48,128]{2,1,0:T(8,128)S(1)}, f32[3,48,128]{2,1,0:T(8,128)S(1)}, u32[]{:S(2)}, u32[]{:S(2)}) %collective-permute-start.9) | collective-permute-done | bytes 73760 | tf_op jit(solution)/shard_map/ppermute | solution.py:307
  52.1 0.6 %collective-permute-done.10.refs_3_ = f32[3,48,128]{2,1,0:T(8,128)S(1)} collective-permute-done((f32[3,48,128]{2,1,0:T(8,128)S(1)}, f32[3,48,128]{2,1,0:T(8,128)S(1)}, u32[]{:S(2)}, u32[]{:S(2)}) %collective-permute-start.10) | collective-permute-done | bytes 73760 | tf_op jit(solution)/shard_map/ppermute | solution.py:307
  52.8 1.6 %add.25 = f32[768,128]{1,0:T(8,128)} custom-call(s32[48]{0:T(128)S(1)} %copy-done.2, f32[768,128]{1,0:T(8,128)S(1)} %get-tuple-element.25.acc, f32[3,48,128]{2,1,0:T(8,128)S(1)} %pad_maximum_fusion.4.refs_0_, f32[3,48,128]{2,1,0:T(8,128)S(1)} %collective-permute-done.8.refs_1_, f32[3,48,128]{2,1,0:T(8,128)S(1)} %collective-permute-done.9.refs_2_, ...), custom_call_target="tpu_custom_call" | custom-call | tf_op jit(solution)/shard_map/add/pallas_call | solution.py:379
  (22 shorter events, 0.2 us)
Async XLA Ops:
  3.9 12.6 %collective-permute-start = (f32[3,104,128]{2,1,0:T(8,128)}, f32[3,104,128]{2,1,0:T(8,128)S(1)}, u32[]{:S(2)}, u32[]{:S(2)}) collective-permute-start(f32[3,104,128]{2,1,0:T(8,128)} %get-tuple-element.18), channel_id=1, source_target_pairs={{0,2},{1,3},{2,0},{3,1},{4,6},{5,7},{6,4},{7,5},{8,10},{9,11},{10,... | collective-permute-start | bytes 479240 | tf_op jit(solution)/shard_map/ppermute | solution.py:307
  6.9 1.6 %collective-permute-start.1 = (f32[3,104,128]{2,1,0:T(8,128)}, f32[3,104,128]{2,1,0:T(8,128)S(1)}, u32[]{:S(2)}, u32[]{:S(2)}) collective-permute-start(f32[3,104,128]{2,1,0:T(8,128)} %get-tuple-element.20), channel_id=1, source_target_pairs={{0,1},{1,0},{2,3},{3,2},{4,5},{5,4},{6,7},{7,6},{8,9},{9,8},{10,11... | collective-permute-start | bytes 479240 | tf_op jit(solution)/shard_map/ppermute | solution.py:307
  6.9 9.6 %collective-permute-start.2 = (f32[3,104,128]{2,1,0:T(8,128)}, f32[3,104,128]{2,1,0:T(8,128)S(1)}, u32[]{:S(2)}, u32[]{:S(2)}) collective-permute-start(f32[3,104,128]{2,1,0:T(8,128)} %get-tuple-element.22), channel_id=1, source_target_pairs={{0,3},{1,2},{2,1},{3,0},{4,7},{5,6},{6,5},{7,4},{8,11},{9,10},{10,... | collective-permute-start | bytes 479240 | tf_op jit(solution)/shard_map/ppermute | solution.py:307
  7.1 3.0 %copy-start = (f32[64,3,512]{2,0,1:T(8,128)S(1)}, f32[64,3,512]{2,0,1:T(8,128)}, u32[]{:S(2)}) copy-start(f32[64,3,512]{2,0,1:T(8,128)} %param.4) | copy-start | bytes 1179652
  7.1 3.0 %copy-start.1 = (f32[64,3,512]{2,0,1:T(8,128)S(1)}, f32[64,3,512]{2,0,1:T(8,128)}, u32[]{:S(2)}) copy-start(f32[64,3,512]{2,0,1:T(8,128)} %param.5) | copy-start | bytes 1179652
  8.5 11.3 %collective-permute-start.5 = (f32[2,104,128]{2,1,0:T(8,128)S(1)}, f32[2,104,128]{2,1,0:T(8,128)S(1)}, u32[]{:S(2)}, u32[]{:S(2)}) collective-permute-start(f32[2,104,128]{2,1,0:T(8,128)S(1)} %pad_maximum_fusion.2), channel_id=1, source_target_pairs={{0,4},{4,0},{8,12},{12,8},{16,20},{20,16},{24,28},{28,24},{1,5},{5... | collective-permute-start | bytes 319496 | tf_op jit(solution)/shard_map/ppermute | solution.py:311
  16.6 7.2 %collective-permute-start.3 = (f32[2,104,128]{2,1,0:T(8,128)S(1)}, f32[2,104,128]{2,1,0:T(8,128)S(1)}, u32[]{:S(2)}, u32[]{:S(2)}) collective-permute-start(f32[2,104,128]{2,1,0:T(8,128)S(1)} %pad_maximum_fusion.1), channel_id=1, source_target_pairs={{0,4},{4,0},{8,12},{12,8},{16,20},{20,16},{24,28},{28,24},{1,5},{5... | collective-permute-start | bytes 319496 | tf_op jit(solution)/shard_map/ppermute | solution.py:311
  16.7 9.3 %collective-permute-start.4 = (f32[4,104,128]{2,1,0:T(8,128)S(1)}, f32[4,104,128]{2,1,0:T(8,128)S(1)}, u32[]{:S(2)}, u32[]{:S(2)}) collective-permute-start(f32[4,104,128]{2,1,0:T(8,128)S(1)} %pad_maximum_fusion), channel_id=1, source_target_pairs={{0,28},{4,8},{8,4},{12,16},{16,12},{20,24},{24,20},{28,0},{1,29},{... | collective-permute-start | bytes 638984 | tf_op jit(solution)/shard_map/ppermute | solution.py:311
  19.8 0.6 %copy-start.2 = (s32[48]{0:T(128)S(1)}, s32[48]{0:T(128)}, u32[]{:S(2)}) copy-start(s32[48]{0:T(128)} %get-tuple-element.17.refs_0_.table) | copy-start | bytes 580
  38.9 4.7 %collective-permute-start.6 = (f32[4,48,128]{2,1,0:T(8,128)S(1)}, f32[4,48,128]{2,1,0:T(8,128)S(1)}, u32[]{:S(2)}, u32[]{:S(2)}) collective-permute-start(f32[4,48,128]{2,1,0:T(8,128)S(1)} %pad_maximum_fusion.3), channel_id=1, source_target_pairs={{0,4},{4,0},{8,12},{12,8},{16,20},{20,16},{24,28},{28,24},{1,5},{5... | collective-permute-start | bytes 294920 | tf_op jit(solution)/shard_map/ppermute | solution.py:311
  39.0 7.8 %collective-permute-start.7 = (f32[4,48,128]{2,1,0:T(8,128)S(1)}, f32[4,48,128]{2,1,0:T(8,128)S(1)}, u32[]{:S(2)}, u32[]{:S(2)}) collective-permute-start(f32[4,48,128]{2,1,0:T(8,128)S(1)} %bitcast.44), channel_id=1, source_target_pairs={{0,28},{4,8},{8,4},{12,16},{16,12},{20,24},{24,20},{28,0},{1,29},{... | collective-permute-start | bytes 294920 | tf_op jit(solution)/shard_map/ppermute | solution.py:311
  46.9 2.0 %collective-permute-start.8 = (f32[3,48,128]{2,1,0:T(8,128)S(1)}, f32[3,48,128]{2,1,0:T(8,128)S(1)}, u32[]{:S(2)}, u32[]{:S(2)}) collective-permute-start(f32[3,48,128]{2,1,0:T(8,128)S(1)} %pad_maximum_fusion.5), channel_id=1, source_target_pairs={{0,1},{1,0},{2,3},{3,2},{4,5},{5,4},{6,7},{7,6},{8,9},{9,8},{10,11... | collective-permute-start | bytes 221192 | tf_op jit(solution)/shard_map/ppermute | solution.py:307
  47.0 5.1 %collective-permute-start.9 = (f32[3,48,128]{2,1,0:T(8,128)S(1)}, f32[3,48,128]{2,1,0:T(8,128)S(1)}, u32[]{:S(2)}, u32[]{:S(2)}) collective-permute-start(f32[3,48,128]{2,1,0:T(8,128)S(1)} %pad_maximum_fusion.6), channel_id=1, source_target_pairs={{0,2},{1,3},{2,0},{3,1},{4,6},{5,7},{6,4},{7,5},{8,10},{9,11},{10,... | collective-permute-start | bytes 221192 | tf_op jit(solution)/shard_map/ppermute | solution.py:307
  47.2 5.5 %collective-permute-start.10 = (f32[3,48,128]{2,1,0:T(8,128)S(1)}, f32[3,48,128]{2,1,0:T(8,128)S(1)}, u32[]{:S(2)}, u32[]{:S(2)}) collective-permute-start(f32[3,48,128]{2,1,0:T(8,128)S(1)} %pad_maximum_fusion.7), channel_id=1, source_target_pairs={{0,3},{1,2},{2,1},{3,0},{4,7},{5,6},{6,5},{7,4},{8,11},{9,10},{10,... | collective-permute-start | bytes 221192 | tf_op jit(solution)/shard_map/ppermute | solution.py:307

commit v4 on v0

--- a/solution.py
+++ b/solution.py
@@ -118,8 +118,8 @@
 
 def pack_kernel(sizes, cells, count, pos_hbm, frc_hbm, *refs):
     n_space, n_pairs, share, cell_dev, tiles = sizes
-    outs, table = refs[:n_pairs], refs[n_pairs]
-    slots, used, pos, frc, sems = refs[n_pairs + 1 :]
+    outs = refs[:n_pairs]
+    slots, used, pos, frc, sems = refs[n_pairs:]
     fetches = [
         pltpu.make_async_copy(pos_hbm, pos, sems.at[0]),
         pltpu.make_async_copy(frc_hbm, frc, sems.at[1]),
@@ -145,6 +145,8 @@
         fetch.wait()
     lane = lax.broadcasted_iota(jnp.int32, (1, LANES), 1)
     plane = cell_dev * tiles
+    last = share * 6 * tiles
+    table = jnp.full((1, LANES), -1.0, f32)
     for m in range(3 * n_pairs):
         kind, turn = m // n_pairs, m % n_pairs
         out = outs[turn]
@@ -154,7 +156,7 @@
             a = lax.rem(cells[0, s], cell_dev)
             live = s < count[0]
             b = jnp.where(live, lax.rem(cells[1, s], cell_dev), -1)
-            table[m * share + k] = jnp.where(live, a, -1)
+            table = jnp.where(lane == m * share + k, jnp.where(live, a, -1).astype(f32), table)
             label = jnp.where(lane == k, b.astype(f32), label)
             base = row_base(a, tiles)
             for c in range(6):
@@ -163,11 +165,11 @@
                 out[kind, row : row + tiles, :] = source[
                     pl.ds(base + c % 3 * plane, tiles, stride=8), :
                 ]
-        last = share * 6 * tiles
         out[kind, last : last + 1, :] = label
-
-
-def pair_kernel(sizes, kinds, started, *refs):
+    outs[0][0, last + 1 : last + 2, :] = table
+
+
+def pair_kernel(sizes, kinds, started, marked, *refs):
     n_space, n_pairs, share, cell_dev, tiles = sizes
     n = len(kinds)
     messages, (pos, frc) = refs[:n], refs[n : n + 2]
@@ -177,6 +179,7 @@
     plane = cell_dev * tiles
     if not started:
         acc[...] = jnp.zeros_like(acc)
+    if marked:
         outs[2][...] = jnp.zeros_like(outs[2])
     here = lax.axis_index("space")
     number = jnp.int32(0)
@@ -248,22 +251,23 @@
         several([number - 1])
 
 
-def add_kernel(sizes, table, acc, *refs):
+def add_kernel(sizes, where, acc, mine, *refs):
     n_space, n_pairs, share, cell_dev, tiles = sizes
     replies, out = refs[:-1], refs[-1]
     plane = cell_dev * tiles
+    last = share * 6 * tiles
+    table = mine[0, last + 1 : last + 2, :].astype(jnp.int32)
     out[...] = acc[...]
-    for m in range(3 * n_pairs):
-        kind, turn = m // n_pairs, m % n_pairs
+    for m, (operand, block) in enumerate(where):
         for k in range(share):
-            a = table[m * share + k]
+            a = table[0, m * share + k]
             live = a >= 0
             base = row_base(jnp.maximum(a, 0), tiles)
             places = [pl.ds(base + c * plane, tiles, stride=8) for c in range(3)]
             totals = []
             for c in range(3):
                 row = (k * 3 + c) * tiles
-                term = jnp.where(live, replies[turn][kind, row : row + tiles, :], 0.0)
+                term = jnp.where(live, replies[operand][block, row : row + tiles, :], 0.0)
                 totals.append(out[places[c], :] + term)
             for c in range(3):
                 out[places[c], :] = totals[c]
@@ -306,11 +310,11 @@
         moves = [(i, (i + away_of(kind, i % 2)) % n_space) for i in range(n_space)]
         return lax.ppermute(value, "space", moves)
 
-    packed = pl.pallas_call(
+    sent = pl.pallas_call(
         functools.partial(pack_kernel, sizes),
-        out_shape=[message] * n_pairs + [jax.ShapeDtypeStruct((n_slots,), jnp.int32)],
+        out_shape=[message] * n_pairs,
         in_specs=[smem, smem, hbm, hbm],
-        out_specs=[vmem] * n_pairs + [smem],
+        out_specs=[vmem] * n_pairs,
         scratch_shapes=[
             pltpu.SMEM((n_slots,), jnp.int32),
             pltpu.SMEM((3 * n_pairs,), jnp.int32),
@@ -321,20 +325,19 @@
         compiler_params=pltpu.CompilerParams(vmem_limit_bytes=60 * 1024 * 1024),
         name="pack",
     )(pair_cells, pair_count, pos, frc)
-    sent, table = packed[:n_pairs], packed[n_pairs]
     got = [sent[0]] + [across(sent[turn], turn) for turn in range(1, n_pairs)]
 
-    def pairs(arrived, before):
+    def pairs(arrived, before, marked=False):
         kinds = [kind for kind, _ in arrived]
         values = [value for _, value in arrived]
         n = len(values)
         blocks = sum(value.shape[0] for value in values)
         return pl.pallas_call(
-            functools.partial(pair_kernel, sizes, kinds, len(before)),
+            functools.partial(pair_kernel, sizes, kinds, len(before), marked),
             out_shape=[total, jax.ShapeDtypeStruct((blocks * rows_out, LANES), f32)]
-            + [jax.ShapeDtypeStruct((1, LANES), f32)] * (not before),
+            + [jax.ShapeDtypeStruct((1, LANES), f32)] * marked,
             in_specs=[vmem] * (n + 2 + len(before)),
-            out_specs=[vmem] * (2 + (not before)),
+            out_specs=[vmem] * (2 + marked),
             scratch_shapes=[
                 pltpu.VMEM((blocks * rows_in, LANES), f32),
                 pltpu.SMEM((2, blocks * share + 1), jnp.int32),
@@ -352,31 +355,38 @@
     own = [sent[0][kind : kind + 1] for kind in range(3)]
     core = [got[1][kind : kind + 1] for kind in range(3)]
     out_1n = beyond(jnp.concatenate([own[1], core[1]]), 1)
-    acc, reply_0n, nothing = pairs([(0, own[0]), (0, core[0])], [])
+    acc, reply_0n, nothing = pairs([(0, own[0]), (0, core[0])], [], True)
     rest = [got[turn] + nothing[None] for turn in far]
     out_1f = beyond(jnp.stack([value[1] for value in rest]), 1)
     out_2 = beyond(jnp.concatenate([own[2], core[2]] + [value[2:] for value in rest]), 2)
     acc, reply_m = pairs([(1, out_1n)] + [(0, got[turn][0:1]) for turn in far], [acc])
-    acc, reply_f = pairs([(1, out_1f), (2, out_2)], [acc])
+    acc, reply_f, later = pairs([(1, out_1f), (2, out_2)], [acc], True)
     reply_0n, reply_m, reply_f = (
         value.reshape(-1, rows_out, LANES) for value in (reply_0n, reply_m, reply_f)
     )
     cut = n_pairs - 2
-    back_0 = jnp.concatenate([reply_0n, reply_m[2:]])
-    back_1 = beyond(jnp.concatenate([reply_m[:2], reply_f[:cut]]), 1)
-    back_2 = beyond(reply_f[cut:], 2)
-    back = []
-    for turn in range(n_pairs):
-        value = jnp.stack([back_0[turn], back_1[turn], back_2[turn]])
-        back.append(across(value, turn) if turn else value)
+    back_1n = beyond(reply_m[:2] + later[None], 1)
+    back_2n = beyond(reply_f[cut : cut + 2], 2)
+    home = [
+        across(jnp.stack([reply_m[turn], reply_f[turn - 2], reply_f[cut + turn]]), turn)
+        for turn in far
+    ]
+    back_1f = beyond(jnp.stack([value[1] for value in home]), 1)
+    back_2f = beyond(jnp.stack([value[2] for value in home]), 2)
+    core = across(jnp.stack([reply_0n[1], back_1n[1], back_2n[1]]), 1)
+    mine = jnp.stack([reply_0n[0], back_1n[0], back_2n[0]])
+    replies = [mine, core, back_1f, back_2f] + home
+    where = [(0, 0), (1, 0)] + [(2 + turn, 0) for turn in far]
+    where += [(0, 1), (1, 1)] + [(2, turn - 2) for turn in far]
+    where += [(0, 2), (1, 2)] + [(3, turn - 2) for turn in far]
     velocity = pl.pallas_call(
-        functools.partial(add_kernel, sizes),
+        functools.partial(add_kernel, sizes, where),
         out_shape=total,
-        in_specs=[smem] + [vmem] * (1 + n_pairs),
+        in_specs=[vmem] * (2 + len(replies)),
         out_specs=vmem,
         compiler_params=pltpu.CompilerParams(vmem_limit_bytes=48 * 1024 * 1024),
         name="add",
-    )(table, acc, *back)
+    )(acc, own[0], *replies)
     return cell_rows(velocity, cell_dev, points)
 
 

time: 53.1 us -> 54.7 us (1.030); the launches traced: 52.8 us -> 55.2 us
  starting transfers between devices: 12.6 us -> 19.1 us
  Pallas kernels: 24.2 us -> 19.9 us
  waiting for transfers between devices: 13.4 us -> 14.2 us
  local copies, waits for them, and re-layouts: 1.67 us -> 1.05 us
    ppermute x5 -> x7, starting transfers between devices: 7.47 us -> 15.7 us  [beyond(): return lax.ppermute(value, 'space', moves)]
    pallas_call x4, Pallas kernels: 20.9 us -> 16.6 us  [the longest x3 15.5 us: pairs(): pl.pallas_call(functools.partial(pair_kernel, sizes, kinds, len(before),...]
    ppermute x6, starting transfers between devices: 5.13 us -> 3.36 us  [across(): return lax.ppermute(value, 'pairs', [(j, j ^ turn) for j in range(n_pairs)])]
    ppermute x5 -> x7, waiting for transfers between devices: 9.03 us -> 9.79 us  [beyond(): return lax.ppermute(value, 'space', moves)]
    unnamed x6 -> x4, local copies, waits for them, and re-layouts: 0.64 us -> 0.01 us
  transfers between devices with their start and end apart: 11 -> 13, of which waited for: 6 -> 9; matrix products, arithmetic and copies ran while one was open for 2% -> 2% of each run, Pallas kernels for 16% -> 12%
where the time goes in v4:
time: 54.7 us; the launch traced here: 55.2 us
  Pallas kernels  19.9 us (36%)
  starting transfers between devices  19.1 us (35%)
  waiting for transfers between devices  14.2 us (26%)
  local copies, waits for them, and re-layouts  1.05 us (2%)
  between operations  0.86 us (2%)
    ppermute x7, starting transfers between devices, beyond(): return lax.ppermute(value, 'space', moves)  15.7 us
    pallas_call x3, Pallas kernels, pairs(): pl.pallas_call(functools.partial(pair_kernel, sizes, kinds, len(before),...  15.5 us
    ppermute x7, waiting for transfers between devices, beyond(): return lax.ppermute(value, 'space', moves)  9.79 us
    ppermute x6, waiting for transfers between devices, across(): return lax.ppermute(value, 'pairs', [(j, j ^ turn) for j in range(n_pairs)])  4.39 us
    ppermute x6, starting transfers between devices, across(): return lax.ppermute(value, 'pairs', [(j, j ^ turn) for j in range(n_pairs)])  3.36 us
    pallas_call x1, Pallas kernels, body(): pl.pallas_call(functools.partial(pack_kernel, sizes), out_shape=[message]...  3.25 us
    pallas_call x1, Pallas kernels, body(): pl.pallas_call(functools.partial(add_kernel, sizes, where), out_shape=tot...  1.13 us
  transfers between devices with their start and end apart: 13, of which 9 were waited for; matrix products, arithmetic and copies ran while one was open for 2% of the time, Pallas kernels for 12%

profile of v4, /device:TPU:0, one launch (start us, length us, event | category | flops | bytes accessed | tf_op | source)
XLA Modules:
  0.0 55.2 jit_solution(3675202052479858322)
XLA Ops:
  0.7 3.3 %pack.1 = (f32[3,104,128]{2,1,0:T(8,128)}, f32[3,104,128]{2,1,0:T(8,128)}, f32[3,104,128]{2,1,0:T(8,128)}, f32[3,104,128]{2,1,0:T(8,128)}) custom-call(s32[2,48]{1,0:T(2,128)} %cells.1, s32[1]{0:T(128)S(6)} %copy.9.count, f32[768,128]{1,0:T(8,128)} %bitcast.41, f32[768,128]{1,0:T(8,128)} %bitcast.45), custom_call_target="tpu_custom_call" | custom-call | tf_op jit(solution)/shard_map/pack/pallas_call | solution.py:313
  3.9 3.0 %collective-permute-start = (f32[3,104,128]{2,1,0:T(8,128)}, f32[3,104,128]{2,1,0:T(8,128)S(1)}, u32[]{:S(2)}, u32[]{:S(2)}) collective-permute-start(f32[3,104,128]{2,1,0:T(8,128)} %get-tuple-element.17), channel_id=1, source_target_pairs={{0,2},{1,3},{2,0},{3,1},{4,6},{5,7},{6,4},{7,5},{8,10},{9,11},{10,... | collective-permute-start | bytes 479240 | tf_op jit(solution)/shard_map/ppermute | solution.py:307
  6.9 0.0 collective-permute-start.1
  6.9 0.2 collective-permute-start.2
  7.1 0.9 %fusion = (f32[1,104,128]{2,1,0:T(8,128)S(1)}, f32[1,104,128]{2,1,0:T(8,128)S(1)}, f32[1,104,128]{2,1,0:T(8,128)S(1)}) fusion(f32[3,104,128]{2,1,0:T(8,128)} %get-tuple-element.18), kind=kLoop, calls=%fused_computation.20 | loop fusion | bytes 319488 | tf_op jit(solution)/shard_map/slice | solution.py:355
  8.1 0.4 collective-permute-done.1
  8.6 1.6 %collective-permute-start.5 = (f32[2,104,128]{2,1,0:T(8,128)S(1)}, f32[2,104,128]{2,1,0:T(8,128)S(1)}, u32[]{:S(2)}, u32[]{:S(2)}) collective-permute-start(f32[2,104,128]{2,1,0:T(8,128)S(1)} %pad_maximum_fusion.2), channel_id=1, source_target_pairs={{0,4},{4,0},{8,12},{12,8},{16,20},{20,16},{24,28},{28,24},{1,5},{5... | collective-permute-start | bytes 319496 | tf_op jit(solution)/shard_map/ppermute | solution.py:311
  10.2 2.9 %pairs.3 = (f32[768,128]{1,0:T(8,128)S(1)}, f32[96,128]{1,0:T(8,128)S(1)}, f32[1,128]{1,0:T(1,128)S(1)}) custom-call(f32[1,104,128]{2,1,0:T(8,128)S(1)} %get-tuple-element.31.refs_0_.mine, f32[1,104,128]{2,1,0:T(8,128)S(1)} %get-tuple-element.34.refs_1_, f32[768,128]{1,0:T(8,128)S(1)} %bitcast.42, f32[768,128]{1,0:T(8,128)S(1)} %bitcast.46), custom_call_target="tpu_custom_call" | custom-call | flops 2000000000 | bytes 2000000 | tf_op jit(solution)/shard_map/pairs/pallas_call | solution.py:335
  13.1 0.0 collective-permute-done
  13.1 0.9 %collective-permute-done.2 = f32[3,104,128]{2,1,0:T(8,128)S(1)} collective-permute-done((f32[3,104,128]{2,1,0:T(8,128)}, f32[3,104,128]{2,1,0:T(8,128)S(1)}, u32[]{:S(2)}, u32[]{:S(2)}) %collective-permute-start.2) | collective-permute-done | bytes 159776 | tf_op jit(solution)/shard_map/ppermute | solution.py:307
  14.1 1.6 %collective-permute-start.3 = (f32[2,104,128]{2,1,0:T(8,128)S(1)}, f32[2,104,128]{2,1,0:T(8,128)S(1)}, u32[]{:S(2)}, u32[]{:S(2)}) collective-permute-start(f32[2,104,128]{2,1,0:T(8,128)S(1)} %pad_maximum_fusion.1), channel_id=1, source_target_pairs={{0,4},{4,0},{8,12},{12,8},{16,20},{20,16},{24,28},{28,24},{1,5},{5... | collective-permute-start | bytes 319496 | tf_op jit(solution)/shard_map/ppermute | solution.py:311
  15.7 3.6 %collective-permute-start.4 = (f32[4,104,128]{2,1,0:T(8,128)S(1)}, f32[4,104,128]{2,1,0:T(8,128)S(1)}, u32[]{:S(2)}, u32[]{:S(2)}) collective-permute-start(f32[4,104,128]{2,1,0:T(8,128)S(1)} %pad_maximum_fusion), channel_id=1, source_target_pairs={{0,28},{4,8},{8,4},{12,16},{16,12},{20,24},{24,20},{28,0},{1,29},{... | collective-permute-start | bytes 638984 | tf_op jit(solution)/shard_map/ppermute | solution.py:311
  19.3 0.0 collective-permute-done.5.refs_0_
  19.3 3.9 %pairs.4 = (f32[768,128]{1,0:T(8,128)S(1)}, f32[192,128]{1,0:T(8,128)S(1)}) custom-call(f32[2,104,128]{2,1,0:T(8,128)S(1)} %collective-permute-done.5.refs_0_, f32[1,104,128]{2,1,0:T(8,128)S(1)} %slice.167.refs_1_, f32[1,104,128]{2,1,0:T(8,128)S(1)} %slice.168.refs_2_, f32[768,128]{1,0:T(8,128)S(1)} %bitcast.43, ...), custom_call_target="tpu_custom_call", output_to_operand_aliasing={{0}: (5, {})} | custom-call | flops 4000000000 | bytes 2000000 | tf_op jit(solution)/shard_map/pairs/pallas_call | solution.py:335
  23.2 0.1 collective-permute-done.3.refs_0_
  23.4 2.7 %collective-permute-done.4.refs_1_ = f32[4,104,128]{2,1,0:T(8,128)S(1)} collective-permute-done((f32[4,104,128]{2,1,0:T(8,128)S(1)}, f32[4,104,128]{2,1,0:T(8,128)S(1)}, u32[]{:S(2)}, u32[]{:S(2)}) %collective-permute-start.4) | collective-permute-done | bytes 213024 | tf_op jit(solution)/shard_map/ppermute | solution.py:311
  26.1 8.7 %pairs.5 = (f32[768,128]{1,0:T(8,128)S(1)}, f32[288,128]{1,0:T(8,128)S(1)}, f32[1,128]{1,0:T(1,128)S(1)}) custom-call(f32[2,104,128]{2,1,0:T(8,128)S(1)} %collective-permute-done.3.refs_0_, f32[4,104,128]{2,1,0:T(8,128)S(1)} %collective-permute-done.4.refs_1_, f32[768,128]{1,0:T(8,128)S(1)} %bitcast.44, ...), custom_call_target="tpu_custom_call", output_to_operand_aliasing={{0}: (4, {})} | custom-call | flops 6000000000 | bytes 2000000 | tf_op jit(solution)/shard_map/pairs/pallas_call | solution.py:335
  34.9 0.1 collective-permute-start.6
  34.9 7.0 %collective-permute-start.7 = (f32[2,48,128]{2,1,0:T(8,128)S(1)}, f32[2,48,128]{2,1,0:T(8,128)S(1)}, u32[]{:S(2)}, u32[]{:S(2)}) collective-permute-start(f32[2,48,128]{2,1,0:T(8,128)S(1)} %bitcast.52), channel_id=1, source_target_pairs={{0,28},{4,8},{8,4},{12,16},{16,12},{20,24},{24,20},{28,0},{1,29},{... | collective-permute-start | bytes 147464 | tf_op jit(solution)/shard_map/ppermute | solution.py:311
  41.9 0.0 collective-permute-start.10
  41.9 0.1 collective-permute-start.9
  42.0 0.0 collective-permute-done.6
  42.0 1.9 %collective-permute-done.7 = f32[2,48,128]{2,1,0:T(8,128)S(1)} collective-permute-done((f32[2,48,128]{2,1,0:T(8,128)S(1)}, f32[2,48,128]{2,1,0:T(8,128)S(1)}, u32[]{:S(2)}, u32[]{:S(2)}) %collective-permute-start.7) | collective-permute-done | bytes 49184 | tf_op jit(solution)/shard_map/ppermute | solution.py:311
  44.0 0.1 collective-permute-start.8
  44.1 1.8 %collective-permute-done.10.refs_5_ = f32[3,48,128]{2,1,0:T(8,128)S(1)} collective-permute-done((f32[3,48,128]{2,1,0:T(8,128)S(1)}, f32[3,48,128]{2,1,0:T(8,128)S(1)}, u32[]{:S(2)}, u32[]{:S(2)}) %collective-permute-start.10) | collective-permute-done | bytes 73760 | tf_op jit(solution)/shard_map/ppermute | solution.py:307
  45.9 1.2 %collective-permute-done.9.refs_4_ = f32[3,48,128]{2,1,0:T(8,128)S(1)} collective-permute-done((f32[3,48,128]{2,1,0:T(8,128)S(1)}, f32[3,48,128]{2,1,0:T(8,128)S(1)}, u32[]{:S(2)}, u32[]{:S(2)}) %collective-permute-start.9) | collective-permute-done | bytes 73760 | tf_op jit(solution)/shard_map/ppermute | solution.py:307
  47.1 0.1 collective-permute-start.11
  47.2 1.8 %collective-permute-start.12 = (f32[2,48,128]{2,1,0:T(8,128)S(1)}, f32[2,48,128]{2,1,0:T(8,128)S(1)}, u32[]{:S(2)}, u32[]{:S(2)}) collective-permute-start(f32[2,48,128]{2,1,0:T(8,128)S(1)} %pad_maximum_fusion.8), channel_id=1, source_target_pairs={{0,28},{4,8},{8,4},{12,16},{16,12},{20,24},{24,20},{28,0},{1,29},{... | collective-permute-start | bytes 147464 | tf_op jit(solution)/shard_map/ppermute | solution.py:311
  49.0 0.0 collective-permute-done.8.refs_1_
  49.0 2.2 %collective-permute-done.11.refs_2_ = f32[2,48,128]{2,1,0:T(8,128)S(1)} collective-permute-done((f32[2,48,128]{2,1,0:T(8,128)S(1)}, f32[2,48,128]{2,1,0:T(8,128)S(1)}, u32[]{:S(2)}, u32[]{:S(2)}) %collective-permute-start.11) | collective-permute-done | bytes 49184 | tf_op jit(solution)/shard_map/ppermute | solution.py:311
  51.3 2.8 %collective-permute-done.12.refs_3_ = f32[2,48,128]{2,1,0:T(8,128)S(1)} collective-permute-done((f32[2,48,128]{2,1,0:T(8,128)S(1)}, f32[2,48,128]{2,1,0:T(8,128)S(1)}, u32[]{:S(2)}, u32[]{:S(2)}) %collective-permute-start.12) | collective-permute-done | bytes 49184 | tf_op jit(solution)/shard_map/ppermute | solution.py:311
  54.0 1.1 %add.40 = f32[768,128]{1,0:T(8,128)} custom-call(f32[768,128]{1,0:T(8,128)S(1)} %get-tuple-element.24.acc, f32[1,104,128]{2,1,0:T(8,128)S(1)} %get-tuple-element.31.refs_0_.mine, f32[3,48,128]{2,1,0:T(8,128)S(1)} %pad_maximum_fusion.3.refs_0_, f32[3,48,128]{2,1,0:T(8,128)S(1)} %collective-permute-done.8.refs_1_, ...), custom_call_target="tpu_custom_call" | custom-call | tf_op jit(solution)/shard_map/add/pallas_call | solution.py:382
  (28 shorter events, 0.2 us)
Async XLA Ops:
  3.9 9.2 %collective-permute-start = (f32[3,104,128]{2,1,0:T(8,128)}, f32[3,104,128]{2,1,0:T(8,128)S(1)}, u32[]{:S(2)}, u32[]{:S(2)}) collective-permute-start(f32[3,104,128]{2,1,0:T(8,128)} %get-tuple-element.17), channel_id=1, source_target_pairs={{0,2},{1,3},{2,0},{3,1},{4,6},{5,7},{6,4},{7,5},{8,10},{9,11},{10,... | collective-permute-start | bytes 479240 | tf_op jit(solution)/shard_map/ppermute | solution.py:307
  6.9 1.6 %collective-permute-start.1 = (f32[3,104,128]{2,1,0:T(8,128)}, f32[3,104,128]{2,1,0:T(8,128)S(1)}, u32[]{:S(2)}, u32[]{:S(2)}) collective-permute-start(f32[3,104,128]{2,1,0:T(8,128)} %get-tuple-element.19), channel_id=1, source_target_pairs={{0,1},{1,0},{2,3},{3,2},{4,5},{5,4},{6,7},{7,6},{8,9},{9,8},{10,11... | collective-permute-start | bytes 479240 | tf_op jit(solution)/shard_map/ppermute | solution.py:307
  6.9 7.1 %collective-permute-start.2 = (f32[3,104,128]{2,1,0:T(8,128)}, f32[3,104,128]{2,1,0:T(8,128)S(1)}, u32[]{:S(2)}, u32[]{:S(2)}) collective-permute-start(f32[3,104,128]{2,1,0:T(8,128)} %get-tuple-element.21), channel_id=1, source_target_pairs={{0,3},{1,2},{2,1},{3,0},{4,7},{5,6},{6,5},{7,4},{8,11},{9,10},{10,... | collective-permute-start | bytes 479240 | tf_op jit(solution)/shard_map/ppermute | solution.py:307
  7.1 3.0 %copy-start = (f32[64,3,512]{2,0,1:T(8,128)S(1)}, f32[64,3,512]{2,0,1:T(8,128)}, u32[]{:S(2)}) copy-start(f32[64,3,512]{2,0,1:T(8,128)} %param.4) | copy-start | bytes 1179652
  7.1 3.0 %copy-start.1 = (f32[64,3,512]{2,0,1:T(8,128)S(1)}, f32[64,3,512]{2,0,1:T(8,128)}, u32[]{:S(2)}) copy-start(f32[64,3,512]{2,0,1:T(8,128)} %param.5) | copy-start | bytes 1179652
  8.6 10.8 %collective-permute-start.5 = (f32[2,104,128]{2,1,0:T(8,128)S(1)}, f32[2,104,128]{2,1,0:T(8,128)S(1)}, u32[]{:S(2)}, u32[]{:S(2)}) collective-permute-start(f32[2,104,128]{2,1,0:T(8,128)S(1)} %pad_maximum_fusion.2), channel_id=1, source_target_pairs={{0,4},{4,0},{8,12},{12,8},{16,20},{20,16},{24,28},{28,24},{1,5},{5... | collective-permute-start | bytes 319496 | tf_op jit(solution)/shard_map/ppermute | solution.py:311
  14.1 9.2 %collective-permute-start.3 = (f32[2,104,128]{2,1,0:T(8,128)S(1)}, f32[2,104,128]{2,1,0:T(8,128)S(1)}, u32[]{:S(2)}, u32[]{:S(2)}) collective-permute-start(f32[2,104,128]{2,1,0:T(8,128)S(1)} %pad_maximum_fusion.1), channel_id=1, source_target_pairs={{0,4},{4,0},{8,12},{12,8},{16,20},{20,16},{24,28},{28,24},{1,5},{5... | collective-permute-start | bytes 319496 | tf_op jit(solution)/shard_map/ppermute | solution.py:311
  15.7 10.4 %collective-permute-start.4 = (f32[4,104,128]{2,1,0:T(8,128)S(1)}, f32[4,104,128]{2,1,0:T(8,128)S(1)}, u32[]{:S(2)}, u32[]{:S(2)}) collective-permute-start(f32[4,104,128]{2,1,0:T(8,128)S(1)} %pad_maximum_fusion), channel_id=1, source_target_pairs={{0,28},{4,8},{8,4},{12,16},{16,12},{20,24},{24,20},{28,0},{1,29},{... | collective-permute-start | bytes 638984 | tf_op jit(solution)/shard_map/ppermute | solution.py:311
  34.9 7.2 %collective-permute-start.6 = (f32[2,48,128]{2,1,0:T(8,128)S(1)}, f32[2,48,128]{2,1,0:T(8,128)S(1)}, u32[]{:S(2)}, u32[]{:S(2)}) collective-permute-start(f32[2,48,128]{2,1,0:T(8,128)S(1)} %broadcast_add_fusion.2), channel_id=1, source_target_pairs={{0,4},{4,0},{8,12},{12,8},{16,20},{20,16},{24,28},{28,24},{1,5},{5... | collective-permute-start | bytes 147464 | tf_op jit(solution)/shard_map/ppermute | solution.py:311
  34.9 9.0 %collective-permute-start.7 = (f32[2,48,128]{2,1,0:T(8,128)S(1)}, f32[2,48,128]{2,1,0:T(8,128)S(1)}, u32[]{:S(2)}, u32[]{:S(2)}) collective-permute-start(f32[2,48,128]{2,1,0:T(8,128)S(1)} %bitcast.52), channel_id=1, source_target_pairs={{0,28},{4,8},{8,4},{12,16},{16,12},{20,24},{24,20},{28,0},{1,29},{... | collective-permute-start | bytes 147464 | tf_op jit(solution)/shard_map/ppermute | solution.py:311
  41.9 3.9 %collective-permute-start.10 = (f32[3,48,128]{2,1,0:T(8,128)S(1)}, f32[3,48,128]{2,1,0:T(8,128)S(1)}, u32[]{:S(2)}, u32[]{:S(2)}) collective-permute-start(f32[3,48,128]{2,1,0:T(8,128)S(1)} %pad_maximum_fusion.6), channel_id=1, source_target_pairs={{0,3},{1,2},{2,1},{3,0},{4,7},{5,6},{6,5},{7,4},{8,11},{9,10},{10,... | collective-permute-start | bytes 221192 | tf_op jit(solution)/shard_map/ppermute | solution.py:307
  41.9 5.2 %collective-permute-start.9 = (f32[3,48,128]{2,1,0:T(8,128)S(1)}, f32[3,48,128]{2,1,0:T(8,128)S(1)}, u32[]{:S(2)}, u32[]{:S(2)}) collective-permute-start(f32[3,48,128]{2,1,0:T(8,128)S(1)} %pad_maximum_fusion.5), channel_id=1, source_target_pairs={{0,2},{1,3},{2,0},{3,1},{4,6},{5,7},{6,4},{7,5},{8,10},{9,11},{10,... | collective-permute-start | bytes 221192 | tf_op jit(solution)/shard_map/ppermute | solution.py:307
  44.0 5.0 %collective-permute-start.8 = (f32[3,48,128]{2,1,0:T(8,128)S(1)}, f32[3,48,128]{2,1,0:T(8,128)S(1)}, u32[]{:S(2)}, u32[]{:S(2)}) collective-permute-start(f32[3,48,128]{2,1,0:T(8,128)S(1)} %pad_maximum_fusion.4), channel_id=1, source_target_pairs={{0,1},{1,0},{2,3},{3,2},{4,5},{5,4},{6,7},{7,6},{8,9},{9,8},{10,11... | collective-permute-start | bytes 221192 | tf_op jit(solution)/shard_map/ppermute | solution.py:307
  47.1 4.2 %collective-permute-start.11 = (f32[2,48,128]{2,1,0:T(8,128)S(1)}, f32[2,48,128]{2,1,0:T(8,128)S(1)}, u32[]{:S(2)}, u32[]{:S(2)}) collective-permute-start(f32[2,48,128]{2,1,0:T(8,128)S(1)} %pad_maximum_fusion.7), channel_id=1, source_target_pairs={{0,4},{4,0},{8,12},{12,8},{16,20},{20,16},{24,28},{28,24},{1,5},{5... | collective-permute-start | bytes 147464 | tf_op jit(solution)/shard_map/ppermute | solution.py:311
  47.2 6.9 %collective-permute-start.12 = (f32[2,48,128]{2,1,0:T(8,128)S(1)}, f32[2,48,128]{2,1,0:T(8,128)S(1)}, u32[]{:S(2)}, u32[]{:S(2)}) collective-permute-start(f32[2,48,128]{2,1,0:T(8,128)S(1)} %pad_maximum_fusion.8), channel_id=1, source_target_pairs={{0,28},{4,8},{8,4},{12,16},{16,12},{20,24},{24,20},{28,0},{1,29},{... | collective-permute-start | bytes 147464 | tf_op jit(solution)/shard_map/ppermute | solution.py:311

commit v5 on v4

--- a/solution.py
+++ b/solution.py
@@ -304,11 +304,17 @@
     total = jax.ShapeDtypeStruct((3 * cell_dev * tiles, LANES), f32)
 
     def across(value, turn):
-        return lax.ppermute(value, "pairs", [(j, j ^ turn) for j in range(n_pairs)])
+        groups = [[j, j ^ turn] for j in range(n_pairs) if j < j ^ turn]
+        both = lax.all_gather(value, "pairs", axis_index_groups=groups)
+        mine = lax.axis_index("pairs")
+        return lax.dynamic_index_in_dim(both, jnp.where(mine < mine ^ turn, 1, 0), 0, False)
 
     def beyond(value, kind):
-        moves = [(i, (i + away_of(kind, i % 2)) % n_space) for i in range(n_space)]
-        return lax.ppermute(value, "space", moves)
+        first = kind - 1
+        groups = [[i, (i + 1) % n_space] for i in range(first, n_space, 2)]
+        both = lax.all_gather(value, "space", axis_index_groups=groups)
+        mine = lax.axis_index("space")
+        return lax.dynamic_index_in_dim(both, (mine + first + 1) % 2, 0, False)
 
     sent = pl.pallas_call(
         functools.partial(pack_kernel, sizes),

time: 54.7 us -> 102 us (1.86)
  blocking collectives: 0 us -> 79.5 us
  starting transfers between devices: 19.1 us -> 0 us
  waiting for transfers between devices: 14.2 us -> 0 us
  Pallas kernels: 19.9 us -> 21.6 us
    all_gather x0 -> x13, blocking collectives: none -> 79.5 us  [the longest x7 50.5 us: beyond(): both = lax.all_gather(value, 'space', axis_index_groups=groups)]
    ppermute x13 -> x0, starting transfers between devices: 19.1 us -> none  [the longest x7 15.7 us: beyond(): return lax.ppermute(value, 'space', moves)]
    ppermute x13 -> x0, waiting for transfers between devices: 14.2 us -> none  [the longest x7 9.79 us: beyond(): return lax.ppermute(value, 'space', moves)]
    pallas_call x3, Pallas kernels: 15.5 us -> 17.2 us  [pairs(): pl.pallas_call(functools.partial(pair_kernel, sizes, kinds, len(before),...]
  transfers between devices with their start and end apart: 13 -> 0, of which waited for: 9 -> 0; matrix products, arithmetic and copies ran while one was open for 2% -> 0% of each run, Pallas kernels for 12% -> 0%
where the time goes in v5:
time: 102 us; the launch traced here: 103 us
  blocking collectives  79.5 us (78%)
  Pallas kernels  21.6 us (21%)
  local copies, waits for them, and re-layouts  1.06 us (1%)
    all_gather x7, blocking collectives, beyond(): both = lax.all_gather(value, 'space', axis_index_groups=groups)  50.5 us
    all_gather x6, blocking collectives, across(): both = lax.all_gather(value, 'pairs', axis_index_groups=groups)  29 us
    pallas_call x3, Pallas kernels, pairs(): pl.pallas_call(functools.partial(pair_kernel, sizes, kinds, len(before),...  17.2 us
    pallas_call x1, Pallas kernels, body(): pl.pallas_call(functools.partial(pack_kernel, sizes), out_shape=[message]...  3.26 us

profile of v5, /device:TPU:0, one launch (start us, length us, event | category | flops | bytes accessed | tf_op | source)
XLA Modules:
  0.0 103.1 jit_solution(13069748342129650201)
XLA Ops:
  0.7 3.3 %pack.1 = (f32[3,104,128]{2,1,0:T(8,128)}, f32[3,104,128]{2,1,0:T(8,128)}, f32[3,104,128]{2,1,0:T(8,128)}, f32[3,104,128]{2,1,0:T(8,128)}) custom-call(s32[2,48]{1,0:T(2,128)} %cells.1, s32[1]{0:T(128)S(6)} %copy.9.count, f32[768,128]{1,0:T(8,128)} %bitcast.98, f32[768,128]{1,0:T(8,128)} %bitcast.102), custom_call_target="tpu_custom_call" | custom-call | tf_op jit(solution)/shard_map/pack/pallas_call | solution.py:319
  3.9 0.0 copy-start.2
  3.9 8.1 %all-gather = f32[6,104,128]{2,1,0:T(8,128)S(1)} all-gather(f32[3,104,128]{2,1,0:T(8,128)} %get-tuple-element.17), channel_id=2, replica_groups={{0,2},{1,3},{4,6},{5,7},{8,10},{9,11},{12,14},{13,15},{16,18},{17,19},{..., dimensions={0}, use_global_device_ids=true | all-gather | bytes 479232 | tf_op jit(solution)/shard_map/all_gather | solution.py:308
  12.0 0.0 copy-done.2
  12.1 0.0 copy-start.4
  12.1 0.9 copy-done.4
  13.0 2.0 %all-gather.1 = f32[6,104,128]{2,1,0:T(8,128)S(1)} all-gather(f32[3,104,128]{2,1,0:T(8,128)S(1)} %copy-done.4), channel_id=3, replica_groups={{0,1},{2,3},{4,5},{6,7},{8,9},{10,11},{12,13},{14,15},{16,17},{18,19},{..., dimensions={0}, use_global_device_ids=true | all-gather | bytes 479232 | tf_op jit(solution)/shard_map/all_gather | solution.py:308
  15.0 0.0 copy-start.3
  15.0 5.8 %all-gather.5 = f32[4,104,128]{2,1,0:T(8,128)S(1)} all-gather(f32[2,104,128]{2,1,0:T(8,128)S(1)} %pad_maximum_fusion.2), channel_id=7, replica_groups={{0,4},{8,12},{16,20},{24,28},{1,5},{9,13},{17,21},{25,29},{2,6},{10,14}..., dimensions={0}, use_global_device_ids=true | all-gather | bytes 319488 | tf_op jit(solution)/shard_map/all_gather | solution.py:315
  20.9 0.0 copy-start
  20.9 0.0 copy-start.1
  20.9 0.0 copy-done.3
  20.9 7.0 %all-gather.2 = f32[6,104,128]{2,1,0:T(8,128)S(1)} all-gather(f32[3,104,128]{2,1,0:T(8,128)S(1)} %copy-done.3), channel_id=4, replica_groups={{0,3},{1,2},{4,7},{5,6},{8,11},{9,10},{12,15},{13,14},{16,19},{17,18},{..., dimensions={0}, use_global_device_ids=true | all-gather | bytes 479232 | tf_op jit(solution)/shard_map/all_gather | solution.py:308
  27.9 0.0 copy-done
  27.9 0.0 copy-done.1
  27.9 2.6 %pairs.3 = (f32[768,128]{1,0:T(8,128)S(1)}, f32[96,128]{1,0:T(8,128)S(1)}, f32[1,128]{1,0:T(1,128)S(1)}) custom-call(f32[1,104,128]{2,1,0:T(8,128)S(1)} %get-tuple-element.34.refs_0_.mine, f32[1,104,128]{2,1,0:T(8,128)S(1)} %get-tuple-element.31.refs_1_, f32[768,128]{1,0:T(8,128)S(1)} %bitcast.99, f32[768,128]{1,0:T(8,128)S(1)} %bitcast.103), custom_call_target="tpu_custom_call" | custom-call | flops 2000000000 | bytes 2000000 | tf_op jit(solution)/shard_map/pairs/pallas_call | solution.py:341
  30.6 5.9 %all-gather.3 = f32[4,104,128]{2,1,0:T(8,128)S(1)} all-gather(f32[2,104,128]{2,1,0:T(8,128)S(1)} %pad_maximum_fusion.1), channel_id=5, replica_groups={{0,4},{8,12},{16,20},{24,28},{1,5},{9,13},{17,21},{25,29},{2,6},{10,14}..., dimensions={0}, use_global_device_ids=true | all-gather | bytes 319488 | tf_op jit(solution)/shard_map/all_gather | solution.py:315
  36.5 11.5 %all-gather.4 = f32[8,104,128]{2,1,0:T(8,128)S(1)} all-gather(f32[4,104,128]{2,1,0:T(8,128)S(1)} %pad_maximum_fusion), channel_id=6, replica_groups={{4,8},{12,16},{20,24},{28,0},{5,9},{13,17},{21,25},{29,1},{6,10},{14,18..., dimensions={0}, use_global_device_ids=true | all-gather | bytes 638976 | tf_op jit(solution)/shard_map/all_gather | solution.py:315
  48.0 7.2 %pairs.4 = (f32[768,128]{1,0:T(8,128)S(1)}, f32[192,128]{1,0:T(8,128)S(1)}) custom-call(f32[2,104,128]{2,1,0:T(8,128)S(1)} %dynamic-slice_bitcast_fusion.1.refs_0_, f32[1,104,128]{2,1,0:T(8,128)S(1)} %dynamic-slice_bitcast_fusion.7.refs_1_, f32[1,104,128]{2,1,0:T(8,128)S(1)} %dynamic-slice_bitcast_fusion.6.refs_2_, ...), custom_call_target="tpu_custom_call", output_to_operand_aliasing={{0}: (5, {})} | custom-call | flops 4000000000 | bytes 2000000 | tf_op jit(solution)/shard_map/pairs/pallas_call | solution.py:341
  55.2 7.4 %pairs.5 = (f32[768,128]{1,0:T(8,128)S(1)}, f32[288,128]{1,0:T(8,128)S(1)}, f32[1,128]{1,0:T(1,128)S(1)}) custom-call(f32[2,104,128]{2,1,0:T(8,128)S(1)} %dynamic-slice_bitcast_fusion.2.refs_0_, f32[4,104,128]{2,1,0:T(8,128)S(1)} %dynamic-slice_bitcast_fusion.refs_1_, f32[768,128]{1,0:T(8,128)S(1)} %bitcast.101, ...), custom_call_target="tpu_custom_call", output_to_operand_aliasing={{0}: (4, {})} | custom-call | flops 6000000000 | bytes 2000000 | tf_op jit(solution)/shard_map/pairs/pallas_call | solution.py:341
  62.7 10.3 %all_gather.90 = f32[2,2,48,128]{3,2,1,0:T(8,128)S(1)} all-gather(f32[1,2,48,128]{3,2,1,0:T(8,128)S(1)} %bitcast.124), channel_id=1, replica_groups={{4,8},{12,16},{20,24},{28,0},{5,9},{13,17},{21,25},{29,1},{6,10},{14,18..., dimensions={0}, use_global_device_ids=true | all-gather | bytes 147456 | tf_op jit(solution)/shard_map/all_gather | solution.py:315
  73.1 4.8 %all_gather.88 = f32[2,2,48,128]{3,2,1,0:T(8,128)S(1)} all-gather(f32[1,2,48,128]{3,2,1,0:T(8,128)S(1)} %broadcast_add_fusion), channel_id=1, replica_groups={{0,4},{8,12},{16,20},{24,28},{1,5},{9,13},{17,21},{25,29},{2,6},{10,14}..., dimensions={0}, use_global_device_ids=true | all-gather | bytes 147456 | tf_op jit(solution)/shard_map/all_gather | solution.py:315
  77.9 1.9 %all-gather.6 = f32[6,48,128]{2,1,0:T(8,128)S(1)} all-gather(f32[3,48,128]{2,1,0:T(8,128)S(1)} %pad_maximum_fusion.4), channel_id=8, replica_groups={{0,1},{2,3},{4,5},{6,7},{8,9},{10,11},{12,13},{14,15},{16,17},{18,19},{..., dimensions={0}, use_global_device_ids=true | all-gather | bytes 221184 | tf_op jit(solution)/shard_map/all_gather | solution.py:308
  79.8 4.9 %all-gather.8 = f32[6,48,128]{2,1,0:T(8,128)S(1)} all-gather(f32[3,48,128]{2,1,0:T(8,128)S(1)} %pad_maximum_fusion.6), channel_id=10, replica_groups={{0,3},{1,2},{4,7},{5,6},{8,11},{9,10},{12,15},{13,14},{16,19},{17,18},{..., dimensions={0}, use_global_device_ids=true | all-gather | bytes 221184 | tf_op jit(solution)/shard_map/all_gather | solution.py:308
  84.7 5.0 %all-gather.7 = f32[6,48,128]{2,1,0:T(8,128)S(1)} all-gather(f32[3,48,128]{2,1,0:T(8,128)S(1)} %pad_maximum_fusion.5), channel_id=9, replica_groups={{0,2},{1,3},{4,6},{5,7},{8,10},{9,11},{12,14},{13,15},{16,18},{17,19},{..., dimensions={0}, use_global_device_ids=true | all-gather | bytes 221184 | tf_op jit(solution)/shard_map/all_gather | solution.py:308
  89.7 4.8 %all-gather.9 = f32[4,48,128]{2,1,0:T(8,128)S(1)} all-gather(f32[2,48,128]{2,1,0:T(8,128)S(1)} %pad_maximum_fusion.7), channel_id=11, replica_groups={{0,4},{8,12},{16,20},{24,28},{1,5},{9,13},{17,21},{25,29},{2,6},{10,14}..., dimensions={0}, use_global_device_ids=true | all-gather | bytes 147456 | tf_op jit(solution)/shard_map/all_gather | solution.py:315
  94.5 7.5 %all-gather.10 = f32[4,48,128]{2,1,0:T(8,128)S(1)} all-gather(f32[2,48,128]{2,1,0:T(8,128)S(1)} %pad_maximum_fusion.8), channel_id=12, replica_groups={{4,8},{12,16},{20,24},{28,0},{5,9},{13,17},{21,25},{29,1},{6,10},{14,18..., dimensions={0}, use_global_device_ids=true | all-gather | bytes 147456 | tf_op jit(solution)/shard_map/all_gather | solution.py:315
  102.0 1.1 %add.111 = f32[768,128]{1,0:T(8,128)} custom-call(f32[768,128]{1,0:T(8,128)S(1)} %get-tuple-element.24.acc, f32[1,104,128]{2,1,0:T(8,128)S(1)} %get-tuple-element.34.refs_0_.mine, f32[3,48,128]{2,1,0:T(8,128)S(1)} %pad_maximum_fusion.3.refs_0_, f32[3,48,128]{2,1,0:T(8,128)S(1)} %dynamic-slice_bitcast_fusion.5.refs_1_, ...), custom_call_target="tpu_custom_call" | custom-call | tf_op jit(solution)/shard_map/add/pallas_call | solution.py:388
  (33 shorter events, 0.3 us)
Async XLA Ops:
  3.9 8.1 %copy-start.2 = (f32[3,104,128]{2,1,0:T(8,128)S(1)}, f32[3,104,128]{2,1,0:T(8,128)}, u32[]{:S(2)}) copy-start(f32[3,104,128]{2,1,0:T(8,128)} %get-tuple-element.18) | copy-start | bytes 479236
  12.1 0.9 copy-start.4
  15.0 5.9 %copy-start.3 = (f32[3,104,128]{2,1,0:T(8,128)S(1)}, f32[3,104,128]{2,1,0:T(8,128)}, u32[]{:S(2)}) copy-start(f32[3,104,128]{2,1,0:T(8,128)} %get-tuple-element.21) | copy-start | bytes 479236
  20.9 7.0 %copy-start = (f32[64,3,512]{2,0,1:T(8,128)S(1)}, f32[64,3,512]{2,0,1:T(8,128)}, u32[]{:S(2)}) copy-start(f32[64,3,512]{2,0,1:T(8,128)} %param.4) | copy-start | bytes 1179652
  20.9 7.0 %copy-start.1 = (f32[64,3,512]{2,0,1:T(8,128)S(1)}, f32[64,3,512]{2,0,1:T(8,128)}, u32[]{:S(2)}) copy-start(f32[64,3,512]{2,0,1:T(8,128)} %param.5) | copy-start | bytes 1179652

commit v6 on v4

--- a/solution.py
+++ b/solution.py
@@ -14,6 +14,7 @@
 across_middle = 1.0
 LANES = 128
 FEATURES = 16
+GRAM = 8
 
 f32 = jnp.float32
 bf16 = jnp.bfloat16
@@ -29,42 +30,62 @@
     return parts
 
 
-def features(x, f):
-    norm = jnp.sum(x * x, axis=0, keepdims=True)
-    along = jnp.sum(x * f, axis=0, keepdims=True)
-    rows = [f] + [x[k : k + 1] * f for k in range(3)] + [norm * f + x * along]
-    rows.append(jnp.zeros_like(norm))
-    stacked = jnp.concatenate(rows, axis=0)
-    return jnp.concatenate([part.astype(bf16) for part in split(stacked, 3)], axis=0)
-
-
-def combine(sums, y):
-    force = sums[0:3]
-    moment = [sums[3 + 3 * k : 6 + 3 * k] for k in range(3)]
-    second = sums[12:15]
-    norm = jnp.sum(y * y, axis=0, keepdims=True)
-    trace = moment[0][0:1] + moment[1][1:2] + moment[2][2:3]
-    along = jnp.sum(y * force, axis=0, keepdims=True) - trace
-    turned = jnp.concatenate(
-        [jnp.sum(y * moment[k], axis=0, keepdims=True) for k in range(3)], axis=0
-    )
-    mixed = y[0:1] * moment[0] + y[1:2] * moment[1] + y[2:3] * moment[2]
-    velocity = (norm + 2.0 * eps_sq) * force + second - 2.0 * mixed + y * along - turned
-    return velocity * stokes_coef
-
-
-def gram_factors(x, y):
-    one = jnp.ones((1, x.shape[1]), f32)
-    none = jnp.zeros((3, x.shape[1]), f32)
-    norm_x = jnp.sum(x * x, axis=0, keepdims=True)
-    norm_y = jnp.sum(y * y, axis=0, keepdims=True) + eps_sq
-    left = split(jnp.concatenate([x, norm_x, one, none], axis=0), 3)
-    right = split(jnp.concatenate([-2.0 * y, one, norm_y, none], axis=0), 3)
+def matrix(ref, cell, height, tiles):
+    first = cell * tiles
+    return jnp.concatenate(
+        [ref[(first + t) * height : (first + t + 1) * height, :] for t in range(tiles)], axis=1
+    )
+
+
+def lay_out(x, f, first, feat, gram):
+    rows = x[0].shape[0]
+    norm = x[0] * x[0] + x[1] * x[1] + x[2] * x[2]
+    along = x[0] * f[0] + x[1] * f[1] + x[2] * f[2]
+    columns = list(f) + [x[k] * f[c] for k in range(3) for c in range(3)]
+    columns += [norm * f[c] + x[c] * along for c in range(3)]
+    for number, value in enumerate(columns):
+        feat[pl.ds(number, rows, stride=FEATURES), :] = value
+    scale = jnp.where(first, 1.0, -2.0)
+    terms = [x[c] * scale for c in range(3)]
+    terms += [jnp.where(first, norm, 1.0), jnp.where(first, 1.0, norm + eps_sq)]
+    for number, value in enumerate(terms):
+        gram[pl.ds(number, rows, stride=GRAM), :] = value
+    return norm
+
+
+def combine(sums, x, norm):
+    rows = norm.shape[0]
+    at = [sums[pl.ds(number, rows, stride=FEATURES), :] for number in range(15)]
+    force, second = at[0:3], at[12:15]
+    moment = [at[3 + 3 * k : 6 + 3 * k] for k in range(3)]
+    trace = moment[0][0] + moment[1][1] + moment[2][2]
+    along = x[0] * force[0] + x[1] * force[1] + x[2] * force[2] - trace
+    size = norm + 2.0 * eps_sq
+    out = []
+    for c in range(3):
+        mixed = x[0] * moment[0][c] + x[1] * moment[1][c] + x[2] * moment[2][c]
+        turned = x[0] * moment[c][0] + x[1] * moment[c][1] + x[2] * moment[c][2]
+        value = size * force[c] + second[c] - 2.0 * mixed - turned + x[c] * along
+        out.append(value * stokes_coef)
+    return out
+
+
+def gram_product(gram, tiles):
+    left = split(matrix(gram, 0, GRAM, tiles), 3)
+    right = split(matrix(gram, 1, GRAM, tiles), 3)
     order = ((0, 0), (0, 1), (1, 0), (0, 2), (1, 1), (2, 0))
-    return (
+    return dot(
         jnp.concatenate([left[p] for p, _ in order], axis=0).astype(bf16),
         jnp.concatenate([right[q] for _, q in order], axis=0).astype(bf16),
-    )
+        0,
+        0,
+    )
+
+
+def feature_rows(feat, cell, tiles):
+    parts = split(matrix(feat, cell, FEATURES, tiles), 3)
+    terms = jnp.concatenate([part.astype(bf16) for part in parts], axis=0)
+    return jnp.concatenate([terms, terms], axis=1)
 
 
 def dot(left, right, left_dim, right_dim):
@@ -85,23 +106,29 @@
     return high, low
 
 
-def pair_velocities(cells):
-    grams = [dot(*gram_factors(xa, xb), 0, 0) for xa, _, xb, _ in cells]
-    feats = [(features(xa, fa), features(xb, fb)) for xa, fa, xb, fb in cells]
+def pair_velocities(cells, first, feats, grams, totals):
+    tiles = cells[0][0][0].shape[0] // 2
+    n = len(cells)
+    norms = [lay_out(x, f, first, feats.at[i], grams.at[i]) for i, (x, f) in enumerate(cells)]
+    squares = [gram_product(grams.at[i], tiles) for i in range(n)]
+    rows = [[feature_rows(feats.at[i], cell, tiles) for cell in range(2)] for i in range(n)]
     results = []
     waiting = []
 
     def finish():
-        sums_a, sums_b, xa, xb = waiting.pop(0)
-        results.append((combine(fold(sums_a), xa), combine(fold(sums_b), xb)))
-
-    for gram, (feat_a, feat_b), (xa, _, xb, _) in zip(grams, feats, cells):
-        high, low = weights(gram)
-        rows = jnp.concatenate([high, low], axis=0)
-        columns = jnp.concatenate([high, low], axis=1)
-        sums_b = dot(jnp.concatenate([feat_a, feat_a], axis=1), rows, 1, 0)
-        sums_a = dot(jnp.concatenate([feat_b, feat_b], axis=1), columns, 1, 1)
-        waiting.append((sums_a, sums_b, xa, xb))
+        i, sums = waiting.pop(0)
+        for cell in range(2):
+            value = fold(sums[cell])
+            for t in range(tiles):
+                place = (cell * tiles + t) * FEATURES
+                totals[i, place : place + FEATURES, :] = value[:, t * LANES : (t + 1) * LANES]
+        results.append(combine(totals.at[i], cells[i][0], norms[i]))
+
+    for i in range(n):
+        high, low = weights(squares[i])
+        of_b = dot(rows[i][0], jnp.concatenate([high, low], axis=0), 1, 0)
+        of_a = dot(rows[i][1], jnp.concatenate([high, low], axis=1), 1, 1)
+        waiting.append((i, (of_a, of_b)))
         if len(waiting) > 1:
             finish()
     finish()
@@ -174,7 +201,9 @@
     n = len(kinds)
     messages, (pos, frc) = refs[:n], refs[n : n + 2]
     outs = refs[n + 2 + started :]
-    (acc, reply), (inbox, todo, middles) = outs[:2], outs[-3:]
+    (acc, reply), (inbox, feats, grams, totals, todo, middles) = outs[:2], outs[-6:]
+    feats[...] = jnp.zeros_like(feats)
+    grams[...] = jnp.zeros_like(grams)
     rows_in = share * 6 * tiles
     plane = cell_dev * tiles
     if not started:
@@ -202,38 +231,41 @@
                 number = number + jnp.where(b >= 0, 1, 0)
             first += 1
 
-    axis = lax.broadcasted_iota(jnp.int32, (3, 1), 0)
+    first = lax.broadcasted_iota(jnp.int32, (2 * tiles, LANES), 0) < tiles
 
     def load(i):
         base = todo[0, i] * (6 * tiles)
-        data = jnp.concatenate(
-            [inbox[pl.ds(base + t, 6, stride=tiles), :] for t in range(tiles)], axis=1
-        )
         start = row_base(todo[1, i], tiles)
-        xb, fb = (
-            jnp.concatenate(
-                [ref[pl.ds(start + 8 * t, 3, stride=plane), :] for t in range(tiles)], axis=1
+        values = []
+        for c in range(6):
+            ref = pos if c < 3 else frc
+            values.append(
+                jnp.concatenate(
+                    [
+                        inbox[pl.ds(base + c * tiles, tiles), :],
+                        ref[pl.ds(start + c % 3 * plane, tiles, stride=8), :],
+                    ],
+                    axis=0,
+                )
             )
-            for ref in (pos, frc)
-        )
-        xa = data[0:3] - jnp.where(axis == 0, middles[0, i], across_middle)
-        xb = xb - jnp.where(axis == 0, middles[1, i], across_middle)
-        return xa, data[3:6], xb, fb
-
-    def store(i, vel_a, vel_b):
+        x = [values[0] - jnp.where(first, middles[0, i], middles[1, i])]
+        x += [value - across_middle for value in values[1:3]]
+        return x, values[3:]
+
+    def store(i, velocity):
         base = todo[0, i] * (3 * tiles)
         start = row_base(todo[1, i], tiles)
-        parts = [slice(t * LANES, (t + 1) * LANES) for t in range(tiles)]
-        places = [pl.ds(start + 8 * t, 3, stride=plane) for t in range(tiles)]
-        totals = [acc[place, :] + vel_b[:, part] for place, part in zip(places, parts)]
-        for t in range(tiles):
-            acc[places[t], :] = totals[t]
-            reply[pl.ds(base + t, 3, stride=tiles), :] = vel_a[:, parts[t]]
+        places = [pl.ds(start + c * plane, tiles, stride=8) for c in range(3)]
+        added = [acc[places[c], :] + velocity[c][tiles:] for c in range(3)]
+        for c in range(3):
+            acc[places[c], :] = added[c]
+            reply[pl.ds(base + c * tiles, tiles), :] = velocity[c][:tiles]
 
     def several(numbers):
-        results = pair_velocities([load(i) for i in numbers])
+        cells = [load(i) for i in numbers]
+        results = pair_velocities(cells, first, feats, grams, totals)
         for i, result in zip(numbers, results):
-            store(i, *result)
+            store(i, result)
 
     def four(i, _):
         several([4 * i + j for j in range(4)])
@@ -340,6 +372,9 @@
             out_specs=[vmem] * (2 + marked),
             scratch_shapes=[
                 pltpu.VMEM((blocks * rows_in, LANES), f32),
+                pltpu.VMEM((4, 2 * tiles * FEATURES, LANES), f32),
+                pltpu.VMEM((4, 2 * tiles * GRAM, LANES), f32),
+                pltpu.VMEM((4, 2 * tiles * FEATURES, LANES), f32),
                 pltpu.SMEM((2, blocks * share + 1), jnp.int32),
                 pltpu.SMEM((2, blocks * share + 1), f32),
             ],
@@ -360,25 +395,19 @@
     out_1f = beyond(jnp.stack([value[1] for value in rest]), 1)
     out_2 = beyond(jnp.concatenate([own[2], core[2]] + [value[2:] for value in rest]), 2)
     acc, reply_m = pairs([(1, out_1n)] + [(0, got[turn][0:1]) for turn in far], [acc])
-    acc, reply_f, later = pairs([(1, out_1f), (2, out_2)], [acc], True)
+    acc, reply_f = pairs([(1, out_1f), (2, out_2)], [acc])
     reply_0n, reply_m, reply_f = (
         value.reshape(-1, rows_out, LANES) for value in (reply_0n, reply_m, reply_f)
     )
     cut = n_pairs - 2
-    back_1n = beyond(reply_m[:2] + later[None], 1)
-    back_2n = beyond(reply_f[cut : cut + 2], 2)
-    home = [
-        across(jnp.stack([reply_m[turn], reply_f[turn - 2], reply_f[cut + turn]]), turn)
-        for turn in far
-    ]
-    back_1f = beyond(jnp.stack([value[1] for value in home]), 1)
-    back_2f = beyond(jnp.stack([value[2] for value in home]), 2)
-    core = across(jnp.stack([reply_0n[1], back_1n[1], back_2n[1]]), 1)
-    mine = jnp.stack([reply_0n[0], back_1n[0], back_2n[0]])
-    replies = [mine, core, back_1f, back_2f] + home
-    where = [(0, 0), (1, 0)] + [(2 + turn, 0) for turn in far]
-    where += [(0, 1), (1, 1)] + [(2, turn - 2) for turn in far]
-    where += [(0, 2), (1, 2)] + [(3, turn - 2) for turn in far]
+    back_0 = jnp.concatenate([reply_0n, reply_m[2:]])
+    back_1 = beyond(jnp.concatenate([reply_m[:2], reply_f[:cut]]), 1)
+    back_2 = beyond(reply_f[cut:], 2)
+    replies = []
+    for turn in range(n_pairs):
+        value = jnp.stack([back_0[turn], back_1[turn], back_2[turn]])
+        replies.append(across(value, turn) if turn else value)
+    where = [(turn, kind) for kind in range(3) for turn in range(n_pairs)]
     velocity = pl.pallas_call(
         functools.partial(add_kernel, sizes, where),
         out_shape=total,

time: 54.7 us -> 52 us (0.951); the launches traced: 55.2 us -> 51.9 us
  waiting for transfers between devices: 14.2 us -> 7.99 us
  Pallas kernels: 19.9 us -> 23.5 us
  starting transfers between devices: 19.1 us -> 18.4 us
    ppermute x7 -> x5, waiting for transfers between devices: 9.79 us -> 2.59 us  [beyond(): return lax.ppermute(value, 'space', moves)]
    pallas_call x3, Pallas kernels: 15.5 us -> 19.1 us  [pairs(): pl.pallas_call(functools.partial(pair_kernel, sizes, kinds, len(before),...]
    ppermute x7 -> x5, starting transfers between devices: 15.7 us -> 12.6 us  [beyond(): return lax.ppermute(value, 'space', moves)]
    ppermute x6, starting transfers between devices: 3.36 us -> 5.8 us  [across(): return lax.ppermute(value, 'pairs', [(j, j ^ turn) for j in range(n_pairs)])]
    ppermute x6, waiting for transfers between devices: 4.39 us -> 5.4 us  [across(): return lax.ppermute(value, 'pairs', [(j, j ^ turn) for j in range(n_pairs)])]
  transfers between devices with their start and end apart: 13 -> 11, of which waited for: 9 -> 5; matrix products, arithmetic and copies ran while one was open for 2% -> 2% of each run, Pallas kernels for 12% -> 22%
where the time goes in v6:
time: 52 us; the launch traced here: 51.9 us
  Pallas kernels  23.5 us (45%)
  starting transfers between devices  18.4 us (35%)
  waiting for transfers between devices  7.99 us (15%)
  local copies, waits for them, and re-layouts  1.03 us (2%)
  between operations  0.84 us (2%)
    pallas_call x3, Pallas kernels, pairs(): pl.pallas_call(functools.partial(pair_kernel, sizes, kinds, len(before),...  19.1 us
    ppermute x5, starting transfers between devices, beyond(): return lax.ppermute(value, 'space', moves)  12.6 us
    ppermute x6, starting transfers between devices, across(): return lax.ppermute(value, 'pairs', [(j, j ^ turn) for j in range(n_pairs)])  5.8 us
    ppermute x6, waiting for transfers between devices, across(): return lax.ppermute(value, 'pairs', [(j, j ^ turn) for j in range(n_pairs)])  5.4 us
    pallas_call x1, Pallas kernels, body(): pl.pallas_call(functools.partial(pack_kernel, sizes), out_shape=[message]...  3.25 us
    ppermute x5, waiting for transfers between devices, beyond(): return lax.ppermute(value, 'space', moves)  2.59 us
    pallas_call x1, Pallas kernels, body(): pl.pallas_call(functools.partial(add_kernel, sizes, where), out_shape=tot...  1.17 us
  transfers between devices with their start and end apart: 11, of which 5 were waited for; matrix products, arithmetic and copies ran while one was open for 2% of the time, Pallas kernels for 22%

profile of v6, /device:TPU:0, one launch (start us, length us, event | category | flops | bytes accessed | tf_op | source)
XLA Modules:
  0.0 51.9 jit_solution(14192657826979658247)
XLA Ops:
  0.7 3.3 %pack.1 = (f32[3,104,128]{2,1,0:T(8,128)}, f32[3,104,128]{2,1,0:T(8,128)}, f32[3,104,128]{2,1,0:T(8,128)}, f32[3,104,128]{2,1,0:T(8,128)}) custom-call(s32[2,48]{1,0:T(2,128)} %cells.1, s32[1]{0:T(128)S(6)} %copy.9.count, f32[768,128]{1,0:T(8,128)} %bitcast.33, f32[768,128]{1,0:T(8,128)} %bitcast.37), custom_call_target="tpu_custom_call" | custom-call | tf_op jit(solution)/shard_map/pack/pallas_call | solution.py:345
  3.9 3.0 %collective-permute-start = (f32[3,104,128]{2,1,0:T(8,128)}, f32[3,104,128]{2,1,0:T(8,128)S(1)}, u32[]{:S(2)}, u32[]{:S(2)}) collective-permute-start(f32[3,104,128]{2,1,0:T(8,128)} %get-tuple-element.16), channel_id=1, source_target_pairs={{0,2},{1,3},{2,0},{3,1},{4,6},{5,7},{6,4},{7,5},{8,10},{9,11},{10,... | collective-permute-start | bytes 479240 | tf_op jit(solution)/shard_map/ppermute | solution.py:339
  6.9 0.0 collective-permute-start.1
  6.9 0.2 collective-permute-start.2
  7.1 0.0 copy-start
  7.1 0.0 copy-start.1
  7.1 0.9 %fusion = (f32[1,104,128]{2,1,0:T(8,128)S(1)}, f32[1,104,128]{2,1,0:T(8,128)S(1)}, f32[1,104,128]{2,1,0:T(8,128)S(1)}) fusion(f32[3,104,128]{2,1,0:T(8,128)} %get-tuple-element.17), kind=kLoop, calls=%fused_computation.14 | loop fusion | bytes 319488 | tf_op jit(solution)/shard_map/slice | solution.py:390
  8.1 0.4 collective-permute-done.1
  8.6 1.6 %collective-permute-start.5 = (f32[2,104,128]{2,1,0:T(8,128)S(1)}, f32[2,104,128]{2,1,0:T(8,128)S(1)}, u32[]{:S(2)}, u32[]{:S(2)}) collective-permute-start(f32[2,104,128]{2,1,0:T(8,128)S(1)} %pad_maximum_fusion.2), channel_id=1, source_target_pairs={{0,4},{4,0},{8,12},{12,8},{16,20},{20,16},{24,28},{28,24},{1,5},{5... | collective-permute-start | bytes 319496 | tf_op jit(solution)/shard_map/ppermute | solution.py:343
  10.2 0.0 copy-done
  10.2 0.0 copy-done.1
  10.2 3.0 %pairs.3 = (f32[768,128]{1,0:T(8,128)S(1)}, f32[96,128]{1,0:T(8,128)S(1)}, f32[1,128]{1,0:T(1,128)S(1)}) custom-call(f32[1,104,128]{2,1,0:T(8,128)S(1)} %get-tuple-element.29.refs_0_.mine, f32[1,104,128]{2,1,0:T(8,128)S(1)} %get-tuple-element.32.refs_1_, f32[768,128]{1,0:T(8,128)S(1)} %bitcast.34, f32[768,128]{1,0:T(8,128)S(1)} %bitcast.38), custom_call_target="tpu_custom_call" | custom-call | flops 2000000000 | bytes 2000000 | tf_op jit(solution)/shard_map/pairs/pallas_call | solution.py:367
  13.2 0.0 collective-permute-done
  13.2 0.9 %collective-permute-done.2 = f32[3,104,128]{2,1,0:T(8,128)S(1)} collective-permute-done((f32[3,104,128]{2,1,0:T(8,128)}, f32[3,104,128]{2,1,0:T(8,128)S(1)}, u32[]{:S(2)}, u32[]{:S(2)}) %collective-permute-start.2) | collective-permute-done | bytes 159776 | tf_op jit(solution)/shard_map/ppermute | solution.py:339
  14.1 1.6 %collective-permute-start.3 = (f32[2,104,128]{2,1,0:T(8,128)S(1)}, f32[2,104,128]{2,1,0:T(8,128)S(1)}, u32[]{:S(2)}, u32[]{:S(2)}) collective-permute-start(f32[2,104,128]{2,1,0:T(8,128)S(1)} %pad_maximum_fusion.1), channel_id=1, source_target_pairs={{0,4},{4,0},{8,12},{12,8},{16,20},{20,16},{24,28},{28,24},{1,5},{5... | collective-permute-start | bytes 319496 | tf_op jit(solution)/shard_map/ppermute | solution.py:343
  15.7 3.6 %collective-permute-start.4 = (f32[4,104,128]{2,1,0:T(8,128)S(1)}, f32[4,104,128]{2,1,0:T(8,128)S(1)}, u32[]{:S(2)}, u32[]{:S(2)}) collective-permute-start(f32[4,104,128]{2,1,0:T(8,128)S(1)} %pad_maximum_fusion), channel_id=1, source_target_pairs={{0,28},{4,8},{8,4},{12,16},{16,12},{20,24},{24,20},{28,0},{1,29},{... | collective-permute-start | bytes 638984 | tf_op jit(solution)/shard_map/ppermute | solution.py:343
  19.3 0.0 collective-permute-done.5.refs_0_
  19.3 8.6 %pairs.4 = (f32[768,128]{1,0:T(8,128)S(1)}, f32[192,128]{1,0:T(8,128)S(1)}) custom-call(f32[2,104,128]{2,1,0:T(8,128)S(1)} %collective-permute-done.5.refs_0_, f32[1,104,128]{2,1,0:T(8,128)S(1)} %slice.147.refs_1_, f32[1,104,128]{2,1,0:T(8,128)S(1)} %slice.148.refs_2_, f32[768,128]{1,0:T(8,128)S(1)} %bitcast.35, ...), custom_call_target="tpu_custom_call", output_to_operand_aliasing={{0}: (5, {})} | custom-call | flops 4000000000 | bytes 2000000 | tf_op jit(solution)/shard_map/pairs/pallas_call | solution.py:367
  28.0 0.0 collective-permute-done.3.refs_0_
  28.0 0.0 collective-permute-done.4.refs_1_
  28.0 7.5 %pairs.5 = (f32[768,128]{1,0:T(8,128)S(1)}, f32[288,128]{1,0:T(8,128)S(1)}) custom-call(f32[2,104,128]{2,1,0:T(8,128)S(1)} %collective-permute-done.3.refs_0_, f32[4,104,128]{2,1,0:T(8,128)S(1)} %collective-permute-done.4.refs_1_, f32[768,128]{1,0:T(8,128)S(1)} %bitcast.36, f32[768,128]{1,0:T(8,128)S(1)} %bitcast.40, ...), custom_call_target="tpu_custom_call", output_to_operand_aliasing={{0}: (4, {})} | custom-call | flops 6000000000 | bytes 2000000 | tf_op jit(solution)/shard_map/pairs/pallas_call | solution.py:367
  35.6 0.1 collective-permute-start.6
  35.7 5.7 %collective-permute-start.7 = (f32[4,48,128]{2,1,0:T(8,128)S(1)}, f32[4,48,128]{2,1,0:T(8,128)S(1)}, u32[]{:S(2)}, u32[]{:S(2)}) collective-permute-start(f32[4,48,128]{2,1,0:T(8,128)S(1)} %bitcast.44), channel_id=1, source_target_pairs={{0,28},{4,8},{8,4},{12,16},{16,12},{20,24},{24,20},{28,0},{1,29},{... | collective-permute-start | bytes 294920 | tf_op jit(solution)/shard_map/ppermute | solution.py:343
  41.4 0.0 collective-permute-done.6
  41.4 2.6 %collective-permute-done.7 = f32[4,48,128]{2,1,0:T(8,128)S(1)} collective-permute-done((f32[4,48,128]{2,1,0:T(8,128)S(1)}, f32[4,48,128]{2,1,0:T(8,128)S(1)}, u32[]{:S(2)}, u32[]{:S(2)}) %collective-permute-start.7) | collective-permute-done | bytes 98336 | tf_op jit(solution)/shard_map/ppermute | solution.py:343
  44.0 0.1 collective-permute-start.8
  44.1 2.4 %collective-permute-start.9 = (f32[3,48,128]{2,1,0:T(8,128)S(1)}, f32[3,48,128]{2,1,0:T(8,128)S(1)}, u32[]{:S(2)}, u32[]{:S(2)}) collective-permute-start(f32[3,48,128]{2,1,0:T(8,128)S(1)} %pad_maximum_fusion.6), channel_id=1, source_target_pairs={{0,2},{1,3},{2,0},{3,1},{4,6},{5,7},{6,4},{7,5},{8,10},{9,11},{10,... | collective-permute-start | bytes 221192 | tf_op jit(solution)/shard_map/ppermute | solution.py:339
  46.5 0.1 collective-permute-start.10
  46.6 0.0 collective-permute-done.8.refs_1_
  46.6 2.7 %collective-permute-done.9.refs_2_ = f32[3,48,128]{2,1,0:T(8,128)S(1)} collective-permute-done((f32[3,48,128]{2,1,0:T(8,128)S(1)}, f32[3,48,128]{2,1,0:T(8,128)S(1)}, u32[]{:S(2)}, u32[]{:S(2)}) %collective-permute-start.9) | collective-permute-done | bytes 73760 | tf_op jit(solution)/shard_map/ppermute | solution.py:339
  49.4 1.4 %collective-permute-done.10.refs_3_ = f32[3,48,128]{2,1,0:T(8,128)S(1)} collective-permute-done((f32[3,48,128]{2,1,0:T(8,128)S(1)}, f32[3,48,128]{2,1,0:T(8,128)S(1)}, u32[]{:S(2)}, u32[]{:S(2)}) %collective-permute-start.10) | collective-permute-done | bytes 73760 | tf_op jit(solution)/shard_map/ppermute | solution.py:339
  50.7 1.2 %add.25 = f32[768,128]{1,0:T(8,128)} custom-call(f32[768,128]{1,0:T(8,128)S(1)} %get-tuple-element.23.acc, f32[1,104,128]{2,1,0:T(8,128)S(1)} %get-tuple-element.29.refs_0_.mine, f32[3,48,128]{2,1,0:T(8,128)S(1)} %pad_maximum_fusion.4.refs_0_, f32[3,48,128]{2,1,0:T(8,128)S(1)} %collective-permute-done.8.refs_1_, ...), custom_call_target="tpu_custom_call" | custom-call | tf_op jit(solution)/shard_map/add/pallas_call | solution.py:411
  (20 shorter events, 0.2 us)
Async XLA Ops:
  3.9 9.2 %collective-permute-start = (f32[3,104,128]{2,1,0:T(8,128)}, f32[3,104,128]{2,1,0:T(8,128)S(1)}, u32[]{:S(2)}, u32[]{:S(2)}) collective-permute-start(f32[3,104,128]{2,1,0:T(8,128)} %get-tuple-element.16), channel_id=1, source_target_pairs={{0,2},{1,3},{2,0},{3,1},{4,6},{5,7},{6,4},{7,5},{8,10},{9,11},{10,... | collective-permute-start | bytes 479240 | tf_op jit(solution)/shard_map/ppermute | solution.py:339
  6.9 1.6 %collective-permute-start.1 = (f32[3,104,128]{2,1,0:T(8,128)}, f32[3,104,128]{2,1,0:T(8,128)S(1)}, u32[]{:S(2)}, u32[]{:S(2)}) collective-permute-start(f32[3,104,128]{2,1,0:T(8,128)} %get-tuple-element.18), channel_id=1, source_target_pairs={{0,1},{1,0},{2,3},{3,2},{4,5},{5,4},{6,7},{7,6},{8,9},{9,8},{10,11... | collective-permute-start | bytes 479240 | tf_op jit(solution)/shard_map/ppermute | solution.py:339
  6.9 7.1 %collective-permute-start.2 = (f32[3,104,128]{2,1,0:T(8,128)}, f32[3,104,128]{2,1,0:T(8,128)S(1)}, u32[]{:S(2)}, u32[]{:S(2)}) collective-permute-start(f32[3,104,128]{2,1,0:T(8,128)} %get-tuple-element.20), channel_id=1, source_target_pairs={{0,3},{1,2},{2,1},{3,0},{4,7},{5,6},{6,5},{7,4},{8,11},{9,10},{10,... | collective-permute-start | bytes 479240 | tf_op jit(solution)/shard_map/ppermute | solution.py:339
  7.1 3.0 %copy-start = (f32[64,3,512]{2,0,1:T(8,128)S(1)}, f32[64,3,512]{2,0,1:T(8,128)}, u32[]{:S(2)}) copy-start(f32[64,3,512]{2,0,1:T(8,128)} %param.4) | copy-start | bytes 1179652
  7.1 3.0 %copy-start.1 = (f32[64,3,512]{2,0,1:T(8,128)S(1)}, f32[64,3,512]{2,0,1:T(8,128)}, u32[]{:S(2)}) copy-start(f32[64,3,512]{2,0,1:T(8,128)} %param.5) | copy-start | bytes 1179652
  8.6 10.8 %collective-permute-start.5 = (f32[2,104,128]{2,1,0:T(8,128)S(1)}, f32[2,104,128]{2,1,0:T(8,128)S(1)}, u32[]{:S(2)}, u32[]{:S(2)}) collective-permute-start(f32[2,104,128]{2,1,0:T(8,128)S(1)} %pad_maximum_fusion.2), channel_id=1, source_target_pairs={{0,4},{4,0},{8,12},{12,8},{16,20},{20,16},{24,28},{28,24},{1,5},{5... | collective-permute-start | bytes 319496 | tf_op jit(solution)/shard_map/ppermute | solution.py:343
  14.1 13.9 %collective-permute-start.3 = (f32[2,104,128]{2,1,0:T(8,128)S(1)}, f32[2,104,128]{2,1,0:T(8,128)S(1)}, u32[]{:S(2)}, u32[]{:S(2)}) collective-permute-start(f32[2,104,128]{2,1,0:T(8,128)S(1)} %pad_maximum_fusion.1), channel_id=1, source_target_pairs={{0,4},{4,0},{8,12},{12,8},{16,20},{20,16},{24,28},{28,24},{1,5},{5... | collective-permute-start | bytes 319496 | tf_op jit(solution)/shard_map/ppermute | solution.py:343
  15.7 12.3 %collective-permute-start.4 = (f32[4,104,128]{2,1,0:T(8,128)S(1)}, f32[4,104,128]{2,1,0:T(8,128)S(1)}, u32[]{:S(2)}, u32[]{:S(2)}) collective-permute-start(f32[4,104,128]{2,1,0:T(8,128)S(1)} %pad_maximum_fusion), channel_id=1, source_target_pairs={{0,28},{4,8},{8,4},{12,16},{16,12},{20,24},{24,20},{28,0},{1,29},{... | collective-permute-start | bytes 638984 | tf_op jit(solution)/shard_map/ppermute | solution.py:343
  35.6 5.8 %collective-permute-start.6 = (f32[4,48,128]{2,1,0:T(8,128)S(1)}, f32[4,48,128]{2,1,0:T(8,128)S(1)}, u32[]{:S(2)}, u32[]{:S(2)}) collective-permute-start(f32[4,48,128]{2,1,0:T(8,128)S(1)} %pad_maximum_fusion.3), channel_id=1, source_target_pairs={{0,4},{4,0},{8,12},{12,8},{16,20},{20,16},{24,28},{28,24},{1,5},{5... | collective-permute-start | bytes 294920 | tf_op jit(solution)/shard_map/ppermute | solution.py:343
  35.7 8.3 %collective-permute-start.7 = (f32[4,48,128]{2,1,0:T(8,128)S(1)}, f32[4,48,128]{2,1,0:T(8,128)S(1)}, u32[]{:S(2)}, u32[]{:S(2)}) collective-permute-start(f32[4,48,128]{2,1,0:T(8,128)S(1)} %bitcast.44), channel_id=1, source_target_pairs={{0,28},{4,8},{8,4},{12,16},{16,12},{20,24},{24,20},{28,0},{1,29},{... | collective-permute-start | bytes 294920 | tf_op jit(solution)/shard_map/ppermute | solution.py:343
  44.0 2.6 %collective-permute-start.8 = (f32[3,48,128]{2,1,0:T(8,128)S(1)}, f32[3,48,128]{2,1,0:T(8,128)S(1)}, u32[]{:S(2)}, u32[]{:S(2)}) collective-permute-start(f32[3,48,128]{2,1,0:T(8,128)S(1)} %pad_maximum_fusion.5), channel_id=1, source_target_pairs={{0,1},{1,0},{2,3},{3,2},{4,5},{5,4},{6,7},{7,6},{8,9},{9,8},{10,11... | collective-permute-start | bytes 221192 | tf_op jit(solution)/shard_map/ppermute | solution.py:339
  44.1 5.2 %collective-permute-start.9 = (f32[3,48,128]{2,1,0:T(8,128)S(1)}, f32[3,48,128]{2,1,0:T(8,128)S(1)}, u32[]{:S(2)}, u32[]{:S(2)}) collective-permute-start(f32[3,48,128]{2,1,0:T(8,128)S(1)} %pad_maximum_fusion.6), channel_id=1, source_target_pairs={{0,2},{1,3},{2,0},{3,1},{4,6},{5,7},{6,4},{7,5},{8,10},{9,11},{10,... | collective-permute-start | bytes 221192 | tf_op jit(solution)/shard_map/ppermute | solution.py:339
  46.5 4.2 %collective-permute-start.10 = (f32[3,48,128]{2,1,0:T(8,128)S(1)}, f32[3,48,128]{2,1,0:T(8,128)S(1)}, u32[]{:S(2)}, u32[]{:S(2)}) collective-permute-start(f32[3,48,128]{2,1,0:T(8,128)S(1)} %pad_maximum_fusion.7), channel_id=1, source_target_pairs={{0,3},{1,2},{2,1},{3,0},{4,7},{5,6},{6,5},{7,4},{8,11},{9,10},{10,... | collective-permute-start | bytes 221192 | tf_op jit(solution)/shard_map/ppermute | solution.py:339

commit v7 on v6

--- a/solution.py
+++ b/solution.py
@@ -84,8 +84,7 @@
 
 def feature_rows(feat, cell, tiles):
     parts = split(matrix(feat, cell, FEATURES, tiles), 3)
-    terms = jnp.concatenate([part.astype(bf16) for part in parts], axis=0)
-    return jnp.concatenate([terms, terms], axis=1)
+    return jnp.concatenate([part.astype(bf16) for part in parts], axis=0)
 
 
 def dot(left, right, left_dim, right_dim):
@@ -94,8 +93,10 @@
     )
 
 
-def fold(sums):
-    return sums[0:FEATURES] + sums[FEATURES : 2 * FEATURES] + sums[2 * FEATURES :]
+def fold(high, low):
+    third = high[2 * FEATURES :]
+    both = high[: 2 * FEATURES] + low
+    return both[:FEATURES] + both[FEATURES:] + third
 
 
 def weights(dist_sq):
@@ -118,7 +119,7 @@
     def finish():
         i, sums = waiting.pop(0)
         for cell in range(2):
-            value = fold(sums[cell])
+            value = fold(*sums[cell])
             for t in range(tiles):
                 place = (cell * tiles + t) * FEATURES
                 totals[i, place : place + FEATURES, :] = value[:, t * LANES : (t + 1) * LANES]
@@ -126,8 +127,8 @@
 
     for i in range(n):
         high, low = weights(squares[i])
-        of_b = dot(rows[i][0], jnp.concatenate([high, low], axis=0), 1, 0)
-        of_a = dot(rows[i][1], jnp.concatenate([high, low], axis=1), 1, 1)
+        of_b = dot(rows[i][0], high, 1, 0), dot(rows[i][0][: 2 * FEATURES], low, 1, 0)
+        of_a = dot(rows[i][1], high, 1, 1), dot(rows[i][1][: 2 * FEATURES], low, 1, 1)
         waiting.append((i, (of_a, of_b)))
         if len(waiting) > 1:
             finish()
@@ -395,14 +396,14 @@
     out_1f = beyond(jnp.stack([value[1] for value in rest]), 1)
     out_2 = beyond(jnp.concatenate([own[2], core[2]] + [value[2:] for value in rest]), 2)
     acc, reply_m = pairs([(1, out_1n)] + [(0, got[turn][0:1]) for turn in far], [acc])
-    acc, reply_f = pairs([(1, out_1f), (2, out_2)], [acc])
-    reply_0n, reply_m, reply_f = (
-        value.reshape(-1, rows_out, LANES) for value in (reply_0n, reply_m, reply_f)
-    )
-    cut = n_pairs - 2
+    acc, reply_1f = pairs([(1, out_1f)], [acc])
+    acc, reply_2, later = pairs([(2, out_2)], [acc], True)
+    reply_0n, reply_m, reply_1f, reply_2 = (
+        value.reshape(-1, rows_out, LANES) for value in (reply_0n, reply_m, reply_1f, reply_2)
+    )
     back_0 = jnp.concatenate([reply_0n, reply_m[2:]])
-    back_1 = beyond(jnp.concatenate([reply_m[:2], reply_f[:cut]]), 1)
-    back_2 = beyond(reply_f[cut:], 2)
+    back_1 = beyond(jnp.concatenate([reply_m[:2], reply_1f]) + later[None], 1)
+    back_2 = beyond(reply_2, 2)
     replies = []
     for turn in range(n_pairs):
         value = jnp.stack([back_0[turn], back_1[turn], back_2[turn]])

time: 52 us -> 52.4 us (level)
  waiting for transfers between devices: 7.99 us -> 13.8 us
  starting transfers between devices: 18.4 us -> 12.6 us
    ppermute x5, starting transfers between devices: 12.6 us -> 7.53 us  [beyond(): return lax.ppermute(value, 'space', moves)]
    ppermute x5, waiting for transfers between devices: 2.59 us -> 7.01 us  [beyond(): return lax.ppermute(value, 'space', moves)]
    ppermute x6, waiting for transfers between devices: 5.4 us -> 6.8 us  [across(): return lax.ppermute(value, 'pairs', [(j, j ^ turn) for j in range(n_pairs)])]
    ppermute x6, starting transfers between devices: 5.8 us -> 5.08 us  [across(): return lax.ppermute(value, 'pairs', [(j, j ^ turn) for j in range(n_pairs)])]
    pallas_call x3 -> x4, Pallas kernels: 19.1 us -> 19.2 us  [pairs(): pl.pallas_call(functools.partial(pair_kernel, sizes, kinds, len(before),...]
  transfers between devices with their start and end apart: 11 -> 11, of which waited for: 5 -> 5; matrix products, arithmetic and copies ran while one was open for 2% -> 2% of each run, Pallas kernels for 22% -> 27%
where the time goes in v7:
time: 52.4 us; the launch traced here: 52 us
  Pallas kernels  23.6 us (45%)
  waiting for transfers between devices  13.8 us (26%)
  starting transfers between devices  12.6 us (24%)
  local copies, waits for them, and re-layouts  1.02 us (2%)
  between operations  0.84 us (2%)
    pallas_call x4, Pallas kernels, pairs(): pl.pallas_call(functools.partial(pair_kernel, sizes, kinds, len(before),...  19.2 us
    ppermute x5, starting transfers between devices, beyond(): return lax.ppermute(value, 'space', moves)  7.53 us
    ppermute x5, waiting for transfers between devices, beyond(): return lax.ppermute(value, 'space', moves)  7.01 us
    ppermute x6, waiting for transfers between devices, across(): return lax.ppermute(value, 'pairs', [(j, j ^ turn) for j in range(n_pairs)])  6.8 us
    ppermute x6, starting transfers between devices, across(): return lax.ppermute(value, 'pairs', [(j, j ^ turn) for j in range(n_pairs)])  5.08 us
    pallas_call x1, Pallas kernels, body(): pl.pallas_call(functools.partial(pack_kernel, sizes), out_shape=[message]...  3.25 us
    pallas_call x1, Pallas kernels, body(): pl.pallas_call(functools.partial(add_kernel, sizes, where), out_shape=tot...  1.16 us
  transfers between devices with their start and end apart: 11, of which 5 were waited for; matrix products, arithmetic and copies ran while one was open for 2% of the time, Pallas kernels for 27%

profile of v7, /device:TPU:0, one launch (start us, length us, event | category | flops | bytes accessed | tf_op | source)
XLA Modules:
  0.0 52.0 jit_solution(13417855112586961504)
XLA Ops:
  0.7 3.3 %pack.1 = (f32[3,104,128]{2,1,0:T(8,128)}, f32[3,104,128]{2,1,0:T(8,128)}, f32[3,104,128]{2,1,0:T(8,128)}, f32[3,104,128]{2,1,0:T(8,128)}) custom-call(s32[2,48]{1,0:T(2,128)} %cells.1, s32[1]{0:T(128)S(6)} %copy.11.count, f32[768,128]{1,0:T(8,128)} %bitcast.34, f32[768,128]{1,0:T(8,128)} %bitcast.39), custom_call_target="tpu_custom_call" | custom-call | tf_op jit(solution)/shard_map/pack/pallas_call | solution.py:346
  3.9 0.5 collective-permute-start
  4.4 2.6 %collective-permute-start.1 = (f32[3,104,128]{2,1,0:T(8,128)}, f32[3,104,128]{2,1,0:T(8,128)S(1)}, u32[]{:S(2)}, u32[]{:S(2)}) collective-permute-start(f32[3,104,128]{2,1,0:T(8,128)} %get-tuple-element.21), channel_id=1, source_target_pairs={{0,2},{1,3},{2,0},{3,1},{4,6},{5,7},{6,4},{7,5},{8,10},{9,11},{10,... | collective-permute-start | bytes 479240 | tf_op jit(solution)/shard_map/ppermute | solution.py:340
  7.0 0.1 collective-permute-start.2
  7.1 0.0 copy-start
  7.1 0.9 %fusion = (f32[1,104,128]{2,1,0:T(8,128)S(1)}, f32[1,104,128]{2,1,0:T(8,128)S(1)}, f32[1,104,128]{2,1,0:T(8,128)S(1)}) fusion(f32[3,104,128]{2,1,0:T(8,128)} %get-tuple-element.19), kind=kLoop, calls=%fused_computation.14 | loop fusion | bytes 319488 | tf_op jit(solution)/shard_map/slice | solution.py:391
  8.0 0.0 collective-permute-done
  8.1 1.8 %collective-permute-start.5 = (f32[2,104,128]{2,1,0:T(8,128)S(1)}, f32[2,104,128]{2,1,0:T(8,128)S(1)}, u32[]{:S(2)}, u32[]{:S(2)}) collective-permute-start(f32[2,104,128]{2,1,0:T(8,128)S(1)} %pad_maximum_fusion.2), channel_id=1, source_target_pairs={{0,4},{4,0},{8,12},{12,8},{16,20},{20,16},{24,28},{28,24},{1,5},{5... | collective-permute-start | bytes 319496 | tf_op jit(solution)/shard_map/ppermute | solution.py:344
  9.9 0.0 copy-done
  9.9 0.0 copy-done.1
  9.9 2.5 %pairs.4 = (f32[768,128]{1,0:T(8,128)S(1)}, f32[96,128]{1,0:T(8,128)S(1)}, f32[1,128]{1,0:T(1,128)S(1)}) custom-call(f32[1,104,128]{2,1,0:T(8,128)S(1)} %get-tuple-element.34.refs_0_.mine, f32[1,104,128]{2,1,0:T(8,128)S(1)} %get-tuple-element.37.refs_1_, f32[768,128]{1,0:T(8,128)S(1)} %bitcast.35, f32[768,128]{1,0:T(8,128)S(1)} %bitcast.40), custom_call_target="tpu_custom_call" | custom-call | flops 2000000000 | bytes 2000000 | tf_op jit(solution)/shard_map/pairs/pallas_call | solution.py:368
  12.4 0.0 collective-permute-done.1
  12.5 2.6 %collective-permute-done.2 = f32[3,104,128]{2,1,0:T(8,128)S(1)} collective-permute-done((f32[3,104,128]{2,1,0:T(8,128)}, f32[3,104,128]{2,1,0:T(8,128)S(1)}, u32[]{:S(2)}, u32[]{:S(2)}) %collective-permute-start.2) | collective-permute-done | bytes 159776 | tf_op jit(solution)/shard_map/ppermute | solution.py:340
  15.1 1.7 %collective-permute-start.4 = (f32[2,104,128]{2,1,0:T(8,128)S(1)}, f32[2,104,128]{2,1,0:T(8,128)S(1)}, u32[]{:S(2)}, u32[]{:S(2)}) collective-permute-start(f32[2,104,128]{2,1,0:T(8,128)S(1)} %pad_maximum_fusion.1), channel_id=1, source_target_pairs={{0,4},{4,0},{8,12},{12,8},{16,20},{20,16},{24,28},{28,24},{1,5},{5... | collective-permute-start | bytes 319496 | tf_op jit(solution)/shard_map/ppermute | solution.py:344
  16.8 3.6 %collective-permute-start.3 = (f32[4,104,128]{2,1,0:T(8,128)S(1)}, f32[4,104,128]{2,1,0:T(8,128)S(1)}, u32[]{:S(2)}, u32[]{:S(2)}) collective-permute-start(f32[4,104,128]{2,1,0:T(8,128)S(1)} %pad_maximum_fusion), channel_id=1, source_target_pairs={{0,28},{4,8},{8,4},{12,16},{16,12},{20,24},{24,20},{28,0},{1,29},{... | collective-permute-start | bytes 638984 | tf_op jit(solution)/shard_map/ppermute | solution.py:344
  20.4 0.0 collective-permute-done.5.refs_0_
  20.5 5.8 %pairs.5 = (f32[768,128]{1,0:T(8,128)S(1)}, f32[192,128]{1,0:T(8,128)S(1)}) custom-call(f32[2,104,128]{2,1,0:T(8,128)S(1)} %collective-permute-done.5.refs_0_, f32[1,104,128]{2,1,0:T(8,128)S(1)} %slice.131.refs_1_, f32[1,104,128]{2,1,0:T(8,128)S(1)} %slice.132.refs_2_, f32[768,128]{1,0:T(8,128)S(1)} %bitcast.36, ...), custom_call_target="tpu_custom_call", output_to_operand_aliasing={{0}: (5, {})} | custom-call | flops 4000000000 | bytes 2000000 | tf_op jit(solution)/shard_map/pairs/pallas_call | solution.py:368
  26.3 0.0 collective-permute-done.4.refs_0_
  26.3 5.5 %pairs.6 = (f32[768,128]{1,0:T(8,128)S(1)}, f32[96,128]{1,0:T(8,128)S(1)}) custom-call(f32[2,104,128]{2,1,0:T(8,128)S(1)} %collective-permute-done.4.refs_0_, f32[768,128]{1,0:T(8,128)S(1)} %bitcast.37, f32[768,128]{1,0:T(8,128)S(1)} %bitcast.42, f32[768,128]{1,0:T(8,128)S(1)} %get-tuple-element.25.refs_3_), custom_call_target="tpu_custom_call", output_to_operand_aliasing={{0}: (3, {})} | custom-call | flops 2000000000 | bytes 2000000 | tf_op jit(solution)/shard_map/pairs/pallas_call | solution.py:368
  31.8 0.0 collective-permute-done.3.refs_0_
  31.8 5.4 %pairs.7 = (f32[768,128]{1,0:T(8,128)S(1)}, f32[192,128]{1,0:T(8,128)S(1)}, f32[1,128]{1,0:T(1,128)S(1)}) custom-call(f32[4,104,128]{2,1,0:T(8,128)S(1)} %collective-permute-done.3.refs_0_, f32[768,128]{1,0:T(8,128)S(1)} %bitcast.38, f32[768,128]{1,0:T(8,128)S(1)} %bitcast.43, f32[768,128]{1,0:T(8,128)S(1)} %get-tuple-element.26.refs_3_), custom_call_target="tpu_custom_call", output_to_operand_aliasing={{0}: (3, {})} | custom-call | flops 4000000000 | bytes 2000000 | tf_op jit(solution)/shard_map/pairs/pallas_call | solution.py:368
  37.2 0.1 collective-permute-start.6
  37.3 0.4 collective-permute-start.7
  37.7 5.3 %collective-permute-done.6 = f32[4,48,128]{2,1,0:T(8,128)S(1)} collective-permute-done((f32[4,48,128]{2,1,0:T(8,128)S(1)}, f32[4,48,128]{2,1,0:T(8,128)S(1)}, u32[]{:S(2)}, u32[]{:S(2)}) %collective-permute-start.6) | collective-permute-done | bytes 98336 | tf_op jit(solution)/shard_map/ppermute | solution.py:344
  43.0 1.7 %collective-permute-done.7 = f32[4,48,128]{2,1,0:T(8,128)S(1)} collective-permute-done((f32[4,48,128]{2,1,0:T(8,128)S(1)}, f32[4,48,128]{2,1,0:T(8,128)S(1)}, u32[]{:S(2)}, u32[]{:S(2)}) %collective-permute-start.7) | collective-permute-done | bytes 98336 | tf_op jit(solution)/shard_map/ppermute | solution.py:344
  44.7 0.1 collective-permute-start.8
  44.8 1.6 %collective-permute-start.9 = (f32[3,48,128]{2,1,0:T(8,128)S(1)}, f32[3,48,128]{2,1,0:T(8,128)S(1)}, u32[]{:S(2)}, u32[]{:S(2)}) collective-permute-start(f32[3,48,128]{2,1,0:T(8,128)S(1)} %pad_maximum_fusion.5), channel_id=1, source_target_pairs={{0,2},{1,3},{2,0},{3,1},{4,6},{5,7},{6,4},{7,5},{8,10},{9,11},{10,... | collective-permute-start | bytes 221192 | tf_op jit(solution)/shard_map/ppermute | solution.py:340
  46.4 0.3 collective-permute-start.10
  46.7 0.0 collective-permute-done.8.refs_1_
  46.7 2.9 %collective-permute-done.9.refs_2_ = f32[3,48,128]{2,1,0:T(8,128)S(1)} collective-permute-done((f32[3,48,128]{2,1,0:T(8,128)S(1)}, f32[3,48,128]{2,1,0:T(8,128)S(1)}, u32[]{:S(2)}, u32[]{:S(2)}) %collective-permute-start.9) | collective-permute-done | bytes 73760 | tf_op jit(solution)/shard_map/ppermute | solution.py:340
  49.6 1.2 %collective-permute-done.10.refs_3_ = f32[3,48,128]{2,1,0:T(8,128)S(1)} collective-permute-done((f32[3,48,128]{2,1,0:T(8,128)S(1)}, f32[3,48,128]{2,1,0:T(8,128)S(1)}, u32[]{:S(2)}, u32[]{:S(2)}) %collective-permute-start.10) | collective-permute-done | bytes 73760 | tf_op jit(solution)/shard_map/ppermute | solution.py:340
  50.8 1.2 %add.40 = f32[768,128]{1,0:T(8,128)} custom-call(f32[768,128]{1,0:T(8,128)S(1)} %get-tuple-element.27.acc, f32[1,104,128]{2,1,0:T(8,128)S(1)} %get-tuple-element.34.refs_0_.mine, f32[3,48,128]{2,1,0:T(8,128)S(1)} %pad_maximum_fusion.3.refs_0_, f32[3,48,128]{2,1,0:T(8,128)S(1)} %collective-permute-done.8.refs_1_, ...), custom_call_target="tpu_custom_call" | custom-call | tf_op jit(solution)/shard_map/add/pallas_call | solution.py:412
  (19 shorter events, 0.2 us)
Async XLA Ops:
  3.9 4.1 %collective-permute-start = (f32[3,104,128]{2,1,0:T(8,128)}, f32[3,104,128]{2,1,0:T(8,128)S(1)}, u32[]{:S(2)}, u32[]{:S(2)}) collective-permute-start(f32[3,104,128]{2,1,0:T(8,128)} %get-tuple-element.20), channel_id=1, source_target_pairs={{0,1},{1,0},{2,3},{3,2},{4,5},{5,4},{6,7},{7,6},{8,9},{9,8},{10,11... | collective-permute-start | bytes 479240 | tf_op jit(solution)/shard_map/ppermute | solution.py:340
  4.4 8.0 %collective-permute-start.1 = (f32[3,104,128]{2,1,0:T(8,128)}, f32[3,104,128]{2,1,0:T(8,128)S(1)}, u32[]{:S(2)}, u32[]{:S(2)}) collective-permute-start(f32[3,104,128]{2,1,0:T(8,128)} %get-tuple-element.21), channel_id=1, source_target_pairs={{0,2},{1,3},{2,0},{3,1},{4,6},{5,7},{6,4},{7,5},{8,10},{9,11},{10,... | collective-permute-start | bytes 479240 | tf_op jit(solution)/shard_map/ppermute | solution.py:340
  7.0 8.1 %collective-permute-start.2 = (f32[3,104,128]{2,1,0:T(8,128)}, f32[3,104,128]{2,1,0:T(8,128)S(1)}, u32[]{:S(2)}, u32[]{:S(2)}) collective-permute-start(f32[3,104,128]{2,1,0:T(8,128)} %get-tuple-element.23), channel_id=1, source_target_pairs={{0,3},{1,2},{2,1},{3,0},{4,7},{5,6},{6,5},{7,4},{8,11},{9,10},{10,... | collective-permute-start | bytes 479240 | tf_op jit(solution)/shard_map/ppermute | solution.py:340
  7.1 2.8 %copy-start = (f32[64,3,512]{2,0,1:T(8,128)S(1)}, f32[64,3,512]{2,0,1:T(8,128)}, u32[]{:S(2)}) copy-start(f32[64,3,512]{2,0,1:T(8,128)} %param.4) | copy-start | bytes 1179652
  7.1 2.8 %copy-start.1 = (f32[64,3,512]{2,0,1:T(8,128)S(1)}, f32[64,3,512]{2,0,1:T(8,128)}, u32[]{:S(2)}) copy-start(f32[64,3,512]{2,0,1:T(8,128)} %param.5) | copy-start | bytes 1179652
  8.1 12.4 %collective-permute-start.5 = (f32[2,104,128]{2,1,0:T(8,128)S(1)}, f32[2,104,128]{2,1,0:T(8,128)S(1)}, u32[]{:S(2)}, u32[]{:S(2)}) collective-permute-start(f32[2,104,128]{2,1,0:T(8,128)S(1)} %pad_maximum_fusion.2), channel_id=1, source_target_pairs={{0,4},{4,0},{8,12},{12,8},{16,20},{20,16},{24,28},{28,24},{1,5},{5... | collective-permute-start | bytes 319496 | tf_op jit(solution)/shard_map/ppermute | solution.py:344
  15.1 11.1 %collective-permute-start.4 = (f32[2,104,128]{2,1,0:T(8,128)S(1)}, f32[2,104,128]{2,1,0:T(8,128)S(1)}, u32[]{:S(2)}, u32[]{:S(2)}) collective-permute-start(f32[2,104,128]{2,1,0:T(8,128)S(1)} %pad_maximum_fusion.1), channel_id=1, source_target_pairs={{0,4},{4,0},{8,12},{12,8},{16,20},{20,16},{24,28},{28,24},{1,5},{5... | collective-permute-start | bytes 319496 | tf_op jit(solution)/shard_map/ppermute | solution.py:344
  16.8 15.0 %collective-permute-start.3 = (f32[4,104,128]{2,1,0:T(8,128)S(1)}, f32[4,104,128]{2,1,0:T(8,128)S(1)}, u32[]{:S(2)}, u32[]{:S(2)}) collective-permute-start(f32[4,104,128]{2,1,0:T(8,128)S(1)} %pad_maximum_fusion), channel_id=1, source_target_pairs={{0,28},{4,8},{8,4},{12,16},{16,12},{20,24},{24,20},{28,0},{1,29},{... | collective-permute-start | bytes 638984 | tf_op jit(solution)/shard_map/ppermute | solution.py:344
  37.2 5.7 %collective-permute-start.6 = (f32[4,48,128]{2,1,0:T(8,128)S(1)}, f32[4,48,128]{2,1,0:T(8,128)S(1)}, u32[]{:S(2)}, u32[]{:S(2)}) collective-permute-start(f32[4,48,128]{2,1,0:T(8,128)S(1)} %maximum_add_fusion), channel_id=1, source_target_pairs={{0,4},{4,0},{8,12},{12,8},{16,20},{20,16},{24,28},{28,24},{1,5},{5... | collective-permute-start | bytes 294920 | tf_op jit(solution)/shard_map/ppermute | solution.py:344
  37.3 7.4 %collective-permute-start.7 = (f32[4,48,128]{2,1,0:T(8,128)S(1)}, f32[4,48,128]{2,1,0:T(8,128)S(1)}, u32[]{:S(2)}, u32[]{:S(2)}) collective-permute-start(f32[4,48,128]{2,1,0:T(8,128)S(1)} %bitcast.47), channel_id=1, source_target_pairs={{0,28},{4,8},{8,4},{12,16},{16,12},{20,24},{24,20},{28,0},{1,29},{... | collective-permute-start | bytes 294920 | tf_op jit(solution)/shard_map/ppermute | solution.py:344
  44.7 2.0 %collective-permute-start.8 = (f32[3,48,128]{2,1,0:T(8,128)S(1)}, f32[3,48,128]{2,1,0:T(8,128)S(1)}, u32[]{:S(2)}, u32[]{:S(2)}) collective-permute-start(f32[3,48,128]{2,1,0:T(8,128)S(1)} %pad_maximum_fusion.4), channel_id=1, source_target_pairs={{0,1},{1,0},{2,3},{3,2},{4,5},{5,4},{6,7},{7,6},{8,9},{9,8},{10,11... | collective-permute-start | bytes 221192 | tf_op jit(solution)/shard_map/ppermute | solution.py:340
  44.8 4.8 %collective-permute-start.9 = (f32[3,48,128]{2,1,0:T(8,128)S(1)}, f32[3,48,128]{2,1,0:T(8,128)S(1)}, u32[]{:S(2)}, u32[]{:S(2)}) collective-permute-start(f32[3,48,128]{2,1,0:T(8,128)S(1)} %pad_maximum_fusion.5), channel_id=1, source_target_pairs={{0,2},{1,3},{2,0},{3,1},{4,6},{5,7},{6,4},{7,5},{8,10},{9,11},{10,... | collective-permute-start | bytes 221192 | tf_op jit(solution)/shard_map/ppermute | solution.py:340
  46.4 4.5 %collective-permute-start.10 = (f32[3,48,128]{2,1,0:T(8,128)S(1)}, f32[3,48,128]{2,1,0:T(8,128)S(1)}, u32[]{:S(2)}, u32[]{:S(2)}) collective-permute-start(f32[3,48,128]{2,1,0:T(8,128)S(1)} %pad_maximum_fusion.6), channel_id=1, source_target_pairs={{0,3},{1,2},{2,1},{3,0},{4,7},{5,6},{6,5},{7,4},{8,11},{9,10},{10,... | collective-permute-start | bytes 221192 | tf_op jit(solution)/shard_map/ppermute | solution.py:340

commit v8 on v7

--- a/solution.py
+++ b/solution.py
@@ -15,6 +15,7 @@
 LANES = 128
 FEATURES = 16
 GRAM = 8
+PIECES = 4
 
 f32 = jnp.float32
 bf16 = jnp.bfloat16
@@ -148,12 +149,15 @@
     n_space, n_pairs, share, cell_dev, tiles = sizes
     outs = refs[:n_pairs]
     slots, used, pos, frc, sems = refs[n_pairs:]
-    fetches = [
-        pltpu.make_async_copy(pos_hbm, pos, sems.at[0]),
-        pltpu.make_async_copy(frc_hbm, frc, sems.at[1]),
-    ]
-    for fetch in fetches:
-        fetch.start()
+    fetches = []
+    piece = pos.shape[0] // PIECES
+    for source, target in ((pos_hbm, pos), (frc_hbm, frc)):
+        for i in range(PIECES):
+            rows = pl.ds(i * piece, piece)
+            fetches.append(
+                pltpu.make_async_copy(source.at[rows], target.at[rows], sems.at[len(fetches)])
+            )
+            fetches[-1].start()
     n_slots = cells.shape[1]
     owner = cells[0, 0] // cell_dev
     here = owner // n_pairs
@@ -353,7 +357,7 @@
             pltpu.SMEM((3 * n_pairs,), jnp.int32),
             pltpu.VMEM(total.shape, f32),
             pltpu.VMEM(total.shape, f32),
-            pltpu.SemaphoreType.DMA((2,)),
+            pltpu.SemaphoreType.DMA((2 * PIECES,)),
         ],
         compiler_params=pltpu.CompilerParams(vmem_limit_bytes=60 * 1024 * 1024),
         name="pack",
@@ -396,14 +400,14 @@
     out_1f = beyond(jnp.stack([value[1] for value in rest]), 1)
     out_2 = beyond(jnp.concatenate([own[2], core[2]] + [value[2:] for value in rest]), 2)
     acc, reply_m = pairs([(1, out_1n)] + [(0, got[turn][0:1]) for turn in far], [acc])
-    acc, reply_1f = pairs([(1, out_1f)], [acc])
-    acc, reply_2, later = pairs([(2, out_2)], [acc], True)
-    reply_0n, reply_m, reply_1f, reply_2 = (
-        value.reshape(-1, rows_out, LANES) for value in (reply_0n, reply_m, reply_1f, reply_2)
-    )
+    acc, reply_f = pairs([(1, out_1f), (2, out_2)], [acc])
+    reply_0n, reply_m, reply_f = (
+        value.reshape(-1, rows_out, LANES) for value in (reply_0n, reply_m, reply_f)
+    )
+    cut = n_pairs - 2
     back_0 = jnp.concatenate([reply_0n, reply_m[2:]])
-    back_1 = beyond(jnp.concatenate([reply_m[:2], reply_1f]) + later[None], 1)
-    back_2 = beyond(reply_2, 2)
+    back_1 = beyond(jnp.concatenate([reply_m[:2], reply_f[:cut]]), 1)
+    back_2 = beyond(reply_f[cut:], 2)
     replies = []
     for turn in range(n_pairs):
         value = jnp.stack([back_0[turn], back_1[turn], back_2[turn]])

time: 52.4 us -> 52 us (level)
  starting transfers between devices: 12.6 us -> 15.3 us
  waiting for transfers between devices: 13.8 us -> 11.5 us
  Pallas kernels: 23.6 us -> 22.6 us
    ppermute x5, starting transfers between devices: 7.53 us -> 10.2 us  [beyond(): return lax.ppermute(value, 'space', moves)]
    ppermute x6, waiting for transfers between devices: 6.8 us -> 4.28 us  [across(): return lax.ppermute(value, 'pairs', [(j, j ^ turn) for j in range(n_pairs)])]
    pallas_call x4 -> x3, Pallas kernels: 19.2 us -> 18 us  [pairs(): pl.pallas_call(functools.partial(pair_kernel, sizes, kinds, len(before),...]
  transfers between devices with their start and end apart: 11 -> 11, of which waited for: 5 -> 7; matrix products, arithmetic and copies ran while one was open for 2% -> 2% of each run, Pallas kernels for 27% -> 16%
where the time goes in v8:
time: 52 us; the launch traced here: 51.4 us
  Pallas kernels  22.6 us (43%)
  starting transfers between devices  15.3 us (29%)
  waiting for transfers between devices  11.5 us (22%)
  local copies, waits for them, and re-layouts  1.03 us (2%)
  between operations  0.79 us (2%)
    pallas_call x3, Pallas kernels, pairs(): pl.pallas_call(functools.partial(pair_kernel, sizes, kinds, len(before),...  18 us
    ppermute x5, starting transfers between devices, beyond(): return lax.ppermute(value, 'space', moves)  10.2 us
    ppermute x5, waiting for transfers between devices, beyond(): return lax.ppermute(value, 'space', moves)  7.23 us
    ppermute x6, starting transfers between devices, across(): return lax.ppermute(value, 'pairs', [(j, j ^ turn) for j in range(n_pairs)])  5.14 us
    ppermute x6, waiting for transfers between devices, across(): return lax.ppermute(value, 'pairs', [(j, j ^ turn) for j in range(n_pairs)])  4.28 us
    pallas_call x1, Pallas kernels, body(): pl.pallas_call(functools.partial(pack_kernel, sizes), out_shape=[message]...  3.4 us
    pallas_call x1, Pallas kernels, body(): pl.pallas_call(functools.partial(add_kernel, sizes, where), out_shape=tot...  1.16 us
  transfers between devices with their start and end apart: 11, of which 7 were waited for; matrix products, arithmetic and copies ran while one was open for 2% of the time, Pallas kernels for 16%

profile of v8, /device:TPU:0, one launch (start us, length us, event | category | flops | bytes accessed | tf_op | source)
XLA Modules:
  0.0 51.4 jit_solution(16240171642304978333)
XLA Ops:
  0.7 3.4 %pack.1 = (f32[3,104,128]{2,1,0:T(8,128)}, f32[3,104,128]{2,1,0:T(8,128)}, f32[3,104,128]{2,1,0:T(8,128)}, f32[3,104,128]{2,1,0:T(8,128)}) custom-call(s32[2,48]{1,0:T(2,128)} %cells.1, s32[1]{0:T(128)S(6)} %copy.9.count, f32[768,128]{1,0:T(8,128)} %bitcast.33, f32[768,128]{1,0:T(8,128)} %bitcast.37), custom_call_target="tpu_custom_call" | custom-call | tf_op jit(solution)/shard_map/pack/pallas_call | solution.py:350
  4.1 3.0 %collective-permute-start = (f32[3,104,128]{2,1,0:T(8,128)}, f32[3,104,128]{2,1,0:T(8,128)S(1)}, u32[]{:S(2)}, u32[]{:S(2)}) collective-permute-start(f32[3,104,128]{2,1,0:T(8,128)} %get-tuple-element.16), channel_id=1, source_target_pairs={{0,2},{1,3},{2,0},{3,1},{4,6},{5,7},{6,4},{7,5},{8,10},{9,11},{10,... | collective-permute-start | bytes 479240 | tf_op jit(solution)/shard_map/ppermute | solution.py:344
  7.1 0.0 collective-permute-start.1
  7.1 0.2 collective-permute-start.2
  7.3 0.0 copy-start
  7.3 0.0 copy-start.1
  7.3 0.9 %fusion = (f32[1,104,128]{2,1,0:T(8,128)S(1)}, f32[1,104,128]{2,1,0:T(8,128)S(1)}, f32[1,104,128]{2,1,0:T(8,128)S(1)}) fusion(f32[3,104,128]{2,1,0:T(8,128)} %get-tuple-element.17), kind=kLoop, calls=%fused_computation.14 | loop fusion | bytes 319488 | tf_op jit(solution)/shard_map/slice | solution.py:395
  8.2 0.4 collective-permute-done.1
  8.7 1.6 %collective-permute-start.5 = (f32[2,104,128]{2,1,0:T(8,128)S(1)}, f32[2,104,128]{2,1,0:T(8,128)S(1)}, u32[]{:S(2)}, u32[]{:S(2)}) collective-permute-start(f32[2,104,128]{2,1,0:T(8,128)S(1)} %pad_maximum_fusion.2), channel_id=1, source_target_pairs={{0,4},{4,0},{8,12},{12,8},{16,20},{20,16},{24,28},{28,24},{1,5},{5... | collective-permute-start | bytes 319496 | tf_op jit(solution)/shard_map/ppermute | solution.py:348
  10.3 0.0 copy-done
  10.3 0.0 copy-done.1
  10.3 4.4 %pairs.3 = (f32[768,128]{1,0:T(8,128)S(1)}, f32[96,128]{1,0:T(8,128)S(1)}, f32[1,128]{1,0:T(1,128)S(1)}) custom-call(f32[1,104,128]{2,1,0:T(8,128)S(1)} %get-tuple-element.29.refs_0_.mine, f32[1,104,128]{2,1,0:T(8,128)S(1)} %get-tuple-element.32.refs_1_, f32[768,128]{1,0:T(8,128)S(1)} %bitcast.34, f32[768,128]{1,0:T(8,128)S(1)} %bitcast.38), custom_call_target="tpu_custom_call" | custom-call | flops 2000000000 | bytes 2000000 | tf_op jit(solution)/shard_map/pairs/pallas_call | solution.py:372
  14.8 0.0 collective-permute-done
  14.8 0.0 collective-permute-done.2
  14.9 1.0 %collective-permute-start.3 = (f32[2,104,128]{2,1,0:T(8,128)S(1)}, f32[2,104,128]{2,1,0:T(8,128)S(1)}, u32[]{:S(2)}, u32[]{:S(2)}) collective-permute-start(f32[2,104,128]{2,1,0:T(8,128)S(1)} %pad_maximum_fusion.1), channel_id=1, source_target_pairs={{0,4},{4,0},{8,12},{12,8},{16,20},{20,16},{24,28},{28,24},{1,5},{5... | collective-permute-start | bytes 319496 | tf_op jit(solution)/shard_map/ppermute | solution.py:348
  15.9 3.6 %collective-permute-start.4 = (f32[4,104,128]{2,1,0:T(8,128)S(1)}, f32[4,104,128]{2,1,0:T(8,128)S(1)}, u32[]{:S(2)}, u32[]{:S(2)}) collective-permute-start(f32[4,104,128]{2,1,0:T(8,128)S(1)} %pad_maximum_fusion), channel_id=1, source_target_pairs={{0,28},{4,8},{8,4},{12,16},{16,12},{20,24},{24,20},{28,0},{1,29},{... | collective-permute-start | bytes 638984 | tf_op jit(solution)/shard_map/ppermute | solution.py:348
  19.5 0.0 collective-permute-done.5.refs_0_
  19.5 3.9 %pairs.4 = (f32[768,128]{1,0:T(8,128)S(1)}, f32[192,128]{1,0:T(8,128)S(1)}) custom-call(f32[2,104,128]{2,1,0:T(8,128)S(1)} %collective-permute-done.5.refs_0_, f32[1,104,128]{2,1,0:T(8,128)S(1)} %slice.147.refs_1_, f32[1,104,128]{2,1,0:T(8,128)S(1)} %slice.148.refs_2_, f32[768,128]{1,0:T(8,128)S(1)} %bitcast.35, ...), custom_call_target="tpu_custom_call", output_to_operand_aliasing={{0}: (5, {})} | custom-call | flops 4000000000 | bytes 2000000 | tf_op jit(solution)/shard_map/pairs/pallas_call | solution.py:372
  23.4 0.1 collective-permute-done.3.refs_0_
  23.5 2.7 %collective-permute-done.4.refs_1_ = f32[4,104,128]{2,1,0:T(8,128)S(1)} collective-permute-done((f32[4,104,128]{2,1,0:T(8,128)S(1)}, f32[4,104,128]{2,1,0:T(8,128)S(1)}, u32[]{:S(2)}, u32[]{:S(2)}) %collective-permute-start.4) | collective-permute-done | bytes 213024 | tf_op jit(solution)/shard_map/ppermute | solution.py:348
  26.2 9.7 %pairs.5 = (f32[768,128]{1,0:T(8,128)S(1)}, f32[288,128]{1,0:T(8,128)S(1)}) custom-call(f32[2,104,128]{2,1,0:T(8,128)S(1)} %collective-permute-done.3.refs_0_, f32[4,104,128]{2,1,0:T(8,128)S(1)} %collective-permute-done.4.refs_1_, f32[768,128]{1,0:T(8,128)S(1)} %bitcast.36, f32[768,128]{1,0:T(8,128)S(1)} %bitcast.40, ...), custom_call_target="tpu_custom_call", output_to_operand_aliasing={{0}: (4, {})} | custom-call | flops 6000000000 | bytes 2000000 | tf_op jit(solution)/shard_map/pairs/pallas_call | solution.py:372
  36.0 0.1 collective-permute-start.6
  36.1 3.9 %collective-permute-start.7 = (f32[4,48,128]{2,1,0:T(8,128)S(1)}, f32[4,48,128]{2,1,0:T(8,128)S(1)}, u32[]{:S(2)}, u32[]{:S(2)}) collective-permute-start(f32[4,48,128]{2,1,0:T(8,128)S(1)} %bitcast.44), channel_id=1, source_target_pairs={{0,28},{4,8},{8,4},{12,16},{16,12},{20,24},{24,20},{28,0},{1,29},{... | collective-permute-start | bytes 294920 | tf_op jit(solution)/shard_map/ppermute | solution.py:348
  40.0 1.5 %collective-permute-done.6 = f32[4,48,128]{2,1,0:T(8,128)S(1)} collective-permute-done((f32[4,48,128]{2,1,0:T(8,128)S(1)}, f32[4,48,128]{2,1,0:T(8,128)S(1)}, u32[]{:S(2)}, u32[]{:S(2)}) %collective-permute-start.6) | collective-permute-done | bytes 98336 | tf_op jit(solution)/shard_map/ppermute | solution.py:348
  41.6 2.9 %collective-permute-done.7 = f32[4,48,128]{2,1,0:T(8,128)S(1)} collective-permute-done((f32[4,48,128]{2,1,0:T(8,128)S(1)}, f32[4,48,128]{2,1,0:T(8,128)S(1)}, u32[]{:S(2)}, u32[]{:S(2)}) %collective-permute-start.7) | collective-permute-done | bytes 98336 | tf_op jit(solution)/shard_map/ppermute | solution.py:348
  44.5 0.2 collective-permute-start.8
  44.7 0.7 %collective-permute-start.9 = (f32[3,48,128]{2,1,0:T(8,128)S(1)}, f32[3,48,128]{2,1,0:T(8,128)S(1)}, u32[]{:S(2)}, u32[]{:S(2)}) collective-permute-start(f32[3,48,128]{2,1,0:T(8,128)S(1)} %pad_maximum_fusion.6), channel_id=1, source_target_pairs={{0,2},{1,3},{2,0},{3,1},{4,6},{5,7},{6,4},{7,5},{8,10},{9,11},{10,... | collective-permute-start | bytes 221192 | tf_op jit(solution)/shard_map/ppermute | solution.py:344
  45.3 1.1 %collective-permute-start.10 = (f32[3,48,128]{2,1,0:T(8,128)S(1)}, f32[3,48,128]{2,1,0:T(8,128)S(1)}, u32[]{:S(2)}, u32[]{:S(2)}) collective-permute-start(f32[3,48,128]{2,1,0:T(8,128)S(1)} %pad_maximum_fusion.7), channel_id=1, source_target_pairs={{0,3},{1,2},{2,1},{3,0},{4,7},{5,6},{6,5},{7,4},{8,11},{9,10},{10,... | collective-permute-start | bytes 221192 | tf_op jit(solution)/shard_map/ppermute | solution.py:344
  46.4 0.0 collective-permute-done.8.refs_1_
  46.4 3.4 %collective-permute-done.9.refs_2_ = f32[3,48,128]{2,1,0:T(8,128)S(1)} collective-permute-done((f32[3,48,128]{2,1,0:T(8,128)S(1)}, f32[3,48,128]{2,1,0:T(8,128)S(1)}, u32[]{:S(2)}, u32[]{:S(2)}) %collective-permute-start.9) | collective-permute-done | bytes 73760 | tf_op jit(solution)/shard_map/ppermute | solution.py:344
  49.8 0.5 collective-permute-done.10.refs_3_
  50.2 1.2 %add.25 = f32[768,128]{1,0:T(8,128)} custom-call(f32[768,128]{1,0:T(8,128)S(1)} %get-tuple-element.23.acc, f32[1,104,128]{2,1,0:T(8,128)S(1)} %get-tuple-element.29.refs_0_.mine, f32[3,48,128]{2,1,0:T(8,128)S(1)} %pad_maximum_fusion.4.refs_0_, f32[3,48,128]{2,1,0:T(8,128)S(1)} %collective-permute-done.8.refs_1_, ...), custom_call_target="tpu_custom_call" | custom-call | tf_op jit(solution)/shard_map/add/pallas_call | solution.py:416
  (20 shorter events, 0.2 us)
Async XLA Ops:
  4.1 10.7 %collective-permute-start = (f32[3,104,128]{2,1,0:T(8,128)}, f32[3,104,128]{2,1,0:T(8,128)S(1)}, u32[]{:S(2)}, u32[]{:S(2)}) collective-permute-start(f32[3,104,128]{2,1,0:T(8,128)} %get-tuple-element.16), channel_id=1, source_target_pairs={{0,2},{1,3},{2,0},{3,1},{4,6},{5,7},{6,4},{7,5},{8,10},{9,11},{10,... | collective-permute-start | bytes 479240 | tf_op jit(solution)/shard_map/ppermute | solution.py:344
  7.1 1.6 %collective-permute-start.1 = (f32[3,104,128]{2,1,0:T(8,128)}, f32[3,104,128]{2,1,0:T(8,128)S(1)}, u32[]{:S(2)}, u32[]{:S(2)}) collective-permute-start(f32[3,104,128]{2,1,0:T(8,128)} %get-tuple-element.18), channel_id=1, source_target_pairs={{0,1},{1,0},{2,3},{3,2},{4,5},{5,4},{6,7},{7,6},{8,9},{9,8},{10,11... | collective-permute-start | bytes 479240 | tf_op jit(solution)/shard_map/ppermute | solution.py:344
  7.1 7.7 %collective-permute-start.2 = (f32[3,104,128]{2,1,0:T(8,128)}, f32[3,104,128]{2,1,0:T(8,128)S(1)}, u32[]{:S(2)}, u32[]{:S(2)}) collective-permute-start(f32[3,104,128]{2,1,0:T(8,128)} %get-tuple-element.20), channel_id=1, source_target_pairs={{0,3},{1,2},{2,1},{3,0},{4,7},{5,6},{6,5},{7,4},{8,11},{9,10},{10,... | collective-permute-start | bytes 479240 | tf_op jit(solution)/shard_map/ppermute | solution.py:344
  7.3 3.0 %copy-start = (f32[64,3,512]{2,0,1:T(8,128)S(1)}, f32[64,3,512]{2,0,1:T(8,128)}, u32[]{:S(2)}) copy-start(f32[64,3,512]{2,0,1:T(8,128)} %param.4) | copy-start | bytes 1179652
  7.3 3.0 %copy-start.1 = (f32[64,3,512]{2,0,1:T(8,128)S(1)}, f32[64,3,512]{2,0,1:T(8,128)}, u32[]{:S(2)}) copy-start(f32[64,3,512]{2,0,1:T(8,128)} %param.5) | copy-start | bytes 1179652
  8.7 10.8 %collective-permute-start.5 = (f32[2,104,128]{2,1,0:T(8,128)S(1)}, f32[2,104,128]{2,1,0:T(8,128)S(1)}, u32[]{:S(2)}, u32[]{:S(2)}) collective-permute-start(f32[2,104,128]{2,1,0:T(8,128)S(1)} %pad_maximum_fusion.2), channel_id=1, source_target_pairs={{0,4},{4,0},{8,12},{12,8},{16,20},{20,16},{24,28},{28,24},{1,5},{5... | collective-permute-start | bytes 319496 | tf_op jit(solution)/shard_map/ppermute | solution.py:348
  14.9 8.6 %collective-permute-start.3 = (f32[2,104,128]{2,1,0:T(8,128)S(1)}, f32[2,104,128]{2,1,0:T(8,128)S(1)}, u32[]{:S(2)}, u32[]{:S(2)}) collective-permute-start(f32[2,104,128]{2,1,0:T(8,128)S(1)} %pad_maximum_fusion.1), channel_id=1, source_target_pairs={{0,4},{4,0},{8,12},{12,8},{16,20},{20,16},{24,28},{28,24},{1,5},{5... | collective-permute-start | bytes 319496 | tf_op jit(solution)/shard_map/ppermute | solution.py:348
  15.9 10.4 %collective-permute-start.4 = (f32[4,104,128]{2,1,0:T(8,128)S(1)}, f32[4,104,128]{2,1,0:T(8,128)S(1)}, u32[]{:S(2)}, u32[]{:S(2)}) collective-permute-start(f32[4,104,128]{2,1,0:T(8,128)S(1)} %pad_maximum_fusion), channel_id=1, source_target_pairs={{0,28},{4,8},{8,4},{12,16},{16,12},{20,24},{24,20},{28,0},{1,29},{... | collective-permute-start | bytes 638984 | tf_op jit(solution)/shard_map/ppermute | solution.py:348
  36.0 5.6 %collective-permute-start.6 = (f32[4,48,128]{2,1,0:T(8,128)S(1)}, f32[4,48,128]{2,1,0:T(8,128)S(1)}, u32[]{:S(2)}, u32[]{:S(2)}) collective-permute-start(f32[4,48,128]{2,1,0:T(8,128)S(1)} %pad_maximum_fusion.3), channel_id=1, source_target_pairs={{0,4},{4,0},{8,12},{12,8},{16,20},{20,16},{24,28},{28,24},{1,5},{5... | collective-permute-start | bytes 294920 | tf_op jit(solution)/shard_map/ppermute | solution.py:348
  36.1 8.3 %collective-permute-start.7 = (f32[4,48,128]{2,1,0:T(8,128)S(1)}, f32[4,48,128]{2,1,0:T(8,128)S(1)}, u32[]{:S(2)}, u32[]{:S(2)}) collective-permute-start(f32[4,48,128]{2,1,0:T(8,128)S(1)} %bitcast.44), channel_id=1, source_target_pairs={{0,28},{4,8},{8,4},{12,16},{16,12},{20,24},{24,20},{28,0},{1,29},{... | collective-permute-start | bytes 294920 | tf_op jit(solution)/shard_map/ppermute | solution.py:348
  44.5 2.0 %collective-permute-start.8 = (f32[3,48,128]{2,1,0:T(8,128)S(1)}, f32[3,48,128]{2,1,0:T(8,128)S(1)}, u32[]{:S(2)}, u32[]{:S(2)}) collective-permute-start(f32[3,48,128]{2,1,0:T(8,128)S(1)} %pad_maximum_fusion.5), channel_id=1, source_target_pairs={{0,1},{1,0},{2,3},{3,2},{4,5},{5,4},{6,7},{7,6},{8,9},{9,8},{10,11... | collective-permute-start | bytes 221192 | tf_op jit(solution)/shard_map/ppermute | solution.py:344
  44.7 5.1 %collective-permute-start.9 = (f32[3,48,128]{2,1,0:T(8,128)S(1)}, f32[3,48,128]{2,1,0:T(8,128)S(1)}, u32[]{:S(2)}, u32[]{:S(2)}) collective-permute-start(f32[3,48,128]{2,1,0:T(8,128)S(1)} %pad_maximum_fusion.6), channel_id=1, source_target_pairs={{0,2},{1,3},{2,0},{3,1},{4,6},{5,7},{6,4},{7,5},{8,10},{9,11},{10,... | collective-permute-start | bytes 221192 | tf_op jit(solution)/shard_map/ppermute | solution.py:344
  45.3 4.9 %collective-permute-start.10 = (f32[3,48,128]{2,1,0:T(8,128)S(1)}, f32[3,48,128]{2,1,0:T(8,128)S(1)}, u32[]{:S(2)}, u32[]{:S(2)}) collective-permute-start(f32[3,48,128]{2,1,0:T(8,128)S(1)} %pad_maximum_fusion.7), channel_id=1, source_target_pairs={{0,3},{1,2},{2,1},{3,0},{4,7},{5,6},{6,5},{7,4},{8,11},{9,10},{10,... | collective-permute-start | bytes 221192 | tf_op jit(solution)/shard_map/ppermute | solution.py:344

commit v9 on v7

--- a/solution.py
+++ b/solution.py
@@ -147,7 +147,7 @@
 def pack_kernel(sizes, cells, count, pos_hbm, frc_hbm, *refs):
     n_space, n_pairs, share, cell_dev, tiles = sizes
     outs = refs[:n_pairs]
-    slots, used, pos, frc, sems = refs[n_pairs:]
+    pos, frc, sems = refs[n_pairs:]
     fetches = [
         pltpu.make_async_copy(pos_hbm, pos, sems.at[0]),
         pltpu.make_async_copy(frc_hbm, frc, sems.at[1]),
@@ -155,46 +155,50 @@
     for fetch in fetches:
         fetch.start()
     n_slots = cells.shape[1]
-    owner = cells[0, 0] // cell_dev
-    here = owner // n_pairs
-    here_turn = lax.rem(owner, n_pairs)
-    for bucket in range(3 * n_pairs):
-        used[bucket] = 0
-    for s in range(n_slots):
-        owner = cells[1, s] // cell_dev
-        there = owner // n_pairs
-        turn = lax.rem(owner, n_pairs) ^ here_turn
-        kind = jnp.where(there == here, 0, jnp.where(there // 2 == here // 2, 1, 2))
-        bucket = kind * n_pairs + turn
-        rank = used[bucket]
-        used[bucket] = rank + 1
-        slots[bucket * share + rank] = s
+    shape = (n_slots, n_slots)
+    down = lax.broadcasted_iota(jnp.int32, shape, 0)
+    along = lax.broadcasted_iota(jnp.int32, shape, 1)
+    here = lax.axis_index("space")
+    here_turn = lax.axis_index("pairs")
+
+    def bucket(cell):
+        there = cell >> (cell_dev * n_pairs).bit_length() - 1
+        turn = (cell >> cell_dev.bit_length() - 1) & (n_pairs - 1) ^ here_turn
+        kind = jnp.where(there == here, 0, jnp.where(there >> 1 == here >> 1, 1, 2))
+        return kind * n_pairs + turn
+
+    def column(row):
+        return jnp.sum(jnp.where(down == along, row, 0), axis=1, keepdims=True)
+
+    second = column(cells[1:2, :])
+    same = (bucket(second) == bucket(cells[1:2, :])) & (along < down)
+    rank = jnp.sum(jnp.where(same, 1, 0), axis=1, keepdims=True)
+    live = lax.broadcasted_iota(jnp.int32, (n_slots, 1), 0) < count[0]
+    chosen = bucket(second) * share + rank == along
+
+    def by_place(values):
+        local = jnp.where(live, values & (cell_dev - 1), -1)
+        return jnp.sum(jnp.where(chosen, local, 0), axis=0, keepdims=True)
+
+    label = by_place(second)
+    table = by_place(column(cells[0:1, :]))
+    last = share * 6 * tiles
+    plane = cell_dev * tiles
     for fetch in fetches:
         fetch.wait()
-    lane = lax.broadcasted_iota(jnp.int32, (1, LANES), 1)
-    plane = cell_dev * tiles
-    last = share * 6 * tiles
-    table = jnp.full((1, LANES), -1.0, f32)
     for m in range(3 * n_pairs):
         kind, turn = m // n_pairs, m % n_pairs
         out = outs[turn]
-        label = jnp.full((1, LANES), -1.0, f32)
         for k in range(share):
-            s = slots[m * share + k]
-            a = lax.rem(cells[0, s], cell_dev)
-            live = s < count[0]
-            b = jnp.where(live, lax.rem(cells[1, s], cell_dev), -1)
-            table = jnp.where(lane == m * share + k, jnp.where(live, a, -1).astype(f32), table)
-            label = jnp.where(lane == k, b.astype(f32), label)
-            base = row_base(a, tiles)
+            base = row_base(jnp.maximum(table[0, m * share + k], 0), tiles)
             for c in range(6):
                 source = pos if c < 3 else frc
                 row = (k * 6 + c) * tiles
                 out[kind, row : row + tiles, :] = source[
                     pl.ds(base + c % 3 * plane, tiles, stride=8), :
                 ]
-        out[kind, last : last + 1, :] = label
-    outs[0][0, last + 1 : last + 2, :] = table
+        out[kind, last : last + 1, 0:n_slots] = label.astype(f32)
+    outs[0][0, last + 1 : last + 2, 0:n_slots] = table.astype(f32)
 
 
 def pair_kernel(sizes, kinds, started, marked, *refs):
@@ -206,6 +210,7 @@
     feats[...] = jnp.zeros_like(feats)
     grams[...] = jnp.zeros_like(grams)
     rows_in = share * 6 * tiles
+    n_slots = 3 * n_pairs * share
     plane = cell_dev * tiles
     if not started:
         acc[...] = jnp.zeros_like(acc)
@@ -214,17 +219,17 @@
     here = lax.axis_index("space")
     number = jnp.int32(0)
     first = 0
-    for kind, message in zip(kinds, messages):
+    for (kind, turns), message in zip(kinds, messages):
         away = jnp.int32(away_of(kind, lax.rem(here, 2)))
         there = lax.rem(here + away + n_space, n_space)
         half = 0.5 * slab_width * away.astype(f32)
         middle_a = slab_width * (there.astype(f32) + 0.5) - half
         middle_b = slab_width * (here.astype(f32) + 0.5) + half
-        for block in range(message.shape[0]):
+        for block, turn in enumerate(turns):
             inbox[first * rows_in : (first + 1) * rows_in, :] = message[block, 0:rows_in, :]
-            label = message[block, rows_in : rows_in + 1, :].astype(jnp.int32)
+            label = message[block, rows_in : rows_in + 1, 0:n_slots].astype(jnp.int32)
             for k in range(share):
-                b = label[0, k]
+                b = label[0, (kind * n_pairs + turn) * share + k]
                 todo[0, number] = first * share + k
                 todo[1, number] = b
                 middles[0, number] = middle_a
@@ -289,7 +294,7 @@
     replies, out = refs[:-1], refs[-1]
     plane = cell_dev * tiles
     last = share * 6 * tiles
-    table = mine[0, last + 1 : last + 2, :].astype(jnp.int32)
+    table = mine[0, last + 1 : last + 2, 0 : 3 * n_pairs * share].astype(jnp.int32)
     out[...] = acc[...]
     for m, (operand, block) in enumerate(where):
         for k in range(share):
@@ -346,11 +351,9 @@
     sent = pl.pallas_call(
         functools.partial(pack_kernel, sizes),
         out_shape=[message] * n_pairs,
-        in_specs=[smem, smem, hbm, hbm],
+        in_specs=[vmem, smem, hbm, hbm],
         out_specs=[vmem] * n_pairs,
         scratch_shapes=[
-            pltpu.SMEM((n_slots,), jnp.int32),
-            pltpu.SMEM((3 * n_pairs,), jnp.int32),
             pltpu.VMEM(total.shape, f32),
             pltpu.VMEM(total.shape, f32),
             pltpu.SemaphoreType.DMA((2,)),
@@ -361,8 +364,8 @@
     got = [sent[0]] + [across(sent[turn], turn) for turn in range(1, n_pairs)]
 
     def pairs(arrived, before, marked=False):
-        kinds = [kind for kind, _ in arrived]
-        values = [value for _, value in arrived]
+        kinds = [(kind, turns) for kind, turns, _ in arrived]
+        values = [value for _, _, value in arrived]
         n = len(values)
         blocks = sum(value.shape[0] for value in values)
         return pl.pallas_call(
@@ -391,19 +394,21 @@
     own = [sent[0][kind : kind + 1] for kind in range(3)]
     core = [got[1][kind : kind + 1] for kind in range(3)]
     out_1n = beyond(jnp.concatenate([own[1], core[1]]), 1)
-    acc, reply_0n, nothing = pairs([(0, own[0]), (0, core[0])], [], True)
+    acc, reply_0n, nothing = pairs([(0, (0,), own[0]), (0, (1,), core[0])], [], True)
     rest = [got[turn] + nothing[None] for turn in far]
     out_1f = beyond(jnp.stack([value[1] for value in rest]), 1)
     out_2 = beyond(jnp.concatenate([own[2], core[2]] + [value[2:] for value in rest]), 2)
-    acc, reply_m = pairs([(1, out_1n)] + [(0, got[turn][0:1]) for turn in far], [acc])
-    acc, reply_1f = pairs([(1, out_1f)], [acc])
-    acc, reply_2, later = pairs([(2, out_2)], [acc], True)
-    reply_0n, reply_m, reply_1f, reply_2 = (
-        value.reshape(-1, rows_out, LANES) for value in (reply_0n, reply_m, reply_1f, reply_2)
-    )
+    acc, reply_m = pairs(
+        [(1, near, out_1n)] + [(0, (turn,), got[turn][0:1]) for turn in far], [acc]
+    )
+    acc, reply_f = pairs([(1, far, out_1f), (2, range(n_pairs), out_2)], [acc])
+    reply_0n, reply_m, reply_f = (
+        value.reshape(-1, rows_out, LANES) for value in (reply_0n, reply_m, reply_f)
+    )
+    cut = n_pairs - 2
     back_0 = jnp.concatenate([reply_0n, reply_m[2:]])
-    back_1 = beyond(jnp.concatenate([reply_m[:2], reply_1f]) + later[None], 1)
-    back_2 = beyond(reply_2, 2)
+    back_1 = beyond(jnp.concatenate([reply_m[:2], reply_f[:cut]]), 1)
+    back_2 = beyond(reply_f[cut:], 2)
     replies = []
     for turn in range(n_pairs):
         value = jnp.stack([back_0[turn], back_1[turn], back_2[turn]])

time: 52.4 us -> 52.3 us (level); the launches traced: 52 us -> 52.6 us
  Pallas kernels: 23.6 us -> 19 us
  starting transfers between devices: 12.6 us -> 16.8 us
  waiting for transfers between devices: 13.8 us -> 14.8 us
    pallas_call x4 -> x3, Pallas kernels: 19.2 us -> 14.9 us  [pairs(): pl.pallas_call(functools.partial(pair_kernel, sizes, kinds, len(before),...]
    ppermute x5, waiting for transfers between devices: 7.01 us -> 10.2 us  [beyond(): return lax.ppermute(value, 'space', moves)]
    ppermute x5, starting transfers between devices: 7.53 us -> 9.91 us  [beyond(): return lax.ppermute(value, 'space', moves)]
    ppermute x6, waiting for transfers between devices: 6.8 us -> 4.54 us  [across(): return lax.ppermute(value, 'pairs', [(j, j ^ turn) for j in range(n_pairs)])]
    ppermute x6, starting transfers between devices: 5.08 us -> 6.92 us  [across(): return lax.ppermute(value, 'pairs', [(j, j ^ turn) for j in range(n_pairs)])]
  transfers between devices with their start and end apart: 11 -> 11, of which waited for: 5 -> 7; matrix products, arithmetic and copies ran while one was open for 2% -> 2% of each run, Pallas kernels for 27% -> 12%
where the time goes in v9:
time: 52.3 us; the launch traced here: 52.6 us
  Pallas kernels  19 us (36%)
  starting transfers between devices  16.8 us (32%)
  waiting for transfers between devices  14.8 us (28%)
  local copies, waits for them, and re-layouts  1.03 us (2%)
  between operations  0.79 us (2%)
    pallas_call x3, Pallas kernels, pairs(): pl.pallas_call(functools.partial(pair_kernel, sizes, kinds, len(before),...  14.9 us
    ppermute x5, waiting for transfers between devices, beyond(): return lax.ppermute(value, 'space', moves)  10.2 us
    ppermute x5, starting transfers between devices, beyond(): return lax.ppermute(value, 'space', moves)  9.91 us
    ppermute x6, starting transfers between devices, across(): return lax.ppermute(value, 'pairs', [(j, j ^ turn) for j in range(n_pairs)])  6.92 us
    ppermute x6, waiting for transfers between devices, across(): return lax.ppermute(value, 'pairs', [(j, j ^ turn) for j in range(n_pairs)])  4.54 us
    pallas_call x1, Pallas kernels, body(): pl.pallas_call(functools.partial(pack_kernel, sizes), out_shape=[message]...  2.98 us
    pallas_call x1, Pallas kernels, body(): pl.pallas_call(functools.partial(add_kernel, sizes, where), out_shape=tot...  1.14 us
  transfers between devices with their start and end apart: 11, of which 7 were waited for; matrix products, arithmetic and copies ran while one was open for 2% of the time, Pallas kernels for 12%

profile of v9, /device:TPU:0, one launch (start us, length us, event | category | flops | bytes accessed | tf_op | source)
XLA Modules:
  0.0 52.6 jit_solution(12058944935173589583)
XLA Ops:
  0.7 3.0 %pack.1 = (f32[3,104,128]{2,1,0:T(8,128)}, f32[3,104,128]{2,1,0:T(8,128)}, f32[3,104,128]{2,1,0:T(8,128)}, f32[3,104,128]{2,1,0:T(8,128)}) custom-call(s32[2,48]{1,0:T(2,128)} %cells.1, s32[1]{0:T(128)S(6)} %copy.9.count, f32[768,128]{1,0:T(8,128)} %bitcast.33, f32[768,128]{1,0:T(8,128)} %bitcast.37), custom_call_target="tpu_custom_call" | custom-call | tf_op jit(solution)/shard_map/pack/pallas_call | solution.py:351
  3.6 3.0 %collective-permute-start = (f32[3,104,128]{2,1,0:T(8,128)}, f32[3,104,128]{2,1,0:T(8,128)S(1)}, u32[]{:S(2)}, u32[]{:S(2)}) collective-permute-start(f32[3,104,128]{2,1,0:T(8,128)} %get-tuple-element.16), channel_id=1, source_target_pairs={{0,2},{1,3},{2,0},{3,1},{4,6},{5,7},{6,4},{7,5},{8,10},{9,11},{10,... | collective-permute-start | bytes 479240 | tf_op jit(solution)/shard_map/ppermute | solution.py:345
  6.6 0.0 collective-permute-start.1
  6.6 0.2 collective-permute-start.2
  6.8 0.0 copy-start
  6.9 0.0 copy-start.1
  6.9 0.9 %fusion = (f32[1,104,128]{2,1,0:T(8,128)S(1)}, f32[1,104,128]{2,1,0:T(8,128)S(1)}, f32[1,104,128]{2,1,0:T(8,128)S(1)}) fusion(f32[3,104,128]{2,1,0:T(8,128)} %get-tuple-element.17), kind=kLoop, calls=%fused_computation.14 | loop fusion | bytes 319488 | tf_op jit(solution)/shard_map/slice | solution.py:394
  7.8 0.4 collective-permute-done.1
  8.3 1.6 %collective-permute-start.5 = (f32[2,104,128]{2,1,0:T(8,128)S(1)}, f32[2,104,128]{2,1,0:T(8,128)S(1)}, u32[]{:S(2)}, u32[]{:S(2)}) collective-permute-start(f32[2,104,128]{2,1,0:T(8,128)S(1)} %pad_maximum_fusion.2), channel_id=1, source_target_pairs={{0,4},{4,0},{8,12},{12,8},{16,20},{20,16},{24,28},{28,24},{1,5},{5... | collective-permute-start | bytes 319496 | tf_op jit(solution)/shard_map/ppermute | solution.py:349
  9.9 0.0 copy-done
  9.9 0.0 copy-done.1
  9.9 4.4 %pairs.3 = (f32[768,128]{1,0:T(8,128)S(1)}, f32[96,128]{1,0:T(8,128)S(1)}, f32[1,128]{1,0:T(1,128)S(1)}) custom-call(f32[1,104,128]{2,1,0:T(8,128)S(1)} %get-tuple-element.29.refs_0_.mine, f32[1,104,128]{2,1,0:T(8,128)S(1)} %get-tuple-element.32.refs_1_, f32[768,128]{1,0:T(8,128)S(1)} %bitcast.34, f32[768,128]{1,0:T(8,128)S(1)} %bitcast.38), custom_call_target="tpu_custom_call" | custom-call | flops 2000000000 | bytes 2000000 | tf_op jit(solution)/shard_map/pairs/pallas_call | solution.py:371
  14.3 0.0 collective-permute-done
  14.3 0.0 collective-permute-done.2
  14.4 1.0 %collective-permute-start.3 = (f32[2,104,128]{2,1,0:T(8,128)S(1)}, f32[2,104,128]{2,1,0:T(8,128)S(1)}, u32[]{:S(2)}, u32[]{:S(2)}) collective-permute-start(f32[2,104,128]{2,1,0:T(8,128)S(1)} %pad_maximum_fusion.1), channel_id=1, source_target_pairs={{0,4},{4,0},{8,12},{12,8},{16,20},{20,16},{24,28},{28,24},{1,5},{5... | collective-permute-start | bytes 319496 | tf_op jit(solution)/shard_map/ppermute | solution.py:349
  15.4 3.6 %collective-permute-start.4 = (f32[4,104,128]{2,1,0:T(8,128)S(1)}, f32[4,104,128]{2,1,0:T(8,128)S(1)}, u32[]{:S(2)}, u32[]{:S(2)}) collective-permute-start(f32[4,104,128]{2,1,0:T(8,128)S(1)} %pad_maximum_fusion), channel_id=1, source_target_pairs={{0,28},{4,8},{8,4},{12,16},{16,12},{20,24},{24,20},{28,0},{1,29},{... | collective-permute-start | bytes 638984 | tf_op jit(solution)/shard_map/ppermute | solution.py:349
  19.1 0.0 collective-permute-done.5.refs_0_
  19.1 1.7 %pairs.4 = (f32[768,128]{1,0:T(8,128)S(1)}, f32[192,128]{1,0:T(8,128)S(1)}) custom-call(f32[2,104,128]{2,1,0:T(8,128)S(1)} %collective-permute-done.5.refs_0_, f32[1,104,128]{2,1,0:T(8,128)S(1)} %slice.147.refs_1_, f32[1,104,128]{2,1,0:T(8,128)S(1)} %slice.148.refs_2_, f32[768,128]{1,0:T(8,128)S(1)} %bitcast.35, ...), custom_call_target="tpu_custom_call", output_to_operand_aliasing={{0}: (5, {})} | custom-call | flops 4000000000 | bytes 2000000 | tf_op jit(solution)/shard_map/pairs/pallas_call | solution.py:371
  20.8 2.3 %collective-permute-done.3.refs_0_ = f32[2,104,128]{2,1,0:T(8,128)S(1)} collective-permute-done((f32[2,104,128]{2,1,0:T(8,128)S(1)}, f32[2,104,128]{2,1,0:T(8,128)S(1)}, u32[]{:S(2)}, u32[]{:S(2)}) %collective-permute-start.3) | collective-permute-done | bytes 106528 | tf_op jit(solution)/shard_map/ppermute | solution.py:349
  23.1 2.7 %collective-permute-done.4.refs_1_ = f32[4,104,128]{2,1,0:T(8,128)S(1)} collective-permute-done((f32[4,104,128]{2,1,0:T(8,128)S(1)}, f32[4,104,128]{2,1,0:T(8,128)S(1)}, u32[]{:S(2)}, u32[]{:S(2)}) %collective-permute-start.4) | collective-permute-done | bytes 213024 | tf_op jit(solution)/shard_map/ppermute | solution.py:349
  25.8 8.8 %pairs.5 = (f32[768,128]{1,0:T(8,128)S(1)}, f32[288,128]{1,0:T(8,128)S(1)}) custom-call(f32[2,104,128]{2,1,0:T(8,128)S(1)} %collective-permute-done.3.refs_0_, f32[4,104,128]{2,1,0:T(8,128)S(1)} %collective-permute-done.4.refs_1_, f32[768,128]{1,0:T(8,128)S(1)} %bitcast.36, f32[768,128]{1,0:T(8,128)S(1)} %bitcast.40, ...), custom_call_target="tpu_custom_call", output_to_operand_aliasing={{0}: (4, {})} | custom-call | flops 6000000000 | bytes 2000000 | tf_op jit(solution)/shard_map/pairs/pallas_call | solution.py:371
  34.6 1.0 %collective-permute-start.6 = (f32[4,48,128]{2,1,0:T(8,128)S(1)}, f32[4,48,128]{2,1,0:T(8,128)S(1)}, u32[]{:S(2)}, u32[]{:S(2)}) collective-permute-start(f32[4,48,128]{2,1,0:T(8,128)S(1)} %pad_maximum_fusion.3), channel_id=1, source_target_pairs={{0,4},{4,0},{8,12},{12,8},{16,20},{20,16},{24,28},{28,24},{1,5},{5... | collective-permute-start | bytes 294920 | tf_op jit(solution)/shard_map/ppermute | solution.py:349
  35.7 2.7 %collective-permute-start.7 = (f32[4,48,128]{2,1,0:T(8,128)S(1)}, f32[4,48,128]{2,1,0:T(8,128)S(1)}, u32[]{:S(2)}, u32[]{:S(2)}) collective-permute-start(f32[4,48,128]{2,1,0:T(8,128)S(1)} %bitcast.44), channel_id=1, source_target_pairs={{0,28},{4,8},{8,4},{12,16},{16,12},{20,24},{24,20},{28,0},{1,29},{... | collective-permute-start | bytes 294920 | tf_op jit(solution)/shard_map/ppermute | solution.py:349
  38.4 1.0 %collective-permute-done.6 = f32[4,48,128]{2,1,0:T(8,128)S(1)} collective-permute-done((f32[4,48,128]{2,1,0:T(8,128)S(1)}, f32[4,48,128]{2,1,0:T(8,128)S(1)}, u32[]{:S(2)}, u32[]{:S(2)}) %collective-permute-start.6) | collective-permute-done | bytes 98336 | tf_op jit(solution)/shard_map/ppermute | solution.py:349
  39.3 4.3 %collective-permute-done.7 = f32[4,48,128]{2,1,0:T(8,128)S(1)} collective-permute-done((f32[4,48,128]{2,1,0:T(8,128)S(1)}, f32[4,48,128]{2,1,0:T(8,128)S(1)}, u32[]{:S(2)}, u32[]{:S(2)}) %collective-permute-start.7) | collective-permute-done | bytes 98336 | tf_op jit(solution)/shard_map/ppermute | solution.py:349
  43.6 0.4 collective-permute-start.8
  44.0 3.2 %collective-permute-start.9 = (f32[3,48,128]{2,1,0:T(8,128)S(1)}, f32[3,48,128]{2,1,0:T(8,128)S(1)}, u32[]{:S(2)}, u32[]{:S(2)}) collective-permute-start(f32[3,48,128]{2,1,0:T(8,128)S(1)} %pad_maximum_fusion.6), channel_id=1, source_target_pairs={{0,2},{1,3},{2,0},{3,1},{4,6},{5,7},{6,4},{7,5},{8,10},{9,11},{10,... | collective-permute-start | bytes 221192 | tf_op jit(solution)/shard_map/ppermute | solution.py:345
  47.2 0.1 collective-permute-start.10
  47.4 0.0 collective-permute-done.8.refs_1_
  47.4 2.7 %collective-permute-done.9.refs_2_ = f32[3,48,128]{2,1,0:T(8,128)S(1)} collective-permute-done((f32[3,48,128]{2,1,0:T(8,128)S(1)}, f32[3,48,128]{2,1,0:T(8,128)S(1)}, u32[]{:S(2)}, u32[]{:S(2)}) %collective-permute-start.9) | collective-permute-done | bytes 73760 | tf_op jit(solution)/shard_map/ppermute | solution.py:345
  50.1 1.4 %collective-permute-done.10.refs_3_ = f32[3,48,128]{2,1,0:T(8,128)S(1)} collective-permute-done((f32[3,48,128]{2,1,0:T(8,128)S(1)}, f32[3,48,128]{2,1,0:T(8,128)S(1)}, u32[]{:S(2)}, u32[]{:S(2)}) %collective-permute-start.10) | collective-permute-done | bytes 73760 | tf_op jit(solution)/shard_map/ppermute | solution.py:345
  51.5 1.1 %add.25 = f32[768,128]{1,0:T(8,128)} custom-call(f32[768,128]{1,0:T(8,128)S(1)} %get-tuple-element.23.acc, f32[1,104,128]{2,1,0:T(8,128)S(1)} %get-tuple-element.29.refs_0_.mine, f32[3,48,128]{2,1,0:T(8,128)S(1)} %pad_maximum_fusion.4.refs_0_, f32[3,48,128]{2,1,0:T(8,128)S(1)} %collective-permute-done.8.refs_1_, ...), custom_call_target="tpu_custom_call" | custom-call | tf_op jit(solution)/shard_map/add/pallas_call | solution.py:417
  (20 shorter events, 0.2 us)
Async XLA Ops:
  3.6 10.7 %collective-permute-start = (f32[3,104,128]{2,1,0:T(8,128)}, f32[3,104,128]{2,1,0:T(8,128)S(1)}, u32[]{:S(2)}, u32[]{:S(2)}) collective-permute-start(f32[3,104,128]{2,1,0:T(8,128)} %get-tuple-element.16), channel_id=1, source_target_pairs={{0,2},{1,3},{2,0},{3,1},{4,6},{5,7},{6,4},{7,5},{8,10},{9,11},{10,... | collective-permute-start | bytes 479240 | tf_op jit(solution)/shard_map/ppermute | solution.py:345
  6.6 1.6 %collective-permute-start.1 = (f32[3,104,128]{2,1,0:T(8,128)}, f32[3,104,128]{2,1,0:T(8,128)S(1)}, u32[]{:S(2)}, u32[]{:S(2)}) collective-permute-start(f32[3,104,128]{2,1,0:T(8,128)} %get-tuple-element.18), channel_id=1, source_target_pairs={{0,1},{1,0},{2,3},{3,2},{4,5},{5,4},{6,7},{7,6},{8,9},{9,8},{10,11... | collective-permute-start | bytes 479240 | tf_op jit(solution)/shard_map/ppermute | solution.py:345
  6.6 7.7 %collective-permute-start.2 = (f32[3,104,128]{2,1,0:T(8,128)}, f32[3,104,128]{2,1,0:T(8,128)S(1)}, u32[]{:S(2)}, u32[]{:S(2)}) collective-permute-start(f32[3,104,128]{2,1,0:T(8,128)} %get-tuple-element.20), channel_id=1, source_target_pairs={{0,3},{1,2},{2,1},{3,0},{4,7},{5,6},{6,5},{7,4},{8,11},{9,10},{10,... | collective-permute-start | bytes 479240 | tf_op jit(solution)/shard_map/ppermute | solution.py:345
  6.8 3.0 %copy-start = (f32[64,3,512]{2,0,1:T(8,128)S(1)}, f32[64,3,512]{2,0,1:T(8,128)}, u32[]{:S(2)}) copy-start(f32[64,3,512]{2,0,1:T(8,128)} %param.4) | copy-start | bytes 1179652
  6.9 3.0 %copy-start.1 = (f32[64,3,512]{2,0,1:T(8,128)S(1)}, f32[64,3,512]{2,0,1:T(8,128)}, u32[]{:S(2)}) copy-start(f32[64,3,512]{2,0,1:T(8,128)} %param.5) | copy-start | bytes 1179652
  8.3 10.8 %collective-permute-start.5 = (f32[2,104,128]{2,1,0:T(8,128)S(1)}, f32[2,104,128]{2,1,0:T(8,128)S(1)}, u32[]{:S(2)}, u32[]{:S(2)}) collective-permute-start(f32[2,104,128]{2,1,0:T(8,128)S(1)} %pad_maximum_fusion.2), channel_id=1, source_target_pairs={{0,4},{4,0},{8,12},{12,8},{16,20},{20,16},{24,28},{28,24},{1,5},{5... | collective-permute-start | bytes 319496 | tf_op jit(solution)/shard_map/ppermute | solution.py:349
  14.4 8.6 %collective-permute-start.3 = (f32[2,104,128]{2,1,0:T(8,128)S(1)}, f32[2,104,128]{2,1,0:T(8,128)S(1)}, u32[]{:S(2)}, u32[]{:S(2)}) collective-permute-start(f32[2,104,128]{2,1,0:T(8,128)S(1)} %pad_maximum_fusion.1), channel_id=1, source_target_pairs={{0,4},{4,0},{8,12},{12,8},{16,20},{20,16},{24,28},{28,24},{1,5},{5... | collective-permute-start | bytes 319496 | tf_op jit(solution)/shard_map/ppermute | solution.py:349
  15.4 10.4 %collective-permute-start.4 = (f32[4,104,128]{2,1,0:T(8,128)S(1)}, f32[4,104,128]{2,1,0:T(8,128)S(1)}, u32[]{:S(2)}, u32[]{:S(2)}) collective-permute-start(f32[4,104,128]{2,1,0:T(8,128)S(1)} %pad_maximum_fusion), channel_id=1, source_target_pairs={{0,28},{4,8},{8,4},{12,16},{16,12},{20,24},{24,20},{28,0},{1,29},{... | collective-permute-start | bytes 638984 | tf_op jit(solution)/shard_map/ppermute | solution.py:349
  34.6 4.7 %collective-permute-start.6 = (f32[4,48,128]{2,1,0:T(8,128)S(1)}, f32[4,48,128]{2,1,0:T(8,128)S(1)}, u32[]{:S(2)}, u32[]{:S(2)}) collective-permute-start(f32[4,48,128]{2,1,0:T(8,128)S(1)} %pad_maximum_fusion.3), channel_id=1, source_target_pairs={{0,4},{4,0},{8,12},{12,8},{16,20},{20,16},{24,28},{28,24},{1,5},{5... | collective-permute-start | bytes 294920 | tf_op jit(solution)/shard_map/ppermute | solution.py:349
  35.7 7.9 %collective-permute-start.7 = (f32[4,48,128]{2,1,0:T(8,128)S(1)}, f32[4,48,128]{2,1,0:T(8,128)S(1)}, u32[]{:S(2)}, u32[]{:S(2)}) collective-permute-start(f32[4,48,128]{2,1,0:T(8,128)S(1)} %bitcast.44), channel_id=1, source_target_pairs={{0,28},{4,8},{8,4},{12,16},{16,12},{20,24},{24,20},{28,0},{1,29},{... | collective-permute-start | bytes 294920 | tf_op jit(solution)/shard_map/ppermute | solution.py:349
  43.6 3.7 %collective-permute-start.8 = (f32[3,48,128]{2,1,0:T(8,128)S(1)}, f32[3,48,128]{2,1,0:T(8,128)S(1)}, u32[]{:S(2)}, u32[]{:S(2)}) collective-permute-start(f32[3,48,128]{2,1,0:T(8,128)S(1)} %pad_maximum_fusion.5), channel_id=1, source_target_pairs={{0,1},{1,0},{2,3},{3,2},{4,5},{5,4},{6,7},{7,6},{8,9},{9,8},{10,11... | collective-permute-start | bytes 221192 | tf_op jit(solution)/shard_map/ppermute | solution.py:345
  44.0 6.0 %collective-permute-start.9 = (f32[3,48,128]{2,1,0:T(8,128)S(1)}, f32[3,48,128]{2,1,0:T(8,128)S(1)}, u32[]{:S(2)}, u32[]{:S(2)}) collective-permute-start(f32[3,48,128]{2,1,0:T(8,128)S(1)} %pad_maximum_fusion.6), channel_id=1, source_target_pairs={{0,2},{1,3},{2,0},{3,1},{4,6},{5,7},{6,4},{7,5},{8,10},{9,11},{10,... | collective-permute-start | bytes 221192 | tf_op jit(solution)/shard_map/ppermute | solution.py:345
  47.2 4.2 %collective-permute-start.10 = (f32[3,48,128]{2,1,0:T(8,128)S(1)}, f32[3,48,128]{2,1,0:T(8,128)S(1)}, u32[]{:S(2)}, u32[]{:S(2)}) collective-permute-start(f32[3,48,128]{2,1,0:T(8,128)S(1)} %pad_maximum_fusion.7), channel_id=1, source_target_pairs={{0,3},{1,2},{2,1},{3,0},{4,7},{5,6},{6,5},{7,4},{8,11},{9,10},{10,... | collective-permute-start | bytes 221192 | tf_op jit(solution)/shard_map/ppermute | solution.py:345

commit v10 on v9

--- a/solution.py
+++ b/solution.py
@@ -144,16 +144,18 @@
     return (0, 1 - 2 * odd, 2 * odd - 1)[kind]
 
 
-def pack_kernel(sizes, cells, count, pos_hbm, frc_hbm, *refs):
+def pack_kernel(sizes, cells_hbm, count, pos_hbm, frc_hbm, *refs):
     n_space, n_pairs, share, cell_dev, tiles = sizes
     outs = refs[:n_pairs]
-    pos, frc, sems = refs[n_pairs:]
+    cells, pos, frc, sems = refs[n_pairs:]
     fetches = [
-        pltpu.make_async_copy(pos_hbm, pos, sems.at[0]),
-        pltpu.make_async_copy(frc_hbm, frc, sems.at[1]),
+        pltpu.make_async_copy(cells_hbm, cells, sems.at[0]),
+        pltpu.make_async_copy(pos_hbm, pos, sems.at[1]),
+        pltpu.make_async_copy(frc_hbm, frc, sems.at[2]),
     ]
     for fetch in fetches:
         fetch.start()
+    fetches.pop(0).wait()
     n_slots = cells.shape[1]
     shape = (n_slots, n_slots)
     down = lax.broadcasted_iota(jnp.int32, shape, 0)
@@ -351,12 +353,13 @@
     sent = pl.pallas_call(
         functools.partial(pack_kernel, sizes),
         out_shape=[message] * n_pairs,
-        in_specs=[vmem, smem, hbm, hbm],
+        in_specs=[hbm, smem, hbm, hbm],
         out_specs=[vmem] * n_pairs,
         scratch_shapes=[
+            pltpu.VMEM(pair_cells.shape, jnp.int32),
             pltpu.VMEM(total.shape, f32),
             pltpu.VMEM(total.shape, f32),
-            pltpu.SemaphoreType.DMA((2,)),
+            pltpu.SemaphoreType.DMA((3,)),
         ],
         compiler_params=pltpu.CompilerParams(vmem_limit_bytes=60 * 1024 * 1024),
         name="pack",

time: 52.3 us -> 50.1 us (0.958)
  waiting for transfers between devices: 14.8 us -> 8.04 us
  starting transfers between devices: 16.8 us -> 20.9 us
    ppermute x5, waiting for transfers between devices: 10.2 us -> 3.5 us  [beyond(): return lax.ppermute(value, 'space', moves)]
    ppermute x5, starting transfers between devices: 9.91 us -> 13.2 us  [beyond(): return lax.ppermute(value, 'space', moves)]
    pallas_call x3, Pallas kernels: 14.9 us -> 15.6 us  [pairs(): pl.pallas_call(functools.partial(pair_kernel, sizes, kinds, len(before),...]
    ppermute x6, starting transfers between devices: 6.92 us -> 7.62 us  [across(): return lax.ppermute(value, 'pairs', [(j, j ^ turn) for j in range(n_pairs)])]
    pallas_call x1, Pallas kernels: 2.98 us -> 2.31 us  [body(): pl.pallas_call(functools.partial(pack_kernel, sizes), out_shape=[message]...]
  transfers between devices with their start and end apart: 11 -> 11, of which waited for: 7 -> 5; matrix products, arithmetic and copies ran while one was open for 2% -> 2% of each run, Pallas kernels for 12% -> 19%
where the time goes in v10:
time: 50.1 us; the launch traced here: 50 us
  starting transfers between devices  20.9 us (42%)
  Pallas kernels  19.1 us (38%)
  waiting for transfers between devices  8.04 us (16%)
  local copies, waits for them, and re-layouts  1.03 us (2%)
  between operations  0.82 us (2%)
    pallas_call x3, Pallas kernels, pairs(): pl.pallas_call(functools.partial(pair_kernel, sizes, kinds, len(before),...  15.6 us
    ppermute x5, starting transfers between devices, beyond(): return lax.ppermute(value, 'space', moves)  13.2 us
    ppermute x6, starting transfers between devices, across(): return lax.ppermute(value, 'pairs', [(j, j ^ turn) for j in range(n_pairs)])  7.62 us
    ppermute x6, waiting for transfers between devices, across(): return lax.ppermute(value, 'pairs', [(j, j ^ turn) for j in range(n_pairs)])  4.54 us
    ppermute x5, waiting for transfers between devices, beyond(): return lax.ppermute(value, 'space', moves)  3.5 us
    pallas_call x1, Pallas kernels, body(): pl.pallas_call(functools.partial(pack_kernel, sizes), out_shape=[message]...  2.31 us
    pallas_call x1, Pallas kernels, body(): pl.pallas_call(functools.partial(add_kernel, sizes, where), out_shape=tot...  1.14 us
  transfers between devices with their start and end apart: 11, of which 5 were waited for; matrix products, arithmetic and copies ran while one was open for 2% of the time, Pallas kernels for 19%

profile of v10, /device:TPU:0, one launch (start us, length us, event | category | flops | bytes accessed | tf_op | source)
XLA Modules:
  0.0 50.0 jit_solution(1527300605074882215)
XLA Ops:
  0.7 2.3 %pack.1 = (f32[3,104,128]{2,1,0:T(8,128)}, f32[3,104,128]{2,1,0:T(8,128)}, f32[3,104,128]{2,1,0:T(8,128)}, f32[3,104,128]{2,1,0:T(8,128)}) custom-call(s32[2,48]{1,0:T(2,128)} %cells_hbm.1, s32[1]{0:T(128)S(6)} %copy.9.count, f32[768,128]{1,0:T(8,128)} %bitcast.33, f32[768,128]{1,0:T(8,128)} %bitcast.37), custom_call_target="tpu_custom_call" | custom-call | tf_op jit(solution)/shard_map/pack/pallas_call | solution.py:353
  3.0 3.0 %collective-permute-start = (f32[3,104,128]{2,1,0:T(8,128)}, f32[3,104,128]{2,1,0:T(8,128)S(1)}, u32[]{:S(2)}, u32[]{:S(2)}) collective-permute-start(f32[3,104,128]{2,1,0:T(8,128)} %get-tuple-element.16), channel_id=1, source_target_pairs={{0,2},{1,3},{2,0},{3,1},{4,6},{5,7},{6,4},{7,5},{8,10},{9,11},{10,... | collective-permute-start | bytes 479240 | tf_op jit(solution)/shard_map/ppermute | solution.py:347
  6.0 0.0 collective-permute-start.1
  6.0 0.2 collective-permute-start.2
  6.2 0.0 copy-start
  6.2 0.0 copy-start.1
  6.2 0.9 %fusion = (f32[1,104,128]{2,1,0:T(8,128)S(1)}, f32[1,104,128]{2,1,0:T(8,128)S(1)}, f32[1,104,128]{2,1,0:T(8,128)S(1)}) fusion(f32[3,104,128]{2,1,0:T(8,128)} %get-tuple-element.17), kind=kLoop, calls=%fused_computation.14 | loop fusion | bytes 319488 | tf_op jit(solution)/shard_map/slice | solution.py:397
  7.1 0.4 collective-permute-done.1
  7.6 1.6 %collective-permute-start.5 = (f32[2,104,128]{2,1,0:T(8,128)S(1)}, f32[2,104,128]{2,1,0:T(8,128)S(1)}, u32[]{:S(2)}, u32[]{:S(2)}) collective-permute-start(f32[2,104,128]{2,1,0:T(8,128)S(1)} %pad_maximum_fusion.2), channel_id=1, source_target_pairs={{0,4},{4,0},{8,12},{12,8},{16,20},{20,16},{24,28},{28,24},{1,5},{5... | collective-permute-start | bytes 319496 | tf_op jit(solution)/shard_map/ppermute | solution.py:351
  9.2 0.0 copy-done
  9.2 0.0 copy-done.1
  9.2 3.8 %pairs.3 = (f32[768,128]{1,0:T(8,128)S(1)}, f32[96,128]{1,0:T(8,128)S(1)}, f32[1,128]{1,0:T(1,128)S(1)}) custom-call(f32[1,104,128]{2,1,0:T(8,128)S(1)} %get-tuple-element.29.refs_0_.mine, f32[1,104,128]{2,1,0:T(8,128)S(1)} %get-tuple-element.32.refs_1_, f32[768,128]{1,0:T(8,128)S(1)} %bitcast.34, f32[768,128]{1,0:T(8,128)S(1)} %bitcast.38), custom_call_target="tpu_custom_call" | custom-call | flops 2000000000 | bytes 2000000 | tf_op jit(solution)/shard_map/pairs/pallas_call | solution.py:374
  13.1 0.0 collective-permute-done
  13.1 0.0 collective-permute-done.2
  13.2 1.6 %collective-permute-start.3 = (f32[2,104,128]{2,1,0:T(8,128)S(1)}, f32[2,104,128]{2,1,0:T(8,128)S(1)}, u32[]{:S(2)}, u32[]{:S(2)}) collective-permute-start(f32[2,104,128]{2,1,0:T(8,128)S(1)} %pad_maximum_fusion.1), channel_id=1, source_target_pairs={{0,4},{4,0},{8,12},{12,8},{16,20},{20,16},{24,28},{28,24},{1,5},{5... | collective-permute-start | bytes 319496 | tf_op jit(solution)/shard_map/ppermute | solution.py:351
  14.8 3.6 %collective-permute-start.4 = (f32[4,104,128]{2,1,0:T(8,128)S(1)}, f32[4,104,128]{2,1,0:T(8,128)S(1)}, u32[]{:S(2)}, u32[]{:S(2)}) collective-permute-start(f32[4,104,128]{2,1,0:T(8,128)S(1)} %pad_maximum_fusion), channel_id=1, source_target_pairs={{0,28},{4,8},{8,4},{12,16},{16,12},{20,24},{24,20},{28,0},{1,29},{... | collective-permute-start | bytes 638984 | tf_op jit(solution)/shard_map/ppermute | solution.py:351
  18.4 0.0 collective-permute-done.5.refs_0_
  18.4 5.8 %pairs.4 = (f32[768,128]{1,0:T(8,128)S(1)}, f32[192,128]{1,0:T(8,128)S(1)}) custom-call(f32[2,104,128]{2,1,0:T(8,128)S(1)} %collective-permute-done.5.refs_0_, f32[1,104,128]{2,1,0:T(8,128)S(1)} %slice.147.refs_1_, f32[1,104,128]{2,1,0:T(8,128)S(1)} %slice.148.refs_2_, f32[768,128]{1,0:T(8,128)S(1)} %bitcast.35, ...), custom_call_target="tpu_custom_call", output_to_operand_aliasing={{0}: (5, {})} | custom-call | flops 4000000000 | bytes 2000000 | tf_op jit(solution)/shard_map/pairs/pallas_call | solution.py:374
  24.2 0.0 collective-permute-done.3.refs_0_
  24.2 0.9 %collective-permute-done.4.refs_1_ = f32[4,104,128]{2,1,0:T(8,128)S(1)} collective-permute-done((f32[4,104,128]{2,1,0:T(8,128)S(1)}, f32[4,104,128]{2,1,0:T(8,128)S(1)}, u32[]{:S(2)}, u32[]{:S(2)}) %collective-permute-start.4) | collective-permute-done | bytes 213024 | tf_op jit(solution)/shard_map/ppermute | solution.py:351
  25.1 6.0 %pairs.5 = (f32[768,128]{1,0:T(8,128)S(1)}, f32[288,128]{1,0:T(8,128)S(1)}) custom-call(f32[2,104,128]{2,1,0:T(8,128)S(1)} %collective-permute-done.3.refs_0_, f32[4,104,128]{2,1,0:T(8,128)S(1)} %collective-permute-done.4.refs_1_, f32[768,128]{1,0:T(8,128)S(1)} %bitcast.36, f32[768,128]{1,0:T(8,128)S(1)} %bitcast.40, ...), custom_call_target="tpu_custom_call", output_to_operand_aliasing={{0}: (4, {})} | custom-call | flops 6000000000 | bytes 2000000 | tf_op jit(solution)/shard_map/pairs/pallas_call | solution.py:374
  31.2 0.1 collective-permute-start.6
  31.3 6.4 %collective-permute-start.7 = (f32[4,48,128]{2,1,0:T(8,128)S(1)}, f32[4,48,128]{2,1,0:T(8,128)S(1)}, u32[]{:S(2)}, u32[]{:S(2)}) collective-permute-start(f32[4,48,128]{2,1,0:T(8,128)S(1)} %bitcast.44), channel_id=1, source_target_pairs={{0,28},{4,8},{8,4},{12,16},{16,12},{20,24},{24,20},{28,0},{1,29},{... | collective-permute-start | bytes 294920 | tf_op jit(solution)/shard_map/ppermute | solution.py:351
  37.7 0.0 collective-permute-done.6
  37.7 2.6 %collective-permute-done.7 = f32[4,48,128]{2,1,0:T(8,128)S(1)} collective-permute-done((f32[4,48,128]{2,1,0:T(8,128)S(1)}, f32[4,48,128]{2,1,0:T(8,128)S(1)}, u32[]{:S(2)}, u32[]{:S(2)}) %collective-permute-start.7) | collective-permute-done | bytes 98336 | tf_op jit(solution)/shard_map/ppermute | solution.py:351
  40.3 1.1 %collective-permute-start.8 = (f32[3,48,128]{2,1,0:T(8,128)S(1)}, f32[3,48,128]{2,1,0:T(8,128)S(1)}, u32[]{:S(2)}, u32[]{:S(2)}) collective-permute-start(f32[3,48,128]{2,1,0:T(8,128)S(1)} %pad_maximum_fusion.5), channel_id=1, source_target_pairs={{0,1},{1,0},{2,3},{3,2},{4,5},{5,4},{6,7},{7,6},{8,9},{9,8},{10,11... | collective-permute-start | bytes 221192 | tf_op jit(solution)/shard_map/ppermute | solution.py:347
  41.4 3.2 %collective-permute-start.9 = (f32[3,48,128]{2,1,0:T(8,128)S(1)}, f32[3,48,128]{2,1,0:T(8,128)S(1)}, u32[]{:S(2)}, u32[]{:S(2)}) collective-permute-start(f32[3,48,128]{2,1,0:T(8,128)S(1)} %pad_maximum_fusion.6), channel_id=1, source_target_pairs={{0,2},{1,3},{2,0},{3,1},{4,6},{5,7},{6,4},{7,5},{8,10},{9,11},{10,... | collective-permute-start | bytes 221192 | tf_op jit(solution)/shard_map/ppermute | solution.py:347
  44.6 0.1 collective-permute-start.10
  44.7 0.0 collective-permute-done.8.refs_1_
  44.7 2.7 %collective-permute-done.9.refs_2_ = f32[3,48,128]{2,1,0:T(8,128)S(1)} collective-permute-done((f32[3,48,128]{2,1,0:T(8,128)S(1)}, f32[3,48,128]{2,1,0:T(8,128)S(1)}, u32[]{:S(2)}, u32[]{:S(2)}) %collective-permute-start.9) | collective-permute-done | bytes 73760 | tf_op jit(solution)/shard_map/ppermute | solution.py:347
  47.4 1.4 %collective-permute-done.10.refs_3_ = f32[3,48,128]{2,1,0:T(8,128)S(1)} collective-permute-done((f32[3,48,128]{2,1,0:T(8,128)S(1)}, f32[3,48,128]{2,1,0:T(8,128)S(1)}, u32[]{:S(2)}, u32[]{:S(2)}) %collective-permute-start.10) | collective-permute-done | bytes 73760 | tf_op jit(solution)/shard_map/ppermute | solution.py:347
  48.8 1.1 %add.25 = f32[768,128]{1,0:T(8,128)} custom-call(f32[768,128]{1,0:T(8,128)S(1)} %get-tuple-element.23.acc, f32[1,104,128]{2,1,0:T(8,128)S(1)} %get-tuple-element.29.refs_0_.mine, f32[3,48,128]{2,1,0:T(8,128)S(1)} %pad_maximum_fusion.4.refs_0_, f32[3,48,128]{2,1,0:T(8,128)S(1)} %collective-permute-done.8.refs_1_, ...), custom_call_target="tpu_custom_call" | custom-call | tf_op jit(solution)/shard_map/add/pallas_call | solution.py:420
  (20 shorter events, 0.2 us)
Async XLA Ops:
  3.0 10.1 %collective-permute-start = (f32[3,104,128]{2,1,0:T(8,128)}, f32[3,104,128]{2,1,0:T(8,128)S(1)}, u32[]{:S(2)}, u32[]{:S(2)}) collective-permute-start(f32[3,104,128]{2,1,0:T(8,128)} %get-tuple-element.16), channel_id=1, source_target_pairs={{0,2},{1,3},{2,0},{3,1},{4,6},{5,7},{6,4},{7,5},{8,10},{9,11},{10,... | collective-permute-start | bytes 479240 | tf_op jit(solution)/shard_map/ppermute | solution.py:347
  6.0 1.6 %collective-permute-start.1 = (f32[3,104,128]{2,1,0:T(8,128)}, f32[3,104,128]{2,1,0:T(8,128)S(1)}, u32[]{:S(2)}, u32[]{:S(2)}) collective-permute-start(f32[3,104,128]{2,1,0:T(8,128)} %get-tuple-element.18), channel_id=1, source_target_pairs={{0,1},{1,0},{2,3},{3,2},{4,5},{5,4},{6,7},{7,6},{8,9},{9,8},{10,11... | collective-permute-start | bytes 479240 | tf_op jit(solution)/shard_map/ppermute | solution.py:347
  6.0 7.1 %collective-permute-start.2 = (f32[3,104,128]{2,1,0:T(8,128)}, f32[3,104,128]{2,1,0:T(8,128)S(1)}, u32[]{:S(2)}, u32[]{:S(2)}) collective-permute-start(f32[3,104,128]{2,1,0:T(8,128)} %get-tuple-element.20), channel_id=1, source_target_pairs={{0,3},{1,2},{2,1},{3,0},{4,7},{5,6},{6,5},{7,4},{8,11},{9,10},{10,... | collective-permute-start | bytes 479240 | tf_op jit(solution)/shard_map/ppermute | solution.py:347
  6.2 3.0 %copy-start = (f32[64,3,512]{2,0,1:T(8,128)S(1)}, f32[64,3,512]{2,0,1:T(8,128)}, u32[]{:S(2)}) copy-start(f32[64,3,512]{2,0,1:T(8,128)} %param.4) | copy-start | bytes 1179652
  6.2 3.0 %copy-start.1 = (f32[64,3,512]{2,0,1:T(8,128)S(1)}, f32[64,3,512]{2,0,1:T(8,128)}, u32[]{:S(2)}) copy-start(f32[64,3,512]{2,0,1:T(8,128)} %param.5) | copy-start | bytes 1179652
  7.6 10.8 %collective-permute-start.5 = (f32[2,104,128]{2,1,0:T(8,128)S(1)}, f32[2,104,128]{2,1,0:T(8,128)S(1)}, u32[]{:S(2)}, u32[]{:S(2)}) collective-permute-start(f32[2,104,128]{2,1,0:T(8,128)S(1)} %pad_maximum_fusion.2), channel_id=1, source_target_pairs={{0,4},{4,0},{8,12},{12,8},{16,20},{20,16},{24,28},{28,24},{1,5},{5... | collective-permute-start | bytes 319496 | tf_op jit(solution)/shard_map/ppermute | solution.py:351
  13.2 11.0 %collective-permute-start.3 = (f32[2,104,128]{2,1,0:T(8,128)S(1)}, f32[2,104,128]{2,1,0:T(8,128)S(1)}, u32[]{:S(2)}, u32[]{:S(2)}) collective-permute-start(f32[2,104,128]{2,1,0:T(8,128)S(1)} %pad_maximum_fusion.1), channel_id=1, source_target_pairs={{0,4},{4,0},{8,12},{12,8},{16,20},{20,16},{24,28},{28,24},{1,5},{5... | collective-permute-start | bytes 319496 | tf_op jit(solution)/shard_map/ppermute | solution.py:351
  14.8 10.4 %collective-permute-start.4 = (f32[4,104,128]{2,1,0:T(8,128)S(1)}, f32[4,104,128]{2,1,0:T(8,128)S(1)}, u32[]{:S(2)}, u32[]{:S(2)}) collective-permute-start(f32[4,104,128]{2,1,0:T(8,128)S(1)} %pad_maximum_fusion), channel_id=1, source_target_pairs={{0,28},{4,8},{8,4},{12,16},{16,12},{20,24},{24,20},{28,0},{1,29},{... | collective-permute-start | bytes 638984 | tf_op jit(solution)/shard_map/ppermute | solution.py:351
  31.2 6.5 %collective-permute-start.6 = (f32[4,48,128]{2,1,0:T(8,128)S(1)}, f32[4,48,128]{2,1,0:T(8,128)S(1)}, u32[]{:S(2)}, u32[]{:S(2)}) collective-permute-start(f32[4,48,128]{2,1,0:T(8,128)S(1)} %pad_maximum_fusion.3), channel_id=1, source_target_pairs={{0,4},{4,0},{8,12},{12,8},{16,20},{20,16},{24,28},{28,24},{1,5},{5... | collective-permute-start | bytes 294920 | tf_op jit(solution)/shard_map/ppermute | solution.py:351
  31.3 9.0 %collective-permute-start.7 = (f32[4,48,128]{2,1,0:T(8,128)S(1)}, f32[4,48,128]{2,1,0:T(8,128)S(1)}, u32[]{:S(2)}, u32[]{:S(2)}) collective-permute-start(f32[4,48,128]{2,1,0:T(8,128)S(1)} %bitcast.44), channel_id=1, source_target_pairs={{0,28},{4,8},{8,4},{12,16},{16,12},{20,24},{24,20},{28,0},{1,29},{... | collective-permute-start | bytes 294920 | tf_op jit(solution)/shard_map/ppermute | solution.py:351
  40.3 4.4 %collective-permute-start.8 = (f32[3,48,128]{2,1,0:T(8,128)S(1)}, f32[3,48,128]{2,1,0:T(8,128)S(1)}, u32[]{:S(2)}, u32[]{:S(2)}) collective-permute-start(f32[3,48,128]{2,1,0:T(8,128)S(1)} %pad_maximum_fusion.5), channel_id=1, source_target_pairs={{0,1},{1,0},{2,3},{3,2},{4,5},{5,4},{6,7},{7,6},{8,9},{9,8},{10,11... | collective-permute-start | bytes 221192 | tf_op jit(solution)/shard_map/ppermute | solution.py:347
  41.4 6.0 %collective-permute-start.9 = (f32[3,48,128]{2,1,0:T(8,128)S(1)}, f32[3,48,128]{2,1,0:T(8,128)S(1)}, u32[]{:S(2)}, u32[]{:S(2)}) collective-permute-start(f32[3,48,128]{2,1,0:T(8,128)S(1)} %pad_maximum_fusion.6), channel_id=1, source_target_pairs={{0,2},{1,3},{2,0},{3,1},{4,6},{5,7},{6,4},{7,5},{8,10},{9,11},{10,... | collective-permute-start | bytes 221192 | tf_op jit(solution)/shard_map/ppermute | solution.py:347
  44.6 4.2 %collective-permute-start.10 = (f32[3,48,128]{2,1,0:T(8,128)S(1)}, f32[3,48,128]{2,1,0:T(8,128)S(1)}, u32[]{:S(2)}, u32[]{:S(2)}) collective-permute-start(f32[3,48,128]{2,1,0:T(8,128)S(1)} %pad_maximum_fusion.7), channel_id=1, source_target_pairs={{0,3},{1,2},{2,1},{3,0},{4,7},{5,6},{6,5},{7,4},{8,11},{9,10},{10,... | collective-permute-start | bytes 221192 | tf_op jit(solution)/shard_map/ppermute | solution.py:347
